TPU v7x, 32 devices: a whole 2x2x4 slice. The times are simulated.
32 devices in a mesh: groups: 2 (over x), shard: 16 (over z, y, core).
Axes of the slice: x: 2, y: 2, z: 4, core: 2. Of those that a mesh axis runs over, the one named last changes fastest.
Arguments:
- queries: bfloat16 [64, 8192], P(('groups', 'shard')), parts along dimension 0, may hold values from -2.5 to 2.5
- new_kv: bfloat16 [64, 2, 512], P(('groups', 'shard')), parts along dimension 0, may hold values from -2.5 to 2.5
- kv_pages: bfloat16 [512, 2, 32, 512], P(('groups', 'shard')), parts along dimension 0, may hold values from -2.5 to 2.5
- page_table: int32 [64, 8], P('groups'), parts along dimension 0, may hold values from 0 to 255, as said below
- lengths: int32 [64], P('groups'), parts along dimension 0, may hold values from 1 to 256, as said below
- residual: bfloat16 [64, 8192], P('groups', 'shard'), parts along dimension 0, may hold values from -2 to 2
- out_weight: bfloat16 [8192, 8192], P(None, 'shard'), may hold values from -0.1875 to 0.1875
- norm_gain: float32 [8192], P('shard'), may hold values from 0.25 to 1.75
- gate_weight: bfloat16 [8192, 26624], P(None, 'shard'), may hold values from -0.0625 to 0.0625
- up_weight: bfloat16 [8192, 26624], P(None, 'shard'), may hold values from -0.0625 to 0.0625
- down_weight: bfloat16 [26624, 8192], P('shard'), may hold values from -0.0546875 to 0.0546875
Outputs:
- mixed: bfloat16 [64, 8192], P('groups', 'shard'), parts along dimension 0
There are 2 independent parts, one for each index of `groups`. A program takes and returns all parts, laid end to end along the dimension named above; an argument that names none is the same for every part. Nothing has to cross between parts.
Inputs may be any that keep to these rules, and one draw needn't show every extreme that they name: `page_table`: entry (b, k) is the global index of page k of sequence b; every page appears exactly once; pages i * 16 to (i + 1) * 16 - 1 are stored on device i of shard; the 16 pages of the sequences of device i of shard lie one on each device of the aligned block of 16 consecutive devices of shard that contains i. `lengths`: some sequence has exactly 256 cached tokens.
All inputs are finite; a program needn't handle non-finite values.
Results may differ from a plain program's by a relative error of at most 0.015.
Values may be sent and summed in bfloat16 or wider, within the bound.
No kernel may reach another device: no remote copies, remote signals or barrier semaphores. Data moves between devices by JAX's collectives and lax.ppermute only.
A program may use at most 192 MiB of HBM per device.

v0:
```python
import math

import jax
import jax.numpy as jnp
from jax import lax
from jax.sharding import PartitionSpec as P

D = 8192
HEADS = 64
KV_HEADS = 4
HEAD_DIM = 128


norm_eps = 1e-05


def swapped(array, axis, distance):
    return lax.ppermute(array, axis, [(i, i ^ 1 << distance) for i in range(lax.axis_size(axis))])


def new_token_terms(queries, new_kv, score_scale):
    seq_dev = queries.shape[0]
    group_size = HEADS // KV_HEADS
    query_heads = queries.reshape(seq_dev, KV_HEADS, group_size, HEAD_DIM)
    new_keys = new_kv[:, 0].reshape(seq_dev, KV_HEADS, HEAD_DIM)
    new_values = new_kv[:, 1].reshape(seq_dev, KV_HEADS, HEAD_DIM)
    scores = (
        jnp.einsum("bgqd,bgd->bgq", query_heads, new_keys, preferred_element_type=jnp.float32)
        * score_scale
    )
    weights = jnp.exp(scores)
    numerator = jnp.einsum(
        "bgq,bgd->bgqd",
        weights.astype(jnp.bfloat16),
        new_values,
        preferred_element_type=jnp.float32,
    )
    return (numerator.reshape(seq_dev, D), weights.reshape(seq_dev, HEADS))


def butterfly(items, position, mover):
    count = items[0].shape[0]
    for level in range(count.bit_length() - 1):
        upper_half = position // (1 << level) % 2 == 1
        halves = [
            entry.reshape((count >> level + 1, 2, 1 << level) + entry.shape[1:]) for entry in items
        ]
        outgoing = tuple(
            (jnp.where(upper_half, halves_one[:, 0], halves_one[:, 1]) for halves_one in halves)
        )
        incoming = mover(outgoing, level)
        rebuilt = []
        for entry, halves_one, arrived_one in zip(items, halves, incoming):
            lower_part = jnp.where(upper_half, arrived_one, halves_one[:, 0])
            upper_part = jnp.where(upper_half, halves_one[:, 1], arrived_one)
            rebuilt.append(jnp.stack([lower_part, upper_part], axis=1).reshape(entry.shape))
        items = tuple(rebuilt)
    return items


def body(
    queries,
    new_kv,
    kv_pages,
    page_table,
    lengths,
    residual,
    out_weight,
    norm_gain,
    gate_weight,
    up_weight,
    down_weight,
):
    seq_dev = queries.shape[0]
    page_count = kv_pages.shape[0]
    page_len = kv_pages.shape[2]
    all_seqs = page_table.shape[0]
    max_pages = page_table.shape[1]
    group_size = HEADS // KV_HEADS
    score_scale = 1.0 / math.sqrt(HEAD_DIM)
    device_pos = lax.axis_index("shard")
    own_first = device_pos * seq_dev
    own_lengths = lax.dynamic_slice_in_dim(lengths, own_first, seq_dev, 0)
    own_table = lax.dynamic_slice_in_dim(page_table, own_first, seq_dev, 0)
    holder_local = own_table // page_count % page_count
    page_ids = device_pos * page_count + jnp.arange(page_count, dtype=jnp.int32)
    matches = page_table[None, :, :] == page_ids[:, None, None]
    seq_of = jnp.sum(
        jnp.where(matches, jnp.arange(all_seqs, dtype=jnp.int32)[None, :, None], 0), axis=(1, 2)
    )
    owner_local = seq_of // seq_dev % page_count
    own_numerator, own_denominator = new_token_terms(queries, new_kv, score_scale)
    outgoing = jnp.zeros_like(kv_pages).at[owner_local].set(kv_pages)
    arrived = butterfly(
        (outgoing,), device_pos, lambda sending, level: (swapped(sending[0], "shard", level),)
    )[0]
    fetched = arrived[holder_local]
    context = max_pages * page_len
    key_rows = fetched[:, :, 0].reshape(seq_dev, context, KV_HEADS, HEAD_DIM)
    value_rows = fetched[:, :, 1].reshape(seq_dev, context, KV_HEADS, HEAD_DIM)
    query_heads = queries.reshape(seq_dev, KV_HEADS, group_size, HEAD_DIM)
    scores = (
        jnp.einsum("bgqd,btgd->bgqt", query_heads, key_rows, preferred_element_type=jnp.float32)
        * score_scale
    )
    position = jnp.arange(context, dtype=jnp.int32)
    alive = position[None, :] < own_lengths[:, None]
    weights = jnp.where(alive[:, None, None, :], jnp.exp(scores), 0.0)
    denominator = jnp.sum(weights, axis=-1).reshape(seq_dev, HEADS)
    numerator = jnp.einsum(
        "bgqt,btgd->bgqd",
        weights.astype(jnp.bfloat16),
        value_rows,
        preferred_element_type=jnp.float32,
    )
    numer_rows = numerator.reshape(seq_dev, D) + own_numerator
    denom_rows = denominator + own_denominator
    attended = (
        (numer_rows.reshape(seq_dev, HEADS, HEAD_DIM) / denom_rows[:, :, None])
        .reshape(seq_dev, D)
        .astype(jnp.bfloat16)
    )
    projected = jnp.dot(
        lax.all_gather(attended, "shard", axis=0, tiled=True),
        out_weight,
        preferred_element_type=jnp.float32,
    )
    stream = (residual.astype(jnp.float32) + projected).astype(jnp.bfloat16)
    wide = stream.astype(jnp.float32)
    square_sums = lax.psum(jnp.sum(wide * wide, axis=1), "shard")
    normed = (wide * lax.rsqrt(square_sums / D + norm_eps)[:, None] * norm_gain[None, :]).astype(
        jnp.bfloat16
    )
    block_cols = lax.all_gather(normed, "shard", axis=1, tiled=True)
    gate_acts = jnp.dot(block_cols, gate_weight, preferred_element_type=jnp.float32)
    up_acts = jnp.dot(block_cols, up_weight, preferred_element_type=jnp.float32)
    hidden = (jax.nn.silu(gate_acts) * up_acts).astype(jnp.bfloat16)
    partial_terms = jnp.dot(hidden, down_weight, preferred_element_type=jnp.float32)
    down_terms = lax.psum_scatter(partial_terms, "shard", scatter_dimension=1, tiled=True)
    return (wide + down_terms).astype(jnp.bfloat16)


def solution(mesh):
    placed = (
        P(("groups", "shard"), None),
        P(("groups", "shard"), None, None),
        P(("groups", "shard"), None, None, None),
        P("groups", None),
        P("groups"),
        P("groups", "shard"),
        P(None, "shard"),
        P("shard"),
        P(None, "shard"),
        P(None, "shard"),
        P("shard", None),
    )
    return jax.shard_map(
        body, mesh=mesh, in_specs=placed, out_specs=P("groups", "shard"), check_vma=False
    )
```

profile of v0, /device:TPU:0, one launch (start us, length us, event | category | flops | bytes accessed | tf_op | source)
XLA Modules:
  0.0 242.4 jit_solution(14289175598357823270)
XLA Ops:
  6.5 1.1 select_reduce_fusion
  7.8 2.3 scatter_fusion
  10.2 0.5 collective-permute-start
  10.7 1.5 collective-permute-done
  12.4 3.0 %collective-permute-start.1 = (bf16[4,2,2,32,512]{4,3,2,0,1:T(8,128)(2,1)S(1)}, bf16[4,2,2,32,512]{4,3,2,0,1:T(8,128)(2,1)S(1)}, u32[]{:S(2)}, u32[]{:S(2)}) collective-permute-start(bf16[4,2,2,32,512]{4,3,2,0,1:T(8,128)(2,1)S(1)} %broadcast_select_fusion.3), channel_id=1, source_target_pairs={{0,2},{1,3},{2,0},{3,1},{4,6},{5,7},{6,4},{7,5},{8,10},{9,11},{10,... | collective-permute-start | bytes 1572872 | tf_op jit(solution)/shard_map/ppermute | solution.py:18
  15.4 12.2 %collective-permute-done.1 = bf16[4,2,2,32,512]{4,3,2,0,1:T(8,128)(2,1)S(1)} collective-permute-done((bf16[4,2,2,32,512]{4,3,2,0,1:T(8,128)(2,1)S(1)}, bf16[4,2,2,32,512]{4,3,2,0,1:T(8,128)(2,1)S(1)}, u32[]{:S(2)}, u32[]{:S(2)}) %collective-permute-start.1) | collective-permute-done | bytes 524320 | tf_op jit(solution)/shard_map/ppermute | solution.py:18
  28.1 1.9 collective-permute-start.2
  30.0 0.8 compare_select_fusion
  30.9 0.7 dynamic_slice.6
  31.6 0.8 copy.63
  32.5 9.2 %collective-permute-done.2 = bf16[2,4,2,32,512]{4,3,2,1,0:T(8,128)(2,1)S(1)} collective-permute-done((bf16[2,4,2,32,512]{4,3,2,1,0:T(8,128)(2,1)S(1)}, bf16[2,4,2,32,512]{4,3,2,1,0:T(8,128)(2,1)S(1)}, u32[]{:S(2)}, u32[]{:S(2)}) %collective-permute-start.2) | collective-permute-done | bytes 524320 | tf_op jit(solution)/shard_map/ppermute | solution.py:18
  42.2 2.6 %collective-permute-start.3 = (bf16[1,8,2,32,512]{4,3,2,1,0:T(8,128)(2,1)S(1)}, bf16[1,8,2,32,512]{4,3,2,1,0:T(8,128)(2,1)S(1)}, u32[]{:S(2)}, u32[]{:S(2)}) collective-permute-start(bf16[1,8,2,32,512]{4,3,2,1,0:T(8,128)(2,1)S(1)} %broadcast_select_fusion.5), channel_id=1, source_target_pairs={{0,8},{1,9},{2,10},{3,11},{4,12},{5,13},{6,14},{7,15},{8,0},{9,1},... | collective-permute-start | bytes 1572872 | tf_op jit(solution)/shard_map/ppermute | solution.py:18
  44.8 0.7 slice_convert_fusion
  45.5 0.8 fusion.23
  46.3 20.7 %collective-permute-done.3 = bf16[1,8,2,32,512]{4,3,2,1,0:T(8,128)(2,1)S(1)} collective-permute-done((bf16[1,8,2,32,512]{4,3,2,1,0:T(8,128)(2,1)S(1)}, bf16[1,8,2,32,512]{4,3,2,1,0:T(8,128)(2,1)S(1)}, u32[]{:S(2)}, u32[]{:S(2)}) %collective-permute-start.3) | collective-permute-done | bytes 524320 | tf_op jit(solution)/shard_map/ppermute | solution.py:18
  67.2 0.6 gather_fusion
  69.0 22.7 %all-gather = bf16[16,2,8192]{2,1,0:T(2,128)(2,1)S(1)} all-gather(bf16[1,2,8192]{2,1,0:T(2,128)(2,1)S(1)} %fusion.20), channel_id=1, replica_groups=mesh['groups'=2,'shard'=16] {'shard'}, dimensions={0}, use_global_device_ids=true | all-gather | bytes 557056 | tf_op jit(solution)/shard_map/all_gather | solution.py:124
  92.0 5.0 %multiply_reduce_fusion = (f32[32]{0:T(128)S(1)}, f32[32,512]{1,0:T(8,128)S(1)}) fusion(bf16[32,8192]{1,0:T(8,128)(2,1)S(1)} %reshape.219, bf16[8192,512]{1,0:T(8,128)(2,1)} %param.17, bf16[32,512]{1,0:T(8,128)(2,1)S(1)} %copy-done), kind=kOutput, calls=%fused_computation.53 | convolution fusion | flops 268533728 | bytes 9011328 | tf_op jit(solution)/shard_map/dot_general | solution.py:123
  97.0 29.8 %psum.7 = f32[32]{0:T(128)S(1)} all-reduce(f32[32]{0:T(128)S(1)} %get-tuple-element.19), channel_id=1, replica_groups=mesh['groups'=2,'shard'=16] {'shard'}, use_global_device_ids=true, to_apply=%region_4.5 | all-reduce | flops 32 | bytes 256 | tf_op jit(solution)/shard_map/psum | solution.py:130
  126.9 18.8 %all_gather.7 = bf16[32,8192]{1,0:T(8,128)(2,1)S(1)} all-gather(bf16[32,512]{1,0:T(8,128)(2,1)S(1)} %multiply_convert_fusion), channel_id=1, replica_groups=mesh['groups'=2,'shard'=16] {'shard'}, dimensions={1}, use_global_device_ids=true | all-gather | bytes 557056 | tf_op jit(solution)/shard_map/all_gather | solution.py:134
  145.7 11.1 %fusion.34 = f32[32,1664]{1,0:T(8,128)S(1)} fusion(bf16[32,8192]{1,0:T(8,128)(2,1)S(1)} %all_gather.7, bf16[8192,1664]{1,0:T(8,128)(2,1)} %param.19), kind=kOutput, calls=%fused_computation.96 | convolution fusion | flops 872415232 | bytes 28000256 | tf_op jit(solution)/shard_map/dot_general | solution.py:135
  156.8 21.4 %fusion.1 = f32[32,8192]{1,0:T(8,128)} fusion(bf16[1664,8192]{1,0:T(8,128)(2,1)} %param.21, bf16[32,8192]{1,0:T(8,128)(2,1)S(1)} %all_gather.7, bf16[8192,1664]{1,0:T(8,128)(2,1)} %param.20, f32[32,1664]{1,0:T(8,128)S(1)} %fusion.34), kind=kOutput, calls=%fused_computation.4 | convolution fusion | flops 1745149952 | bytes 56311808 | tf_op jit(solution)/shard_map/dot_general | solution.py:138
  178.2 55.9 %reduce-scatter.2.cloned.1.call-done = f32[32,512]{1,0:T(8,128)} async-done(((f32[32,8192]{1,0:T(8,128)}), f32[32,512]{1,0:T(8,128)}) %reduce-scatter.2.cloned.1.call-update) | async-done | bytes 65552 | tf_op jit(solution)/shard_map/reduce_scatter | solution.py:139
  234.1 1.5 add_convert_fusion
  (38 shorter events, 3.3 us)
Async XLA Ops:
  6.5 85.4 %copy-start = (bf16[32,512]{1,0:T(8,128)(2,1)S(1)}, bf16[32,512]{1,0:T(8,128)(2,1)}, u32[]{:S(2)}) copy-start(bf16[32,512]{1,0:T(8,128)(2,1)} %param.16) | copy-start | bytes 98308
  6.5 227.6 %reduce-scatter.2.cloned.1.call-start = ((), (), s32[]{:S(2)}) async-start(), calls=%async_computation.1 | async-start | bytes 1114112 | tf_op jit(solution)/shard_map/reduce_scatter | solution.py:139
  10.1 116.7 %copy-start.1 = (f32[512]{0:T(512)S(1)}, f32[512]{0:T(512)}, u32[]{:S(2)}) copy-start(f32[512]{0:T(512)} %param.18) | copy-start | bytes 6148
  10.2 2.1 collective-permute-start
  12.4 15.2 %collective-permute-start.1 = (bf16[4,2,2,32,512]{4,3,2,0,1:T(8,128)(2,1)S(1)}, bf16[4,2,2,32,512]{4,3,2,0,1:T(8,128)(2,1)S(1)}, u32[]{:S(2)}, u32[]{:S(2)}) collective-permute-start(bf16[4,2,2,32,512]{4,3,2,0,1:T(8,128)(2,1)S(1)} %broadcast_select_fusion.3), channel_id=1, source_target_pairs={{0,2},{1,3},{2,0},{3,1},{4,6},{5,7},{6,4},{7,5},{8,10},{9,11},{10,... | collective-permute-start | bytes 1572872 | tf_op jit(solution)/shard_map/ppermute | solution.py:18
  28.1 13.5 %collective-permute-start.2 = (bf16[2,4,2,32,512]{4,3,2,1,0:T(8,128)(2,1)S(1)}, bf16[2,4,2,32,512]{4,3,2,1,0:T(8,128)(2,1)S(1)}, u32[]{:S(2)}, u32[]{:S(2)}) collective-permute-start(bf16[2,4,2,32,512]{4,3,2,1,0:T(8,128)(2,1)S(1)} %broadcast_select_fusion.4), channel_id=1, source_target_pairs={{0,4},{1,5},{2,6},{3,7},{4,0},{5,1},{6,2},{7,3},{8,12},{9,13},{10,... | collective-permute-start | bytes 1572872 | tf_op jit(solution)/shard_map/ppermute | solution.py:18
  42.2 24.8 %collective-permute-start.3 = (bf16[1,8,2,32,512]{4,3,2,1,0:T(8,128)(2,1)S(1)}, bf16[1,8,2,32,512]{4,3,2,1,0:T(8,128)(2,1)S(1)}, u32[]{:S(2)}, u32[]{:S(2)}) collective-permute-start(bf16[1,8,2,32,512]{4,3,2,1,0:T(8,128)(2,1)S(1)} %broadcast_select_fusion.5), channel_id=1, source_target_pairs={{0,8},{1,9},{2,10},{3,11},{4,12},{5,13},{6,14},{7,15},{8,0},{9,1},... | collective-permute-start | bytes 1572872 | tf_op jit(solution)/shard_map/ppermute | solution.py:18
Sparse Core Ops, SparseCore 0:
  178.4 55.7 reduce-scatter.1
where the time goes:
time: 243 us; the launch traced here: 242 us
  waiting for transfers between devices  99.5 us (41%)
  blocking collectives  71.4 us (29%)
  matrix products  38.9 us (16%)
  between operations  13.6 us (6%)
  starting transfers between devices  7.89 us (3%)
  other arithmetic  5.62 us (2%)
  local copies, waits for them, and re-layouts  5.58 us (2%)
    reduce_scatter x1, waiting for transfers between devices, body(): lax.psum_scatter(partial_terms, 'shard', scatter_dimension=1, tiled=True)  55.9 us
    ppermute x4, waiting for transfers between devices, swapped(): lax.ppermute(array, axis, [(i, i ^ 1 << distance) for i in range(lax.axis...  43.6 us
    psum x1, blocking collectives, body(): square_sums = lax.psum(jnp.sum(wide * wide, axis=1), 'shard')  29.8 us
    all_gather x1, blocking collectives, body(): lax.all_gather(attended, 'shard', axis=0, tiled=True)  22.7 us
    dot_general x1, matrix products, body(): jnp.dot(hidden, down_weight, preferred_element_type=jnp.float32)  21.4 us
    all_gather x1, blocking collectives, body(): block_cols = lax.all_gather(normed, 'shard', axis=1, tiled=True)  18.8 us
    dot_general x1, matrix products, body(): jnp.dot(block_cols, gate_weight, preferred_element_type=jnp.float32)  11.1 us
    ppermute x4, starting transfers between devices, swapped(): lax.ppermute(array, axis, [(i, i ^ 1 << distance) for i in range(lax.axis...  7.89 us
  transfers between devices with their start and end apart: 5, of which 5 were waited for; matrix products, arithmetic and copies ran while one was open for 2% of the time, Pallas kernels for 0%

commit v1 on v0

--- a/solution.py
+++ b/solution.py
@@ -3,6 +3,8 @@
 import jax
 import jax.numpy as jnp
 from jax import lax
+from jax.experimental import pallas as pl
+from jax.experimental.pallas import tpu as pltpu
 from jax.sharding import PartitionSpec as P
 
 D = 8192
@@ -140,6 +142,358 @@
     return (wide + down_terms).astype(jnp.bfloat16)
 
 
+GROUP = HEADS // KV_HEADS
+HEAD_ROWS = 80
+MIB = 2**20
+VMEM_SPEC = pl.BlockSpec(memory_space=pltpu.VMEM)
+SMEM_SPEC = pl.BlockSpec(memory_space=pltpu.SMEM)
+
+
+def sent(array, distance):
+    size = lax.axis_size("shard")
+    return lax.ppermute(array, "shard", [(i, i ^ distance) for i in range(size)])
+
+
+def gathered(piece):
+    first = jnp.stack([piece] + [sent(piece, distance) for distance in (4, 8, 12)])
+    even = jnp.concatenate([first, sent(first, 2)])
+    return even, sent(even, 1)
+
+
+PEER = (0, 4, 8, 12, 2, 6, 10, 14)
+
+
+def two_terms(wide):
+    high = wide.astype(jnp.bfloat16).astype(jnp.float32)
+    return high, wide - high
+
+
+def pack_kernel(query_ref, gain_ref, out_ref):
+    rows = query_ref.shape[0]
+    out_ref[:rows, :] = query_ref[...]
+    high, rest = two_terms(gain_ref[...])
+    middle, low = two_terms(rest)
+    filler = jnp.zeros((16 - 3 * high.shape[0], HEAD_DIM), jnp.float32)
+    out_ref[rows:, :] = jnp.concatenate([high, middle, low, filler]).astype(jnp.bfloat16)
+
+
+def packed(queries, norm_gain):
+    query_rows = queries.reshape(-1, HEAD_DIM)
+    gain_rows = norm_gain.reshape(-1, HEAD_DIM)
+    return pl.pallas_call(
+        pack_kernel,
+        in_specs=[VMEM_SPEC] * 2,
+        out_specs=VMEM_SPEC,
+        out_shape=jax.ShapeDtypeStruct((query_rows.shape[0] + 16, HEAD_DIM), jnp.bfloat16),
+    )(query_rows, gain_rows)
+
+
+def row_of(column):
+    return jnp.swapaxes(jnp.broadcast_to(column, (column.shape[0], HEAD_DIM)), 0, 1)[:1]
+
+
+def context_terms(query, keys, values, alive):
+    numerators, denominators = [], []
+    for head in range(KV_HEADS):
+        cols = slice(head * HEAD_DIM, (head + 1) * HEAD_DIM)
+        scores = lax.dot_general(
+            query[head * GROUP : (head + 1) * GROUP],
+            keys[:, cols],
+            (((1,), (1,)), ((), ())),
+            preferred_element_type=jnp.float32,
+        ) * (1.0 / math.sqrt(HEAD_DIM))
+        weights = jnp.where(alive, jnp.exp(scores), 0.0)
+        denominators.append(jnp.sum(weights, axis=1, keepdims=True))
+        numerators.append(
+            jnp.dot(
+                weights.astype(jnp.bfloat16), values[:, cols], preferred_element_type=jnp.float32
+            )
+        )
+    return jnp.concatenate(numerators), jnp.concatenate(denominators)
+
+
+def pages_kernel(table_ref, even_ref, odd_ref, pages_ref, out_ref):
+    me = table_ref[0]
+    page_len = pages_ref.shape[2]
+    position = lax.broadcasted_iota(jnp.int32, (GROUP, page_len), 1)
+    for entry in range(16):
+        source = even_ref if entry < 8 else odd_ref
+        owner = me ^ (PEER[entry % 8] + entry // 8)
+        slot, row, left = (table_ref[1 + 16 * part + owner] for part in range(3))
+        query = source[entry % 8, pl.ds(pl.multiple_of(row * HEADS, HEADS), HEADS), :]
+        numerator, denominator = context_terms(
+            query, pages_ref[slot, 0], pages_ref[slot, 1], position < left
+        )
+        out_ref[owner, :HEADS, :] = numerator.astype(jnp.bfloat16)
+        high, low = two_terms(row_of(denominator))
+        last = jnp.concatenate([high[:, :HEADS], low[:, :HEADS]], axis=1)
+        out_ref[owner, HEADS:, :] = jnp.concatenate(
+            [last, jnp.zeros((HEAD_ROWS - HEADS - 1, HEAD_DIM), jnp.float32)]
+        ).astype(jnp.bfloat16)
+
+
+def page_terms(table, even, odd, kv_pages):
+    return pl.pallas_call(
+        pages_kernel,
+        in_specs=[SMEM_SPEC] + [VMEM_SPEC] * 3,
+        out_specs=VMEM_SPEC,
+        out_shape=jax.ShapeDtypeStruct((16, HEAD_ROWS, HEAD_DIM), jnp.bfloat16),
+        compiler_params=pltpu.CompilerParams(vmem_limit_bytes=16 * MIB),
+        cost_estimate=pl.CostEstimate(flops=2**27, bytes_accessed=2**21, transcendentals=2**15),
+    )(table, even, odd, kv_pages)
+
+
+def combine_kernel(table_ref, arrived_ref, query_ref, new_ref, out_ref, wide):
+    first_token = lax.broadcasted_iota(jnp.int32, (GROUP, 8), 1) < 1
+    totals = []
+    for row in range(2):
+        keys = jnp.broadcast_to(new_ref[row, 0:1, :], (8, new_ref.shape[2]))
+        values = jnp.broadcast_to(new_ref[row, 1:2, :], (8, new_ref.shape[2]))
+        totals.append(
+            context_terms(
+                query_ref[row * HEADS : (row + 1) * HEADS, :], keys, values, first_token
+            )
+        )
+    sums = [numerator for numerator, _ in totals]
+    lower = [jnp.zeros((1, HEADS), jnp.float32)] * 2
+    for sender in range(16):
+        second = table_ref[49 + sender] == 1
+        numerator = arrived_ref[sender, :HEADS, :].astype(jnp.float32)
+        last = arrived_ref[sender, HEADS:, :].astype(jnp.float32)[:1]
+        denominator = last[:, :HEADS] + last[:, HEADS:]
+        sums = [
+            sums[0] + jnp.where(second, 0.0, numerator),
+            sums[1] + jnp.where(second, numerator, 0.0),
+        ]
+        lower = [
+            lower[0] + jnp.where(second, 0.0, denominator),
+            lower[1] + jnp.where(second, denominator, 0.0),
+        ]
+    for row in range(2):
+        padded = jnp.concatenate([lower[row], jnp.zeros((1, HEADS), jnp.float32)], axis=1)
+        column = jnp.swapaxes(jnp.broadcast_to(padded, (8, HEAD_DIM)), 0, 1)[:HEADS, :1]
+        wide[row * HEADS : (row + 1) * HEADS, :] = sums[row] / (column + totals[row][1])
+    out_ref[...] = wide[...].astype(jnp.bfloat16)
+
+
+def combined(table, arrived, query_rows, new_kv):
+    return pl.pallas_call(
+        combine_kernel,
+        in_specs=[SMEM_SPEC] + [VMEM_SPEC] * 3,
+        out_specs=VMEM_SPEC,
+        out_shape=jax.ShapeDtypeStruct((2 * HEADS, HEAD_DIM), jnp.bfloat16),
+        scratch_shapes=[pltpu.VMEM((2 * HEADS, HEAD_DIM), jnp.float32)],
+        compiler_params=pltpu.CompilerParams(vmem_limit_bytes=16 * MIB),
+        cost_estimate=pl.CostEstimate(flops=2**22, bytes_accessed=2**20, transcendentals=2**11),
+    )(table, arrived, query_rows, new_kv)
+
+
+def out_kernel(table_ref, even_ref, odd_ref, residual_ref, weight_ref, out_ref, wide, left, total):
+    step = pl.program_id(0)
+    depth = weight_ref.shape[0]
+
+    @pl.when(step == 0)
+    def _():
+        me = table_ref[0]
+        for entry in range(16):
+            source = even_ref if entry < 8 else odd_ref
+            device = me ^ (PEER[entry % 8] + entry // 8)
+            start = pl.multiple_of(device * 2 * HEADS, 2 * HEADS)
+            wide[pl.ds(start, 2 * HEADS), :] = source[entry % 8].astype(jnp.float32)
+        for head in range(HEADS):
+            rows = [wide[pl.ds(row * HEADS + head, 16, 2 * HEADS), :] for row in range(2)]
+            left[:, head * HEAD_DIM : (head + 1) * HEAD_DIM] = jnp.concatenate(rows).astype(
+                jnp.bfloat16
+            )
+        total[...] = jnp.zeros_like(total)
+
+    here = pl.ds(pl.multiple_of(step * depth, depth), depth)
+    total[...] += jnp.dot(left[:, here], weight_ref[...], preferred_element_type=jnp.float32)
+
+    @pl.when(step == pl.num_programs(0) - 1)
+    def _():
+        line = lax.broadcasted_iota(jnp.int32, (32, 32), 0)
+        entry = lax.broadcasted_iota(jnp.int32, (32, 32), 1)
+        turn = ((line % 2) * 16 + line // 2 == entry).astype(jnp.float32)
+        turned = lax.dot_general(
+            turn,
+            total[...],
+            (((1,), (0,)), ((), ())),
+            precision=lax.Precision.HIGHEST,
+            preferred_element_type=jnp.float32,
+        )
+        out_ref[...] = (residual_ref[...].astype(jnp.float32) + turned).astype(jnp.bfloat16)
+
+
+def projected(table, even, odd, residual, out_weight):
+    depth, (rows, width) = 1024, residual.shape
+    return pl.pallas_call(
+        out_kernel,
+        grid=(D // depth,),
+        in_specs=[SMEM_SPEC]
+        + [VMEM_SPEC] * 3
+        + [pl.BlockSpec((depth, width), lambda step: (step, 0))],
+        out_specs=VMEM_SPEC,
+        out_shape=jax.ShapeDtypeStruct((rows, width), jnp.bfloat16),
+        scratch_shapes=[
+            pltpu.VMEM((32 * HEADS, HEAD_DIM), jnp.float32),
+            pltpu.VMEM((rows, D), jnp.bfloat16),
+            pltpu.VMEM((rows, width), jnp.float32),
+        ],
+        compiler_params=pltpu.CompilerParams(vmem_limit_bytes=16 * MIB),
+        cost_estimate=pl.CostEstimate(
+            flops=2 * rows * D * width, bytes_accessed=2 * D * width, transcendentals=0
+        ),
+    )(table, even, odd, residual, out_weight)
+
+
+def hidden_kernel(
+    table_ref, even_ref, odd_ref, even_gain, odd_gain, gate_ref, up_ref, out_ref, scale, gates, ups
+):
+    step = pl.program_id(0)
+    swap = table_ref[0] % 2 == 1
+
+    @pl.when(step == 0)
+    def _():
+        squares = jnp.zeros(even_ref.shape[1:], jnp.float32)
+        for entry in range(8):
+            for source in (even_ref, odd_ref):
+                wide = source[entry].astype(jnp.float32)
+                squares = squares + wide * wide
+        scale[...] = lax.rsqrt(jnp.sum(squares, axis=1, keepdims=True) / D + norm_eps)
+        gates[...] = jnp.zeros_like(gates)
+        ups[...] = jnp.zeros_like(ups)
+
+    pieces = []
+    for stream_ref, gain_ref in ((even_ref, even_gain), (odd_ref, odd_gain)):
+        terms = gain_ref[step, 2 * HEADS :, :].astype(jnp.float32)
+        gain = terms[0:4] + terms[4:8] + terms[8:12]
+        gain = jnp.concatenate([gain[part : part + 1] for part in range(4)], axis=1)
+        wide = stream_ref[step].astype(jnp.float32)
+        pieces.append((wide * scale[...] * gain).astype(jnp.bfloat16))
+    left = jnp.concatenate(
+        [jnp.where(swap, pieces[1], pieces[0]), jnp.where(swap, pieces[0], pieces[1])], axis=1
+    )
+    gates[...] += jnp.dot(left, gate_ref[...], preferred_element_type=jnp.float32)
+    ups[...] += jnp.dot(left, up_ref[...], preferred_element_type=jnp.float32)
+
+    @pl.when(step == pl.num_programs(0) - 1)
+    def _():
+        out_ref[...] = (jax.nn.silu(gates[...]) * ups[...]).astype(jnp.bfloat16)
+
+
+def pair_of(step, table_ref):
+    distance = (step % 4) * 2 + step // 4
+    return (table_ref[0] // 2) ^ distance
+
+
+def hidden_units(table, stream, gain, gate_weight, up_weight):
+    rows = stream[0].shape[1]
+    width = gate_weight.shape[1]
+    depth = 2 * stream[0].shape[2]
+    whole = lambda array: pl.BlockSpec(array.shape, lambda step, table: (0,) * array.ndim)
+    weights = pl.BlockSpec((depth, width), lambda step, table: (pair_of(step, table), 0))
+    return pl.pallas_call(
+        hidden_kernel,
+        grid_spec=pltpu.PrefetchScalarGridSpec(
+            num_scalar_prefetch=1,
+            grid=(D // depth,),
+            in_specs=[whole(array) for array in (*stream, *gain)] + [weights] * 2,
+            out_specs=pl.BlockSpec((rows, width), lambda step, table: (0, 0)),
+            scratch_shapes=[
+                pltpu.VMEM((rows, 1), jnp.float32),
+                pltpu.VMEM((rows, width), jnp.float32),
+                pltpu.VMEM((rows, width), jnp.float32),
+            ],
+        ),
+        out_shape=jax.ShapeDtypeStruct((rows, width), jnp.bfloat16),
+        compiler_params=pltpu.CompilerParams(vmem_limit_bytes=32 * MIB),
+        cost_estimate=pl.CostEstimate(
+            flops=4 * rows * D * width, bytes_accessed=4 * D * width, transcendentals=rows * width
+        ),
+    )(table, *stream, *gain, gate_weight, up_weight)
+
+
+def down_kernel(table_ref, hidden_ref, weight_ref, out_ref):
+    out_ref[0] = jnp.dot(
+        hidden_ref[...], weight_ref[...], preferred_element_type=jnp.float32
+    ).astype(out_ref.dtype)
+
+
+def down_terms(table, hidden, down_weight, other, held_as):
+    rows, depth = hidden.shape
+    width = D // 16
+
+    def block(step, table_ref):
+        return (0, 2 * step + (table_ref[0] % 2 ^ other))
+
+    return pl.pallas_call(
+        down_kernel,
+        grid_spec=pltpu.PrefetchScalarGridSpec(
+            num_scalar_prefetch=1,
+            grid=(8,),
+            in_specs=[
+                pl.BlockSpec((rows, depth), lambda step, table: (0, 0)),
+                pl.BlockSpec((depth, width), block),
+            ],
+            out_specs=pl.BlockSpec((1, rows, width), lambda step, table: (step, 0, 0)),
+        ),
+        out_shape=jax.ShapeDtypeStruct((8, rows, width), held_as),
+        compiler_params=pltpu.CompilerParams(vmem_limit_bytes=32 * MIB),
+        cost_estimate=pl.CostEstimate(
+            flops=16 * rows * depth * width, bytes_accessed=16 * depth * width, transcendentals=0
+        ),
+    )(table, hidden, down_weight)
+
+
+def tables(page_table, lengths, page_count, page_len):
+    me = lax.axis_index("shard").astype(jnp.int32)
+    seqs, pages = page_table.shape
+    holder = page_table // page_count
+    row = (jnp.arange(seqs, dtype=jnp.int32) % 2)[:, None] + jnp.zeros_like(page_table)
+    left = lengths[:, None] - page_len * jnp.arange(pages, dtype=jnp.int32)[None, :]
+    found = (holder == me).reshape(-1, 2 * pages)
+    parts = [
+        jnp.sum(jnp.where(found, part.reshape(-1, 2 * pages), 0), axis=1)
+        for part in (page_table % page_count, row, left)
+    ]
+    own = lax.dynamic_slice_in_dim(holder, 2 * me, 2, 0)
+    sender = jnp.arange(16, dtype=jnp.int32)
+    parts.append(jnp.sum((own[1][None, :] == sender[:, None]).astype(jnp.int32), axis=1))
+    return jnp.concatenate([me[None]] + parts)
+
+
+def block_body(
+    queries,
+    new_kv,
+    kv_pages,
+    page_table,
+    lengths,
+    residual,
+    out_weight,
+    norm_gain,
+    gate_weight,
+    up_weight,
+    down_weight,
+):
+    table = tables(page_table, lengths, kv_pages.shape[0], kv_pages.shape[2])
+    own = packed(queries, norm_gain)
+    even, odd = gathered(own)
+    terms = page_terms(table, even, odd, kv_pages)
+    arrived = lax.all_to_all(terms, "shard", 0, 0)
+    attended = combined(table, arrived, own[: 2 * HEADS], new_kv)
+    stream = projected(table, *gathered(attended), residual, out_weight)
+    hidden = hidden_units(table, gathered(stream), (even, odd), gate_weight, up_weight)
+    theirs = sent(down_terms(table, hidden, down_weight, 1, jnp.bfloat16), 1)
+    mine = down_terms(table, hidden, down_weight, 0, jnp.float32)
+    pairs = (mine + theirs.astype(jnp.float32)).astype(jnp.bfloat16)
+    same_core = [[core + 2 * step for step in range(8)] for core in range(2)]
+    shares = lax.all_to_all(pairs, "shard", 0, 0, axis_index_groups=same_core)
+    return (stream.astype(jnp.float32) + jnp.sum(shares.astype(jnp.float32), axis=0)).astype(
+        jnp.bfloat16
+    )
+
+
 def solution(mesh):
     placed = (
         P(("groups", "shard"), None),
@@ -154,6 +508,7 @@
         P(None, "shard"),
         P("shard", None),
     )
+    chosen = block_body if mesh.shape["shard"] == 16 else body
     return jax.shard_map(
-        body, mesh=mesh, in_specs=placed, out_specs=P("groups", "shard"), check_vma=False
-    )
+        chosen, mesh=mesh, in_specs=placed, out_specs=P("groups", "shard"), check_vma=False
+    )

time: 243 us -> 140 us (0.58)
  waiting for transfers between devices: 99.5 us -> 37.2 us
  blocking collectives: 71.4 us -> 12.4 us
  Pallas kernels: 0 us -> 54.5 us
  matrix products: 38.9 us -> 0 us
  starting transfers between devices: 7.89 us -> 21.4 us
  between operations: 13.6 us -> 0.18 us
  local copies, waits for them, and re-layouts: 5.58 us -> 9.75 us
    reduce_scatter x1 -> x0, waiting for transfers between devices: 55.9 us -> none  [body(): lax.psum_scatter(partial_terms, 'shard', scatter_dimension=1, tiled=True)]
    pallas_call x0 -> x7, Pallas kernels: none -> 54.5 us  [the longest x1 20.6 us: hidden_units(): pl.pallas_call(hidden_kernel, grid_spec=pltpu.PrefetchScalarGridSpec(num_...]
    all_gather x2 -> x0, blocking collectives: 41.5 us -> none  [the longest x1 22.7 us: body(): lax.all_gather(attended, 'shard', axis=0, tiled=True)]
    dot_general x6 -> x0, matrix products: 38.9 us -> none  [the longest x1 21.4 us: body(): jnp.dot(hidden, down_weight, preferred_element_type=jnp.float32)]
    psum x1 -> x0, blocking collectives: 29.8 us -> none  [body(): square_sums = lax.psum(jnp.sum(wide * wide, axis=1), 'shard')]
    ppermute x4 -> x16, waiting for transfers between devices: 43.6 us -> 26.9 us  [sent(): lax.ppermute(array, 'shard', [(i, i ^ distance) for i in range(size)])]
    all_to_all x0 -> x1, blocking collectives: none -> 12.4 us  [block_body(): shares = lax.all_to_all(pairs, 'shard', 0, 0, axis_index_groups=same_core)]
    all_to_all x0 -> x1, waiting for transfers between devices: none -> 10.3 us  [block_body(): arrived = lax.all_to_all(terms, 'shard', 0, 0)]
  transfers between devices with their start and end apart: 5 -> 17, of which waited for: 5 -> 13; matrix products, arithmetic and copies ran while one was open for 2% -> 3% of each run, Pallas kernels for 0% -> 6%
where the time goes in v1:
time: 140 us; the launch traced here: 139 us
  Pallas kernels  54.5 us (39%)
  waiting for transfers between devices  37.2 us (27%)
  starting transfers between devices  21.4 us (15%)
  blocking collectives  12.4 us (9%)
  local copies, waits for them, and re-layouts  9.75 us (7%)
  other arithmetic  3.52 us (3%)
    ppermute x16, waiting for transfers between devices, sent(): lax.ppermute(array, 'shard', [(i, i ^ distance) for i in range(size)])  26.9 us
    pallas_call x1, Pallas kernels, hidden_units(): pl.pallas_call(hidden_kernel, grid_spec=pltpu.PrefetchScalarGridSpec(num_...  20.6 us
    ppermute x16, starting transfers between devices, sent(): lax.ppermute(array, 'shard', [(i, i ^ distance) for i in range(size)])  17.9 us
    pallas_call x2, Pallas kernels, down_terms(): pl.pallas_call(down_kernel, grid_spec=pltpu.PrefetchScalarGridSpec(num_sc...  17.7 us
    all_to_all x1, blocking collectives, block_body(): shares = lax.all_to_all(pairs, 'shard', 0, 0, axis_index_groups=same_core)  12.4 us
    all_to_all x1, waiting for transfers between devices, block_body(): arrived = lax.all_to_all(terms, 'shard', 0, 0)  10.3 us
    pallas_call x1, Pallas kernels, page_terms(): pl.pallas_call(pages_kernel, in_specs=[SMEM_SPEC] + [VMEM_SPEC] * 3, out_...  9.98 us
    unnamed x20, local copies, waits for them, and re-layouts  6.96 us
  transfers between devices with their start and end apart: 17, of which 13 were waited for; matrix products, arithmetic and copies ran while one was open for 3% of the time, Pallas kernels for 6%

profile of v1, /device:TPU:0, one launch (start us, length us, event | category | flops | bytes accessed | tf_op | source)
XLA Modules:
  0.0 139.0 jit_solution(8732274341129924358)
XLA Ops:
  0.0 1.4 %reshape.38.query_ref = bf16[128,128]{1,0:T(8,128)(2,1)} reshape(bf16[2,8192]{1,0:T(2,128)(2,1)} %param.11) | data formatting | bytes 65536 | tf_op jit(solution)/shard_map/reshape | solution.py:181
  2.8 3.0 %collective-permute-start = (bf16[144,128]{1,0:T(8,128)(2,1)}, bf16[144,128]{1,0:T(8,128)(2,1)S(1)}, u32[]{:S(2)}, u32[]{:S(2)}) collective-permute-start(bf16[144,128]{1,0:T(8,128)(2,1)} %shard_map.109), channel_id=1, source_target_pairs={{0,4},{1,5},{2,6},{3,7},{4,0},{5,1},{6,2},{7,3},{8,12},{9,13},{10,... | collective-permute-start | bytes 110600 | tf_op jit(solution)/shard_map/ppermute | solution.py:154
  5.8 2.6 %collective-permute-start.1 = (bf16[144,128]{1,0:T(8,128)(2,1)}, bf16[144,128]{1,0:T(8,128)(2,1)S(1)}, u32[]{:S(2)}, u32[]{:S(2)}) collective-permute-start(bf16[144,128]{1,0:T(8,128)(2,1)} %shard_map.109), channel_id=1, source_target_pairs={{0,8},{1,9},{2,10},{3,11},{4,12},{5,13},{6,14},{7,15},{8,0},{9,1},... | collective-permute-start | bytes 110600 | tf_op jit(solution)/shard_map/ppermute | solution.py:154
  11.6 2.8 %collective-permute-done.2 = bf16[144,128]{1,0:T(8,128)(2,1)S(1)} collective-permute-done((bf16[144,128]{1,0:T(8,128)(2,1)}, bf16[144,128]{1,0:T(8,128)(2,1)S(1)}, u32[]{:S(2)}, u32[]{:S(2)}) %collective-permute-start.2) | collective-permute-done | bytes 36896 | tf_op jit(solution)/shard_map/ppermute | solution.py:154
  15.2 1.6 %collective-permute-start.3 = (bf16[4,144,128]{2,1,0:T(8,128)(2,1)S(1)}, bf16[4,144,128]{2,1,0:T(8,128)(2,1)S(1)}, u32[]{:S(2)}, u32[]{:S(2)}) collective-permute-start(bf16[4,144,128]{2,1,0:T(8,128)(2,1)S(1)} %pad_maximum_fusion), channel_id=1, source_target_pairs={{0,2},{1,3},{2,0},{3,1},{4,6},{5,7},{6,4},{7,5},{8,10},{9,11},{10,... | collective-permute-start | bytes 442376 | tf_op jit(solution)/shard_map/ppermute | solution.py:154
  16.8 3.6 %collective-permute-done.3 = bf16[4,144,128]{2,1,0:T(8,128)(2,1)S(1)} collective-permute-done((bf16[4,144,128]{2,1,0:T(8,128)(2,1)S(1)}, bf16[4,144,128]{2,1,0:T(8,128)(2,1)S(1)}, u32[]{:S(2)}, u32[]{:S(2)}) %collective-permute-start.3) | collective-permute-done | bytes 147488 | tf_op jit(solution)/shard_map/ppermute | solution.py:154
  23.3 10.0 %shard_map.110 = bf16[16,80,128]{2,1,0:T(8,128)(2,1)} custom-call(s32[65]{0:T(128)S(1)} %concatenate.15.table_ref, bf16[8,144,128]{2,1,0:T(8,128)(2,1)S(1)} %constant_dynamic-update-slice_fusion.even_ref.even_gain, bf16[8,144,128]{2,1,0:T(8,128)(2,1)S(1)} %collective-permute-done.4.odd_ref.odd_gain, bf16[16,2,32,512]{3,2,1,0:T(8,128)(2,1)S(1)} %copy-done.1), custom_call_target="tpu_custom_call" | custom-call | flops 134217728 | bytes 2097152 | tf_op jit(solution)/shard_map/pallas_call | solution.py:236
  33.3 3.5 %all-to-all-start = ((bf16[16,80,128]{2,1,0:T(8,128)(2,1)}), bf16[16,80,128]{2,1,0:T(8,128)(2,1)S(1)}, u32[]{:S(2)}, u32[]{:S(2)}) async-start(bf16[16,80,128]{2,1,0:T(8,128)(2,1)} %shard_map.110), calls=%async_computation | async-start | bytes 655360 | tf_op jit(solution)/shard_map/all_to_all | solution.py:483
  37.6 10.3 %all-to-all-done.arrived_ref = bf16[16,80,128]{2,1,0:T(8,128)(2,1)S(1)} async-done(((bf16[16,80,128]{2,1,0:T(8,128)(2,1)}), bf16[16,80,128]{2,1,0:T(8,128)(2,1)S(1)}, u32[]{:S(2)}, u32[]{:S(2)}) %all-to-all-start) | async-done | bytes 327712 | tf_op jit(solution)/shard_map/all_to_all | solution.py:483
  51.3 2.7 %collective-permute-start.7 = (bf16[128,128]{1,0:T(8,128)(2,1)S(1)}, bf16[128,128]{1,0:T(8,128)(2,1)S(1)}, u32[]{:S(2)}, u32[]{:S(2)}) collective-permute-start(bf16[128,128]{1,0:T(8,128)(2,1)S(1)} %shard_map.111), channel_id=1, source_target_pairs={{0,12},{1,13},{2,14},{3,15},{4,8},{5,9},{6,10},{7,11},{8,4},{9,5},... | collective-permute-start | bytes 98312 | tf_op jit(solution)/shard_map/ppermute | solution.py:154
  55.3 1.8 %collective-permute-done.7 = bf16[128,128]{1,0:T(8,128)(2,1)S(1)} collective-permute-done((bf16[128,128]{1,0:T(8,128)(2,1)S(1)}, bf16[128,128]{1,0:T(8,128)(2,1)S(1)}, u32[]{:S(2)}, u32[]{:S(2)}) %collective-permute-start.7) | collective-permute-done | bytes 32800 | tf_op jit(solution)/shard_map/ppermute | solution.py:154
  57.1 1.4 %collective-permute-start.8 = (bf16[4,128,128]{2,1,0:T(8,128)(2,1)S(1)}, bf16[4,128,128]{2,1,0:T(8,128)(2,1)S(1)}, u32[]{:S(2)}, u32[]{:S(2)}) collective-permute-start(bf16[4,128,128]{2,1,0:T(8,128)(2,1)S(1)} %pad_maximum_fusion.1), channel_id=1, source_target_pairs={{0,2},{1,3},{2,0},{3,1},{4,6},{5,7},{6,4},{7,5},{8,10},{9,11},{10,... | collective-permute-start | bytes 393224 | tf_op jit(solution)/shard_map/ppermute | solution.py:154
  58.5 3.6 %collective-permute-done.8 = bf16[4,128,128]{2,1,0:T(8,128)(2,1)S(1)} collective-permute-done((bf16[4,128,128]{2,1,0:T(8,128)(2,1)S(1)}, bf16[4,128,128]{2,1,0:T(8,128)(2,1)S(1)}, u32[]{:S(2)}, u32[]{:S(2)}) %collective-permute-start.8) | collective-permute-done | bytes 131104 | tf_op jit(solution)/shard_map/ppermute | solution.py:154
  62.2 1.5 %collective-permute-done.9.odd_ref = bf16[8,128,128]{2,1,0:T(8,128)(2,1)S(1)} collective-permute-done((bf16[8,128,128]{2,1,0:T(8,128)(2,1)S(1)}, bf16[8,128,128]{2,1,0:T(8,128)(2,1)S(1)}, u32[]{:S(2)}, u32[]{:S(2)}) %collective-permute-start.9) | collective-permute-done | bytes 262176 | tf_op jit(solution)/shard_map/ppermute | solution.py:154
  63.7 3.4 %copy-done = bf16[8192,512]{1,0:T(8,128)(2,1)S(1)} copy-done((bf16[8192,512]{1,0:T(8,128)(2,1)S(1)}, bf16[8192,512]{1,0:T(8,128)(2,1)}, u32[]{:S(2)}) %copy-start) | copy-done | bytes 8388632
  67.9 3.8 %shard_map.112 = bf16[32,512]{1,0:T(8,128)(2,1)S(1)} custom-call(s32[65]{0:T(128)S(1)} %concatenate.15.table_ref, bf16[8,128,128]{2,1,0:T(8,128)(2,1)S(1)} %constant_dynamic-update-slice_fusion.5.even_ref, bf16[8,128,128]{2,1,0:T(8,128)(2,1)S(1)} %collective-permute-done.9.odd_ref, bf16[32,512]{1,0:T(8,128)(2,1)S(1)} %copy-done.2, bf16[8192,512]{1,0:T(8,128)(2,1)S(1)} %copy-done), custom_call_target="tpu_custom_call" | custom-call | flops 268435456 | bytes 8388608 | tf_op jit(solution)/shard_map/pallas_call | solution.py:330
  71.8 3.1 %collective-permute-start.11 = (bf16[32,512]{1,0:T(8,128)(2,1)S(1)}, bf16[32,512]{1,0:T(8,128)(2,1)S(1)}, u32[]{:S(2)}, u32[]{:S(2)}) collective-permute-start(bf16[32,512]{1,0:T(8,128)(2,1)S(1)} %shard_map.112), channel_id=1, source_target_pairs={{0,8},{1,9},{2,10},{3,11},{4,12},{5,13},{6,14},{7,15},{8,0},{9,1},... | collective-permute-start | bytes 98312 | tf_op jit(solution)/shard_map/ppermute | solution.py:154
  77.4 3.2 %collective-permute-done.12 = bf16[32,512]{1,0:T(8,128)(2,1)S(1)} collective-permute-done((bf16[32,512]{1,0:T(8,128)(2,1)S(1)}, bf16[32,512]{1,0:T(8,128)(2,1)S(1)}, u32[]{:S(2)}, u32[]{:S(2)}) %collective-permute-start.12) | collective-permute-done | bytes 32800 | tf_op jit(solution)/shard_map/ppermute | solution.py:154
  80.8 4.9 %collective-permute-done.13 = bf16[4,32,512]{2,1,0:T(8,128)(2,1)S(1)} collective-permute-done((bf16[4,32,512]{2,1,0:T(8,128)(2,1)S(1)}, bf16[4,32,512]{2,1,0:T(8,128)(2,1)S(1)}, u32[]{:S(2)}, u32[]{:S(2)}) %collective-permute-start.13) | collective-permute-done | bytes 131104 | tf_op jit(solution)/shard_map/ppermute | solution.py:154
  85.8 1.5 %collective-permute-done.14.odd_ref = bf16[8,32,512]{2,1,0:T(8,128)(2,1)S(1)} collective-permute-done((bf16[8,32,512]{2,1,0:T(8,128)(2,1)S(1)}, bf16[8,32,512]{2,1,0:T(8,128)(2,1)S(1)}, u32[]{:S(2)}, u32[]{:S(2)}) %collective-permute-start.14) | collective-permute-done | bytes 262176 | tf_op jit(solution)/shard_map/ppermute | solution.py:154
  87.3 20.6 %shard_map.113.hidden_ref = bf16[32,1664]{1,0:T(8,128)(2,1)S(1)} custom-call(s32[65]{0:T(128)S(1)} %concatenate.15.table_ref, bf16[8,32,512]{2,1,0:T(8,128)(2,1)S(1)} %constant_dynamic-update-slice_fusion.10.even_ref, bf16[8,32,512]{2,1,0:T(8,128)(2,1)S(1)} %collective-permute-done.14.odd_ref, ...), custom_call_target="tpu_custom_call" | custom-call | flops 1744830464 | bytes 54525952 | tf_op jit(solution)/shard_map/pallas_call | solution.py:396
  107.9 8.9 %shard_map.115 = bf16[8,32,512]{2,1,0:T(8,128)(2,1)S(1)} custom-call(s32[65]{0:T(128)S(1)} %concatenate.15.table_ref, bf16[32,1664]{1,0:T(8,128)(2,1)S(1)} %shard_map.113.hidden_ref, bf16[1664,8192]{1,0:T(8,128)(2,1)} %weight_ref.5), custom_call_target="tpu_custom_call" | custom-call | flops 436207616 | bytes 13631488 | tf_op jit(solution)/shard_map/pallas_call | solution.py:430
  116.9 8.8 %shard_map.114 = f32[8,32,512]{2,1,0:T(8,128)S(1)} custom-call(s32[65]{0:T(128)S(1)} %concatenate.15.table_ref, bf16[32,1664]{1,0:T(8,128)(2,1)S(1)} %shard_map.113.hidden_ref, bf16[1664,8192]{1,0:T(8,128)(2,1)} %weight_ref.5), custom_call_target="tpu_custom_call" | custom-call | flops 436207616 | bytes 13631488 | tf_op jit(solution)/shard_map/pallas_call | solution.py:430
  125.9 12.4 %all_to_all.10 = bf16[8,32,512]{2,1,0:T(8,128)(2,1)S(1)} all-to-all(bf16[8,32,512]{2,1,0:T(8,128)(2,1)S(1)} %add_convert_fusion), channel_id=1, replica_groups={{0,2,4,6,8,10,12,14},{1,3,5,7,9,11,13,15},{16,18,20,22,24,26,28,30},{17..., dimensions={0} | all-to-all | bytes 524288 | tf_op jit(solution)/shard_map/all_to_all | solution.py:491
  (63 shorter events, 18.3 us)
Async XLA Ops:
  2.8 8.6 %collective-permute-start = (bf16[144,128]{1,0:T(8,128)(2,1)}, bf16[144,128]{1,0:T(8,128)(2,1)S(1)}, u32[]{:S(2)}, u32[]{:S(2)}) collective-permute-start(bf16[144,128]{1,0:T(8,128)(2,1)} %shard_map.109), channel_id=1, source_target_pairs={{0,4},{1,5},{2,6},{3,7},{4,0},{5,1},{6,2},{7,3},{8,12},{9,13},{10,... | collective-permute-start | bytes 110600 | tf_op jit(solution)/shard_map/ppermute | solution.py:154
  5.8 5.7 %collective-permute-start.1 = (bf16[144,128]{1,0:T(8,128)(2,1)}, bf16[144,128]{1,0:T(8,128)(2,1)S(1)}, u32[]{:S(2)}, u32[]{:S(2)}) collective-permute-start(bf16[144,128]{1,0:T(8,128)(2,1)} %shard_map.109), channel_id=1, source_target_pairs={{0,8},{1,9},{2,10},{3,11},{4,12},{5,13},{6,14},{7,15},{8,0},{9,1},... | collective-permute-start | bytes 110600 | tf_op jit(solution)/shard_map/ppermute | solution.py:154
  8.4 6.0 %collective-permute-start.2 = (bf16[144,128]{1,0:T(8,128)(2,1)}, bf16[144,128]{1,0:T(8,128)(2,1)S(1)}, u32[]{:S(2)}, u32[]{:S(2)}) collective-permute-start(bf16[144,128]{1,0:T(8,128)(2,1)} %shard_map.109), channel_id=1, source_target_pairs={{0,12},{1,13},{2,14},{3,15},{4,8},{5,9},{6,10},{7,11},{8,4},{9,5},... | collective-permute-start | bytes 110600 | tf_op jit(solution)/shard_map/ppermute | solution.py:154
  15.2 5.2 %collective-permute-start.3 = (bf16[4,144,128]{2,1,0:T(8,128)(2,1)S(1)}, bf16[4,144,128]{2,1,0:T(8,128)(2,1)S(1)}, u32[]{:S(2)}, u32[]{:S(2)}) collective-permute-start(bf16[4,144,128]{2,1,0:T(8,128)(2,1)S(1)} %pad_maximum_fusion), channel_id=1, source_target_pairs={{0,2},{1,3},{2,0},{3,1},{4,6},{5,7},{6,4},{7,5},{8,10},{9,11},{10,... | collective-permute-start | bytes 442376 | tf_op jit(solution)/shard_map/ppermute | solution.py:154
  20.4 1.6 %collective-permute-start.4 = (bf16[8,144,128]{2,1,0:T(8,128)(2,1)S(1)}, bf16[8,144,128]{2,1,0:T(8,128)(2,1)S(1)}, u32[]{:S(2)}, u32[]{:S(2)}) collective-permute-start(bf16[8,144,128]{2,1,0:T(8,128)(2,1)S(1)} %constant_dynamic-update-slice_fusion.even_ref.even_gain), channel_id=1, source_target_pairs={{0,1},{1,0},{2,3},{3,2},{4,5},{5,4},{6,7},{7,6},{8,9},{9,8},{10,11... | collective-permute-start | bytes 884744 | tf_op jit(solution)/shard_map/ppermute | solution.py:154
  22.0 1.2 copy-start.1
  33.3 14.6 %all-to-all-start = ((bf16[16,80,128]{2,1,0:T(8,128)(2,1)}), bf16[16,80,128]{2,1,0:T(8,128)(2,1)S(1)}, u32[]{:S(2)}, u32[]{:S(2)}) async-start(bf16[16,80,128]{2,1,0:T(8,128)(2,1)} %shard_map.110), calls=%async_computation | async-start | bytes 655360 | tf_op jit(solution)/shard_map/all_to_all | solution.py:483
  47.9 0.7 copy-start.3
  49.6 4.5 %collective-permute-start.5 = (bf16[128,128]{1,0:T(8,128)(2,1)S(1)}, bf16[128,128]{1,0:T(8,128)(2,1)S(1)}, u32[]{:S(2)}, u32[]{:S(2)}) collective-permute-start(bf16[128,128]{1,0:T(8,128)(2,1)S(1)} %shard_map.111), channel_id=1, source_target_pairs={{0,4},{1,5},{2,6},{3,7},{4,0},{5,1},{6,2},{7,3},{8,12},{9,13},{10,... | collective-permute-start | bytes 98312 | tf_op jit(solution)/shard_map/ppermute | solution.py:154
  49.9 5.4 %collective-permute-start.6 = (bf16[128,128]{1,0:T(8,128)(2,1)S(1)}, bf16[128,128]{1,0:T(8,128)(2,1)S(1)}, u32[]{:S(2)}, u32[]{:S(2)}) collective-permute-start(bf16[128,128]{1,0:T(8,128)(2,1)S(1)} %shard_map.111), channel_id=1, source_target_pairs={{0,8},{1,9},{2,10},{3,11},{4,12},{5,13},{6,14},{7,15},{8,0},{9,1},... | collective-permute-start | bytes 98312 | tf_op jit(solution)/shard_map/ppermute | solution.py:154
  51.3 5.7 %collective-permute-start.7 = (bf16[128,128]{1,0:T(8,128)(2,1)S(1)}, bf16[128,128]{1,0:T(8,128)(2,1)S(1)}, u32[]{:S(2)}, u32[]{:S(2)}) collective-permute-start(bf16[128,128]{1,0:T(8,128)(2,1)S(1)} %shard_map.111), channel_id=1, source_target_pairs={{0,12},{1,13},{2,14},{3,15},{4,8},{5,9},{6,10},{7,11},{8,4},{9,5},... | collective-permute-start | bytes 98312 | tf_op jit(solution)/shard_map/ppermute | solution.py:154
  57.1 5.0 %collective-permute-start.8 = (bf16[4,128,128]{2,1,0:T(8,128)(2,1)S(1)}, bf16[4,128,128]{2,1,0:T(8,128)(2,1)S(1)}, u32[]{:S(2)}, u32[]{:S(2)}) collective-permute-start(bf16[4,128,128]{2,1,0:T(8,128)(2,1)S(1)} %pad_maximum_fusion.1), channel_id=1, source_target_pairs={{0,2},{1,3},{2,0},{3,1},{4,6},{5,7},{6,4},{7,5},{8,10},{9,11},{10,... | collective-permute-start | bytes 393224 | tf_op jit(solution)/shard_map/ppermute | solution.py:154
  62.1 1.6 %collective-permute-start.9 = (bf16[8,128,128]{2,1,0:T(8,128)(2,1)S(1)}, bf16[8,128,128]{2,1,0:T(8,128)(2,1)S(1)}, u32[]{:S(2)}, u32[]{:S(2)}) collective-permute-start(bf16[8,128,128]{2,1,0:T(8,128)(2,1)S(1)} %constant_dynamic-update-slice_fusion.5.even_ref), channel_id=1, source_target_pairs={{0,1},{1,0},{2,3},{3,2},{4,5},{5,4},{6,7},{7,6},{8,9},{9,8},{10,11... | collective-permute-start | bytes 786440 | tf_op jit(solution)/shard_map/ppermute | solution.py:154
  63.7 3.4 %copy-start = (bf16[8192,512]{1,0:T(8,128)(2,1)S(1)}, bf16[8192,512]{1,0:T(8,128)(2,1)}, u32[]{:S(2)}) copy-start(bf16[8192,512]{1,0:T(8,128)(2,1)} %weight_ref.3) | copy-start | bytes 25165828
  67.1 0.8 copy-start.2
  71.6 4.4 %collective-permute-start.10 = (bf16[32,512]{1,0:T(8,128)(2,1)S(1)}, bf16[32,512]{1,0:T(8,128)(2,1)S(1)}, u32[]{:S(2)}, u32[]{:S(2)}) collective-permute-start(bf16[32,512]{1,0:T(8,128)(2,1)S(1)} %shard_map.112), channel_id=1, source_target_pairs={{0,4},{1,5},{2,6},{3,7},{4,0},{5,1},{6,2},{7,3},{8,12},{9,13},{10,... | collective-permute-start | bytes 98312 | tf_op jit(solution)/shard_map/ppermute | solution.py:154
  71.8 5.6 %collective-permute-start.11 = (bf16[32,512]{1,0:T(8,128)(2,1)S(1)}, bf16[32,512]{1,0:T(8,128)(2,1)S(1)}, u32[]{:S(2)}, u32[]{:S(2)}) collective-permute-start(bf16[32,512]{1,0:T(8,128)(2,1)S(1)} %shard_map.112), channel_id=1, source_target_pairs={{0,8},{1,9},{2,10},{3,11},{4,12},{5,13},{6,14},{7,15},{8,0},{9,1},... | collective-permute-start | bytes 98312 | tf_op jit(solution)/shard_map/ppermute | solution.py:154
  75.0 5.7 %collective-permute-start.12 = (bf16[32,512]{1,0:T(8,128)(2,1)S(1)}, bf16[32,512]{1,0:T(8,128)(2,1)S(1)}, u32[]{:S(2)}, u32[]{:S(2)}) collective-permute-start(bf16[32,512]{1,0:T(8,128)(2,1)S(1)} %shard_map.112), channel_id=1, source_target_pairs={{0,12},{1,13},{2,14},{3,15},{4,8},{5,9},{6,10},{7,11},{8,4},{9,5},... | collective-permute-start | bytes 98312 | tf_op jit(solution)/shard_map/ppermute | solution.py:154
  80.7 5.0 %collective-permute-start.13 = (bf16[4,32,512]{2,1,0:T(8,128)(2,1)S(1)}, bf16[4,32,512]{2,1,0:T(8,128)(2,1)S(1)}, u32[]{:S(2)}, u32[]{:S(2)}) collective-permute-start(bf16[4,32,512]{2,1,0:T(8,128)(2,1)S(1)} %pad_maximum_fusion.2), channel_id=1, source_target_pairs={{0,2},{1,3},{2,0},{3,1},{4,6},{5,7},{6,4},{7,5},{8,10},{9,11},{10,... | collective-permute-start | bytes 393224 | tf_op jit(solution)/shard_map/ppermute | solution.py:154
  85.7 1.6 %collective-permute-start.14 = (bf16[8,32,512]{2,1,0:T(8,128)(2,1)S(1)}, bf16[8,32,512]{2,1,0:T(8,128)(2,1)S(1)}, u32[]{:S(2)}, u32[]{:S(2)}) collective-permute-start(bf16[8,32,512]{2,1,0:T(8,128)(2,1)S(1)} %constant_dynamic-update-slice_fusion.10.even_ref), channel_id=1, source_target_pairs={{0,1},{1,0},{2,3},{3,2},{4,5},{5,4},{6,7},{7,6},{8,9},{9,8},{10,11... | collective-permute-start | bytes 786440 | tf_op jit(solution)/shard_map/ppermute | solution.py:154
  116.8 9.0 %collective-permute-start.15 = (bf16[8,32,512]{2,1,0:T(8,128)(2,1)S(1)}, bf16[8,32,512]{2,1,0:T(8,128)(2,1)S(1)}, u32[]{:S(2)}, u32[]{:S(2)}) collective-permute-start(bf16[8,32,512]{2,1,0:T(8,128)(2,1)S(1)} %shard_map.115), channel_id=1, source_target_pairs={{0,1},{1,0},{2,3},{3,2},{4,5},{5,4},{6,7},{7,6},{8,9},{9,8},{10,11... | collective-permute-start | bytes 786440 | tf_op jit(solution)/shard_map/ppermute | solution.py:154

commit v2 on v0

--- a/solution.py
+++ b/solution.py
@@ -1,8 +1,11 @@
+import functools
 import math
 
 import jax
 import jax.numpy as jnp
 from jax import lax
+from jax.experimental import pallas as pl
+from jax.experimental.pallas import tpu as pltpu
 from jax.sharding import PartitionSpec as P
 
 D = 8192
@@ -140,6 +143,704 @@
     return (wide + down_terms).astype(jnp.bfloat16)
 
 
+GROUP = HEADS // KV_HEADS
+HEAD_ROWS = 72
+MIB = 2**20
+VMEM_SPEC = pl.BlockSpec(memory_space=pltpu.VMEM)
+SMEM_SPEC = pl.BlockSpec(memory_space=pltpu.SMEM)
+HBM_SPEC = pl.BlockSpec(memory_space=pltpu.HBM)
+CHUNK = 512
+
+
+def sent(array, distance):
+    size = lax.axis_size("shard")
+    return lax.ppermute(array, "shard", [(i, i ^ distance) for i in range(size)])
+
+
+def stack_kernel(count, *refs):
+    out_ref, place = refs[-1], 0
+    for part in refs[:count]:
+        size = part.shape[0] if len(part.shape) == 3 else 1
+        out_ref[place : place + size] = part[...].reshape((size,) + part.shape[-2:])
+        place += size
+
+
+def stacked(parts, after):
+    size = sum(part.shape[0] if part.ndim == 3 else 1 for part in parts)
+    return pl.pallas_call(
+        functools.partial(stack_kernel, len(parts)),
+        in_specs=[VMEM_SPEC] * len(parts) + [pl.BlockSpec(memory_space=pl.ANY)] * len(after),
+        out_specs=VMEM_SPEC,
+        out_shape=jax.ShapeDtypeStruct((size,) + parts[0].shape[-2:], parts[0].dtype),
+        compiler_params=pltpu.CompilerParams(vmem_limit_bytes=4 * MIB),
+        cost_estimate=pl.CostEstimate(flops=0, bytes_accessed=16 * MIB, transcendentals=0),
+    )(*parts, *after)
+
+
+def near_pieces(piece):
+    return [piece] + [sent(piece, distance) for distance in (4, 8, 12)]
+
+
+PEER = (0, 4, 8, 12, 2, 6, 10, 14)
+
+
+def device_at(me, entry):
+    return me ^ (PEER[entry % 8] + entry // 8)
+
+
+def in_vmem(array):
+    return pltpu.with_memory_space_constraint(array, pltpu.VMEM)
+
+
+def in_hbm(array):
+    return pltpu.with_memory_space_constraint(array, pltpu.HBM)
+
+
+def two_terms(wide):
+    high = wide.astype(jnp.bfloat16).astype(jnp.float32)
+    return high, wide - high
+
+
+def pack_kernel(query_hbm, gain_hbm, out_ref, rows_ref, query, gain, wide, sems):
+    copies = [
+        pltpu.make_async_copy(query_hbm, query, sems.at[0]),
+        pltpu.make_async_copy(gain_hbm, gain, sems.at[1]),
+    ]
+    for copy in copies:
+        copy.start()
+    for copy in copies:
+        copy.wait()
+    rows = 2 * HEADS
+    for head in range(HEADS):
+        cols = slice(head * HEAD_DIM, (head + 1) * HEAD_DIM)
+        wide[pl.ds(head, 2, HEADS), :] = query[:, cols].astype(jnp.float32)
+    out_ref[:rows, :] = wide[...].astype(jnp.bfloat16)
+    rows_ref[...] = wide[...].astype(jnp.bfloat16)
+    high, rest = two_terms(gain[...])
+    middle, low = two_terms(rest)
+    filler = jnp.zeros((16 - 3 * high.shape[0], HEAD_DIM), jnp.float32)
+    out_ref[rows:, :] = jnp.concatenate([high, middle, low, filler]).astype(jnp.bfloat16)
+
+
+def packed(queries, norm_gain):
+    rows = 2 * HEADS
+    gain = norm_gain.reshape(-1, HEAD_DIM)
+    return pl.pallas_call(
+        pack_kernel,
+        in_specs=[HBM_SPEC] * 2,
+        out_specs=[VMEM_SPEC] * 2,
+        out_shape=[
+            jax.ShapeDtypeStruct((rows + 16, HEAD_DIM), jnp.bfloat16),
+            jax.ShapeDtypeStruct((rows, HEAD_DIM), jnp.bfloat16),
+        ],
+        scratch_shapes=[
+            pltpu.VMEM(queries.shape, jnp.bfloat16),
+            pltpu.VMEM(gain.shape, jnp.float32),
+            pltpu.VMEM((rows, HEAD_DIM), jnp.float32),
+            pltpu.SemaphoreType.DMA((2,)),
+        ],
+        compiler_params=pltpu.CompilerParams(vmem_limit_bytes=4 * MIB),
+    )(in_hbm(queries), in_hbm(gain))
+
+
+def context_terms(query, keys, values, alive):
+    numerators, denominators = [], []
+    for head in range(KV_HEADS):
+        cols = slice(head * HEAD_DIM, (head + 1) * HEAD_DIM)
+        scores = lax.dot_general(
+            query[head * GROUP : (head + 1) * GROUP],
+            keys[:, cols],
+            (((1,), (1,)), ((), ())),
+            preferred_element_type=jnp.float32,
+        ) * (1.0 / math.sqrt(HEAD_DIM))
+        weights = jnp.where(alive, jnp.exp(scores), 0.0)
+        denominators.append(jnp.sum(weights, axis=1, keepdims=True))
+        numerators.append(
+            jnp.dot(
+                weights.astype(jnp.bfloat16), values[:, cols], preferred_element_type=jnp.float32
+            )
+        )
+    return jnp.concatenate(numerators), jnp.concatenate(denominators)
+
+
+def ready_kernel(table_ref, query_ref, pages_hbm, new_hbm, pages, found_ref, new_ref, of_second, new, sems):
+    count, _, page_len, features = pages.shape
+    sequences = 2 * 16
+    per_row = (table_ref.shape[0] - 1) // sequences - 1
+    me = table_ref[(per_row + 1) * sequences]
+    copies = [pltpu.make_async_copy(new_hbm, new, sems.at[4])]
+    for part in range(4):
+        here = pl.ds(part * count // 4, count // 4)
+        copies.append(
+            pltpu.make_async_copy(pages_hbm.at[here], pages.at[here], sems.at[part])
+        )
+    for copy in copies:
+        copy.start()
+    found_ref[0] = me
+    for entry in range(16):
+        owner = device_at(me, entry)
+        place = 0
+        for index in range(2 * per_row):
+            hit = table_ref[2 * owner * per_row + index] // count == me
+            place = jnp.where(hit, index, place)
+        slot = table_ref[2 * owner * per_row + place] % count
+        row = place // per_row
+        left = table_ref[sequences * per_row + 2 * owner + row] - page_len * (place % per_row)
+        for place, value in enumerate((slot, row, left)):
+            found_ref[1 + 3 * entry + place] = value
+    for index in range(2 * per_row):
+        holder = table_ref[2 * me * per_row + index] // count
+        of_second[pl.ds(holder, 1), :] = jnp.full(
+            (1, HEAD_DIM), index // per_row, dtype=jnp.float32
+        )
+    first_token = lax.broadcasted_iota(jnp.int32, (GROUP, 8), 1) < 1
+    copies[0].wait()
+    for row in range(2):
+        lines = slice(row * HEADS, (row + 1) * HEADS)
+        numerator, total = context_terms(
+            query_ref[lines, :],
+            jnp.broadcast_to(new[row, 0:1, :], (8, features)),
+            jnp.broadcast_to(new[row, 1:2, :], (8, features)),
+            first_token,
+        )
+        new_ref[0, lines, :] = numerator
+        new_ref[1, lines, :] = jnp.broadcast_to(total, (HEADS, HEAD_DIM))
+    for copy in copies[1:]:
+        copy.wait()
+
+
+def readied(table, query_rows, kv_pages, new_kv):
+    return pl.pallas_call(
+        ready_kernel,
+        in_specs=[SMEM_SPEC, VMEM_SPEC] + [HBM_SPEC] * 2,
+        out_specs=[VMEM_SPEC, SMEM_SPEC, VMEM_SPEC, VMEM_SPEC],
+        out_shape=[
+            pltpu.VMEM(kv_pages.shape, kv_pages.dtype),
+            jax.ShapeDtypeStruct((49,), jnp.int32),
+            jax.ShapeDtypeStruct((2, 2 * HEADS, HEAD_DIM), jnp.float32),
+            jax.ShapeDtypeStruct((16, HEAD_DIM), jnp.float32),
+        ],
+        scratch_shapes=[pltpu.VMEM(new_kv.shape, jnp.bfloat16), pltpu.SemaphoreType.DMA((5,))],
+        compiler_params=pltpu.CompilerParams(vmem_limit_bytes=4 * MIB),
+        cost_estimate=pl.CostEstimate(flops=2**22, bytes_accessed=2**21, transcendentals=2**11),
+    )(table, query_rows, in_hbm(kv_pages), in_hbm(new_kv))
+
+
+def pages_kernel(entries, found_ref, *refs):
+    refs = list(refs)
+    near_ref, second_ref = (refs.pop(0), refs.pop(0)) if entries[0] == 0 else (None, None)
+    odd_ref = None if entries[0] == 0 else refs.pop(0)
+    pages = refs.pop(0)
+    if entries[0] > 0:
+        refs.pop(0)
+    out_ref, scores, weights = refs
+    page_len, features = pages.shape[2:]
+    me = found_ref[0]
+    line = lax.broadcasted_iota(jnp.int32, (HEADS, features), 0) // GROUP
+    block = lax.broadcasted_iota(jnp.int32, (HEADS, features), 1) // HEAD_DIM
+    own_block = (line == block).astype(jnp.float32).astype(jnp.bfloat16)
+    slots = [found_ref[1 + 3 * entry] for entry in entries]
+    for here, entry in enumerate(entries):
+        source, place = piece_at(near_ref, second_ref, odd_ref, entry)
+        row = found_ref[2 + 3 * entry]
+        query = source[place, pl.ds(pl.multiple_of(row * HEADS, HEADS), HEADS), :]
+        spread = jnp.concatenate([query] * KV_HEADS, axis=1) * own_block
+        scores[here] = lax.dot_general(
+            spread,
+            pages[slots[here], 0],
+            (((1,), (1,)), ((), ())),
+            preferred_element_type=jnp.float32,
+        )
+    position = lax.broadcasted_iota(jnp.int32, (HEADS, page_len), 1)
+    lane = lax.broadcasted_iota(jnp.int32, (HEADS, HEAD_DIM), 1)
+    denominators = jnp.zeros((HEADS, HEAD_DIM), jnp.float32)
+    for here, entry in enumerate(entries):
+        raised = jnp.exp(scores[here] * (1.0 / math.sqrt(HEAD_DIM)))
+        weight = jnp.where(position < found_ref[3 + 3 * entry], raised, 0.0)
+        weights[here] = weight.astype(jnp.bfloat16)
+        total = jnp.sum(weight, axis=1, keepdims=True)
+        denominators = jnp.where(lane == here, total, denominators)
+    for here, entry in enumerate(entries):
+        numerator = jnp.dot(
+            weights[here], pages[slots[here], 1], preferred_element_type=jnp.float32
+        )
+        for head in range(KV_HEADS):
+            lines = slice(head * GROUP, (head + 1) * GROUP)
+            out_ref[device_at(me, entry), lines, :] = numerator[
+                lines, head * HEAD_DIM : (head + 1) * HEAD_DIM
+            ].astype(jnp.bfloat16)
+    high, low = two_terms(jnp.swapaxes(denominators, 0, 1)[: len(entries)])
+    lasts = jnp.concatenate([high, low], axis=1)
+    first_line = lax.broadcasted_iota(jnp.int32, (HEAD_ROWS - HEADS, HEAD_DIM), 0) == 0
+    for here, entry in enumerate(entries):
+        out_ref[device_at(me, entry), HEADS:, :] = jnp.where(
+            first_line, lasts[here : here + 1], 0.0
+        ).astype(jnp.bfloat16)
+
+
+def piece_at(near, second, odd, entry):
+    if entry < 4:
+        return near, entry
+    return (second, entry - 4) if entry < 8 else (odd, entry - 8)
+
+
+def page_terms(found, entries, pieces, pages, before=()):
+    return pl.pallas_call(
+        functools.partial(pages_kernel, entries),
+        in_specs=[SMEM_SPEC] + [VMEM_SPEC] * (len(pieces) + 1 + len(before)),
+        out_specs=VMEM_SPEC,
+        out_shape=jax.ShapeDtypeStruct((16, HEAD_ROWS, HEAD_DIM), jnp.bfloat16),
+        scratch_shapes=[
+            pltpu.VMEM((len(entries), HEADS, pages.shape[2]), jnp.float32),
+            pltpu.VMEM((len(entries), HEADS, pages.shape[2]), jnp.bfloat16),
+        ],
+        input_output_aliases={len(pieces) + 2: 0} if before else {},
+        compiler_params=pltpu.CompilerParams(vmem_limit_bytes=6 * MIB),
+        cost_estimate=pl.CostEstimate(flops=2**26, bytes_accessed=2**20, transcendentals=2**14),
+    )(found, *pieces, in_vmem(pages), *before)
+
+
+def combine_kernel(arrived_ref, new_ref, of_second, out_ref):
+    sums = [new_ref[0, row * HEADS : (row + 1) * HEADS, :] for row in range(2)]
+    lower = [jnp.zeros((1, HEADS), jnp.float32)] * 2
+    for sender in range(16):
+        shares = of_second[sender : sender + 1, :]
+        numerator = arrived_ref[sender, :HEADS, :].astype(jnp.float32)
+        last = arrived_ref[sender, HEADS:, :].astype(jnp.float32)[:1]
+        denominator = last[:, :HEADS] + last[:, HEADS:]
+        for row, share in enumerate((1.0 - shares, shares)):
+            sums[row] = sums[row] + numerator * share
+            lower[row] = lower[row] + denominator * share[:, :HEADS]
+    for row in range(2):
+        lines = slice(row * HEADS, (row + 1) * HEADS)
+        padded = jnp.concatenate([lower[row], jnp.zeros((1, HEADS), jnp.float32)], axis=1)
+        column = jnp.swapaxes(jnp.broadcast_to(padded, (8, HEAD_DIM)), 0, 1)[:HEADS, :1]
+        out_ref[lines, :] = (sums[row] / (column + new_ref[1, lines, :])).astype(jnp.bfloat16)
+
+
+def combined(arrived, new_terms, of_second):
+    return pl.pallas_call(
+        combine_kernel,
+        in_specs=[VMEM_SPEC] * 3,
+        out_specs=VMEM_SPEC,
+        out_shape=jax.ShapeDtypeStruct((2 * HEADS, HEAD_DIM), jnp.bfloat16),
+        compiler_params=pltpu.CompilerParams(vmem_limit_bytes=10 * MIB),
+        cost_estimate=pl.CostEstimate(flops=2**22, bytes_accessed=48*2**20, transcendentals=2**11),
+    )(arrived, new_terms, of_second)
+
+
+FETCHES = 8
+
+
+def fetch_kernel(copies_of, me_ref, after_ref, weight_hbm, out_ref, sems):
+    copies = [
+        pltpu.make_async_copy(source, target, sems.at[place])
+        for place, (source, target) in enumerate(copies_of(me_ref[0], weight_hbm, out_ref))
+    ]
+    for copy in copies:
+        copy.start()
+    for copy in copies:
+        copy.wait()
+
+
+def fetched(me, weight, shape, copies_of, after):
+    size = math.prod(shape)
+    return pl.pallas_call(
+        functools.partial(fetch_kernel, copies_of),
+        in_specs=[SMEM_SPEC, pl.BlockSpec(memory_space=pl.ANY), HBM_SPEC],
+        out_specs=VMEM_SPEC,
+        out_shape=pltpu.VMEM(shape, weight.dtype),
+        scratch_shapes=[pltpu.SemaphoreType.DMA((FETCHES,))],
+        compiler_params=pltpu.CompilerParams(vmem_limit_bytes=MIB),
+        cost_estimate=pl.CostEstimate(flops=0, bytes_accessed=2 * size, transcendentals=0),
+    )(me, after, in_hbm(weight))
+
+
+def all_rows(me, weight_hbm, out_ref):
+    rows = out_ref.shape[0] // FETCHES
+    for part in range(FETCHES):
+        here = pl.ds(part * rows, rows)
+        yield weight_hbm.at[here], out_ref.at[here]
+
+
+def device_rows(entries, me, weight_hbm, out_ref):
+    for place, entry in enumerate(entries):
+        here = pl.ds(pl.multiple_of(device_at(me, entry) * CHUNK, CHUNK), CHUNK)
+        yield weight_hbm.at[here], out_ref.at[place]
+
+
+def own_core_columns(me, weight_hbm, out_ref):
+    for index in range(8):
+        here = pl.ds(block_columns(me, index, 0), CHUNK)
+        yield weight_hbm.at[:, here], out_ref.at[index]
+
+
+def out_kernel(
+    me_ref,
+    near_ref,
+    second_ref,
+    odd_ref,
+    weight_ref,
+    residual_hbm,
+    out_ref,
+    wide,
+    left,
+    residual,
+    sem,
+):
+    copy = pltpu.make_async_copy(residual_hbm, residual, sem)
+    copy.start()
+    me = me_ref[0]
+    for entry in range(16):
+        source, place = piece_at(near_ref, second_ref, odd_ref, entry)
+        start = pl.multiple_of(device_at(me, entry) * 2 * HEADS, 2 * HEADS)
+        wide[pl.ds(start, 2 * HEADS), :] = source[place].astype(jnp.float32)
+    for head in range(HEADS):
+        rows = [wide[pl.ds(row * HEADS + head, 16, 2 * HEADS), :] for row in range(2)]
+        left[:, head * HEAD_DIM : (head + 1) * HEAD_DIM] = jnp.concatenate(rows).astype(
+            jnp.bfloat16
+        )
+    depth = 1024
+    total = jnp.zeros(out_ref.shape, jnp.float32)
+    for start in range(0, D, depth):
+        here = slice(start, start + depth)
+        total += jnp.dot(left[:, here], weight_ref[here, :], preferred_element_type=jnp.float32)
+    line = lax.broadcasted_iota(jnp.int32, (32, 32), 0)
+    entry = lax.broadcasted_iota(jnp.int32, (32, 32), 1)
+    turn = ((line % 2) * 16 + line // 2 == entry).astype(jnp.float32)
+    turned = lax.dot_general(
+        turn,
+        total,
+        (((1,), (0,)), ((), ())),
+        precision=lax.Precision.HIGHEST,
+        preferred_element_type=jnp.float32,
+    )
+    copy.wait()
+    out_ref[...] = (residual[...].astype(jnp.float32) + turned).astype(jnp.bfloat16)
+
+
+def projected(me, near, second, odd, residual, held_weight):
+    rows, width = residual.shape
+    return pl.pallas_call(
+        out_kernel,
+        in_specs=[SMEM_SPEC] + [VMEM_SPEC] * 4 + [HBM_SPEC],
+        out_specs=VMEM_SPEC,
+        out_shape=jax.ShapeDtypeStruct((rows, width), jnp.bfloat16),
+        scratch_shapes=[
+            pltpu.VMEM((32 * HEADS, HEAD_DIM), jnp.float32),
+            pltpu.VMEM((rows, D), jnp.bfloat16),
+            pltpu.VMEM((rows, width), jnp.bfloat16),
+            pltpu.SemaphoreType.DMA,
+        ],
+        compiler_params=pltpu.CompilerParams(vmem_limit_bytes=4 * MIB),
+        cost_estimate=pl.CostEstimate(
+            flops=2 * rows * D * width, bytes_accessed=2 * D * width, transcendentals=0
+        ),
+    )(me, near, second, odd, held_weight, in_hbm(residual))
+
+
+def block_columns(me, index, other):
+    return pl.multiple_of((2 * index + (me % 2 ^ other)) * CHUNK, CHUNK)
+
+
+def normed_pieces(entries, pieces, gain_ref, squares):
+    lefts = []
+    for place, entry in enumerate(entries):
+        stream = pieces[place][...] if len(pieces) == len(entries) else pieces[0][place]
+        wide = stream.astype(jnp.float32)
+        squares = squares + wide * wide
+        terms = gain_ref[entry % 4 if entry < 8 else entry - 8, 2 * HEADS :, :]
+        terms = terms.astype(jnp.float32)
+        gain = terms[0:4] + terms[4:8] + terms[8:12]
+        gain = jnp.concatenate([gain[part : part + 1] for part in range(4)], axis=1)
+        lefts.append((wide * gain).astype(jnp.bfloat16))
+    return lefts, squares
+
+
+def rows_of(me, entries):
+    return [
+        pl.ds(pl.multiple_of(device_at(me, entry) * CHUNK, CHUNK), CHUNK) for entry in entries
+    ]
+
+
+def add_terms(total, start, left, weight, place):
+    terms = jnp.dot(left, weight, preferred_element_type=jnp.float32)
+    if place > 0:
+        total[...] += terms
+    else:
+        total[...] = terms if start is None else start[...] + terms
+
+
+def feed_kernel(entries, piece_count, *refs):
+    refs = list(refs)
+    take = lambda number: [refs.pop(0) for _ in range(number)]
+    (me_ref,) = take(1)
+    pieces = take(piece_count)
+    gain_ref, gate_hbm, up_hbm = take(3)
+    gates_in, ups_in, squares_in = [None] * 3 if entries[0] == 0 else take(3)
+    gates, ups, squares_out, gate_held, up_held, gate_sems, up_sems = refs
+    gate_copies, up_copies = [], []
+    for place, here in enumerate(rows_of(me_ref[0], entries)):
+        gate_copies.append(
+            pltpu.make_async_copy(gate_hbm.at[here], gate_held.at[place], gate_sems.at[place])
+        )
+        up_copies.append(
+            pltpu.make_async_copy(up_hbm.at[here], up_held.at[place], up_sems.at[place])
+        )
+        gate_copies[place].start()
+        up_copies[place].start()
+    squares = 0.0 if squares_in is None else squares_in[...]
+    lefts, squares_out[...] = normed_pieces(entries, pieces, gain_ref, squares)
+    for place in range(len(entries)):
+        gate_copies[place].wait()
+        add_terms(gates, gates_in, lefts[place], gate_held[place], place)
+        up_copies[place].wait()
+        add_terms(ups, ups_in, lefts[place], up_held[place], place)
+
+
+def feed(me, entries, pieces, gain, sums, gate_weight, up_weight):
+    rows = pieces[0].shape[-2]
+    width = gate_weight.shape[1]
+    count = len(entries)
+    total = jax.ShapeDtypeStruct((rows, width), jnp.float32)
+    held = pltpu.VMEM((count, CHUNK, width), jnp.bfloat16)
+    return pl.pallas_call(
+        functools.partial(feed_kernel, entries, len(pieces)),
+        in_specs=[SMEM_SPEC]
+        + [VMEM_SPEC] * (len(pieces) + 1)
+        + [HBM_SPEC] * 2
+        + [VMEM_SPEC] * len(sums),
+        out_specs=[VMEM_SPEC] * 3,
+        out_shape=[total, total, jax.ShapeDtypeStruct((rows, CHUNK), jnp.float32)],
+        scratch_shapes=[held, held] + [pltpu.SemaphoreType.DMA((count,))] * 2,
+        compiler_params=pltpu.CompilerParams(
+            vmem_limit_bytes=4 * count * CHUNK * width + 2 * MIB
+        ),
+        cost_estimate=pl.CostEstimate(
+            flops=4 * rows * count * CHUNK * width,
+            bytes_accessed=4 * count * CHUNK * width,
+            transcendentals=0,
+        ),
+    )(me, *pieces, gain, in_hbm(gate_weight), in_hbm(up_weight), *sums)
+
+
+def hidden_kernel(
+    entries,
+    me_ref,
+    odd_ref,
+    gain_ref,
+    early,
+    gate_hbm,
+    up_hbm,
+    down_hbm,
+    gates_in,
+    ups_in,
+    squares_in,
+    hidden_ref,
+    out_ref,
+    gates,
+    ups,
+    gate_held,
+    up_held,
+    down_held,
+    gate_sems,
+    up_sems,
+    down_sems,
+):
+    me = me_ref[0]
+    count, first = len(entries), early.shape[0]
+    rows = rows_of(me, entries)
+    gate_copies = [
+        pltpu.make_async_copy(gate_hbm.at[here], gate_held.at[place], gate_sems.at[place])
+        for place, here in enumerate(rows[first:])
+    ]
+    up_copies = [
+        pltpu.make_async_copy(up_hbm.at[here], up_held.at[place], up_sems.at[place])
+        for place, here in enumerate(rows)
+    ]
+    down_copies = [
+        pltpu.make_async_copy(
+            down_hbm.at[:, pl.ds(block_columns(me, index, 1), CHUNK)],
+            down_held.at[index],
+            down_sems.at[index],
+        )
+        for index in range(8)
+    ]
+    for place in range(count):
+        up_copies[place].start()
+        if place >= first:
+            gate_copies[place - first].start()
+    lefts, squares = normed_pieces(entries, [odd_ref], gain_ref, squares_in[...])
+    for place in range(count):
+        if place < first:
+            weight = early[place]
+        else:
+            gate_copies[place - first].wait()
+            weight = gate_held[place - first]
+        add_terms(gates, gates_in, lefts[place], weight, place)
+        up_copies[place].wait()
+        add_terms(ups, ups_in, lefts[place], up_held[place], place)
+        down_copies[place].start()
+    scale = lax.rsqrt(jnp.sum(squares, axis=1, keepdims=True) / D + norm_eps)
+    hidden_ref[...] = (jax.nn.silu(gates[...] * scale) * (ups[...] * scale)).astype(jnp.bfloat16)
+    for index in range(8):
+        down_copies[index].wait()
+        out_ref[index] = jnp.dot(
+            hidden_ref[...], down_held[index], preferred_element_type=jnp.float32
+        ).astype(jnp.bfloat16)
+
+
+def hidden_units(me, entries, odd, gain, early, gate_weight, up_weight, down_weight, sums):
+    rows = odd.shape[1]
+    width = gate_weight.shape[1]
+    count = len(entries)
+    later = count - early.shape[0]
+    total = pltpu.VMEM((rows, width), jnp.float32)
+    return pl.pallas_call(
+        functools.partial(hidden_kernel, entries),
+        in_specs=[SMEM_SPEC] + [VMEM_SPEC] * 3 + [HBM_SPEC] * 3 + [VMEM_SPEC] * 3,
+        out_specs=[VMEM_SPEC] * 2,
+        out_shape=[
+            jax.ShapeDtypeStruct((rows, width), jnp.bfloat16),
+            jax.ShapeDtypeStruct((8, rows, CHUNK), jnp.bfloat16),
+        ],
+        scratch_shapes=[
+            total,
+            total,
+            pltpu.VMEM((later, CHUNK, width), jnp.bfloat16),
+            pltpu.VMEM((count, CHUNK, width), jnp.bfloat16),
+            pltpu.VMEM((8, width, CHUNK), jnp.bfloat16),
+            pltpu.SemaphoreType.DMA((later,)),
+            pltpu.SemaphoreType.DMA((count,)),
+            pltpu.SemaphoreType.DMA((8,)),
+        ],
+        compiler_params=pltpu.CompilerParams(
+            vmem_limit_bytes=2 * (later + count + 8) * CHUNK * width + 2 * MIB
+        ),
+        cost_estimate=pl.CostEstimate(
+            flops=2 * rows * 3 * count * CHUNK * width,
+            bytes_accessed=2 * 3 * count * CHUNK * width,
+            transcendentals=rows * width,
+        ),
+    )(
+        me,
+        odd,
+        gain,
+        in_vmem(early),
+        in_hbm(gate_weight),
+        in_hbm(up_weight),
+        in_hbm(down_weight),
+        *sums,
+    )
+
+
+def down_kernel(hidden_ref, held_ref, out_ref):
+    for index in range(8):
+        out_ref[index] = jnp.dot(
+            hidden_ref[...], held_ref[index], preferred_element_type=jnp.float32
+        )
+
+
+def own_core_terms(hidden, held):
+    rows, depth = hidden.shape
+    return pl.pallas_call(
+        down_kernel,
+        in_specs=[VMEM_SPEC] * 2,
+        out_specs=VMEM_SPEC,
+        out_shape=jax.ShapeDtypeStruct((8, rows, CHUNK), jnp.float32),
+        compiler_params=pltpu.CompilerParams(vmem_limit_bytes=4 * MIB),
+        cost_estimate=pl.CostEstimate(
+            flops=rows * depth * D, bytes_accessed=depth * D, transcendentals=0
+        ),
+    )(hidden, in_vmem(held))
+
+
+def pair_kernel(mine_ref, theirs_ref, out_ref):
+    for index in range(8):
+        out_ref[index] = (mine_ref[index] + theirs_ref[index].astype(jnp.float32)).astype(
+            jnp.bfloat16
+        )
+
+
+def paired(mine, theirs):
+    return pl.pallas_call(
+        pair_kernel,
+        in_specs=[VMEM_SPEC] * 2,
+        out_specs=VMEM_SPEC,
+        out_shape=jax.ShapeDtypeStruct(theirs.shape, jnp.bfloat16),
+        compiler_params=pltpu.CompilerParams(vmem_limit_bytes=4 * MIB),
+    )(mine, theirs)
+
+
+def finish_kernel(stream_ref, shares_ref, out_ref):
+    total = stream_ref[...].astype(jnp.float32)
+    for index in range(8):
+        total = total + shares_ref[index].astype(jnp.float32)
+    out_ref[...] = total.astype(jnp.bfloat16)
+
+
+def finished(stream, shares):
+    return pl.pallas_call(
+        finish_kernel,
+        in_specs=[VMEM_SPEC] * 2,
+        out_specs=VMEM_SPEC,
+        out_shape=jax.ShapeDtypeStruct(stream.shape, jnp.bfloat16),
+        compiler_params=pltpu.CompilerParams(vmem_limit_bytes=4 * MIB),
+    )(stream, shares)
+
+
+def block_body(
+    queries,
+    new_kv,
+    kv_pages,
+    page_table,
+    lengths,
+    residual,
+    out_weight,
+    norm_gain,
+    gate_weight,
+    up_weight,
+    down_weight,
+):
+    me = lax.axis_index("shard").astype(jnp.int32)[None]
+    table = jnp.concatenate([page_table.reshape(-1), lengths, me])
+    own, query_rows = packed(queries, norm_gain)
+    late = tuple(range(8, 16))
+    early_shape = (5, CHUNK, gate_weight.shape[1])
+    early = fetched(
+        me, gate_weight, early_shape, functools.partial(device_rows, late[:5]), table
+    )
+    near = stacked(near_pieces(own), (early,))
+    second = sent(near, 2)
+    pages, found, new_terms, of_second = readied(table, query_rows, kv_pages, new_kv)
+    odd = sent(stacked([near, second], (new_terms,)), 1)
+    gains = near, second, odd
+    terms = page_terms(found, tuple(range(8)), (near, second), pages)
+    terms = page_terms(found, late, (odd,), pages, (terms,))
+    arrived = lax.all_to_all(terms, "shard", 0, 0)
+    attended = combined(arrived, new_terms, of_second)
+    near = stacked(near_pieces(attended), ())
+    second = sent(near, 2)
+    down_shape = (8, down_weight.shape[0], CHUNK)
+    down_held = fetched(me, down_weight, down_shape, own_core_columns, near)
+    odd = sent(stacked([near, second], (down_held,)), 1)
+    stream = projected(me, near, second, odd, residual, out_weight)
+    weights = gate_weight, up_weight
+    near = near_pieces(stream)
+    sums = feed(me, (0,), near[:1], gains[0], (), *weights)
+    first = stacked(near, sums[:1])
+    second = sent(first, 2)
+    sums = feed(me, (1, 2, 3), near[1:], gains[0], sums, *weights)
+    odd = sent(stacked([first, second], sums[:1]), 1)
+    sums = feed(me, (4, 5, 6, 7), [second], gains[1], sums, *weights)
+    hidden, theirs = hidden_units(me, late, odd, gains[2], early, *weights, down_weight, sums)
+    theirs = sent(theirs, 1)
+    pairs = paired(own_core_terms(hidden, down_held), theirs)
+    same_core = [[core + 2 * step for step in range(8)] for core in range(2)]
+    shares = lax.all_to_all(pairs, "shard", 0, 0, axis_index_groups=same_core)
+    return finished(stream, shares)
+
+
 def solution(mesh):
     placed = (
         P(("groups", "shard"), None),
@@ -154,6 +855,7 @@
         P(None, "shard"),
         P("shard", None),
     )
+    chosen = block_body if mesh.shape["shard"] == 16 else body
     return jax.shard_map(
-        body, mesh=mesh, in_specs=placed, out_specs=P("groups", "shard"), check_vma=False
-    )
+        chosen, mesh=mesh, in_specs=placed, out_specs=P("groups", "shard"), check_vma=False
+    )

time: 243 us -> 99.6 us (0.41)
  waiting for transfers between devices: 99.5 us -> 4.21 us
  Pallas kernels: 0 us -> 45.1 us
  blocking collectives: 71.4 us -> 28.2 us
  matrix products: 38.9 us -> 0 us
  between operations: 13.6 us -> 0.26 us
  starting transfers between devices: 7.89 us -> 19.8 us
  other arithmetic: 5.62 us -> 0.73 us
  local copies, waits for them, and re-layouts: 5.58 us -> 0.86 us
    reduce_scatter x1 -> x0, waiting for transfers between devices: 55.9 us -> none  [body(): lax.psum_scatter(partial_terms, 'shard', scatter_dimension=1, tiled=True)]
    pallas_call x0 -> x21, Pallas kernels: none -> 45.1 us  [the longest x3 12.2 us: feed(): pl.pallas_call(functools.partial(feed_kernel, entries, len(pieces)), in_s...]
    all_gather x2 -> x0, blocking collectives: 41.5 us -> none  [the longest x1 22.7 us: body(): lax.all_gather(attended, 'shard', axis=0, tiled=True)]
    ppermute x4 -> x16, waiting for transfers between devices: 43.6 us -> 4.21 us  [sent(): lax.ppermute(array, 'shard', [(i, i ^ distance) for i in range(size)])]
    dot_general x6 -> x0, matrix products: 38.9 us -> none  [the longest x1 21.4 us: body(): jnp.dot(hidden, down_weight, preferred_element_type=jnp.float32)]
    psum x1 -> x0, blocking collectives: 29.8 us -> none  [body(): square_sums = lax.psum(jnp.sum(wide * wide, axis=1), 'shard')]
    all_to_all x0 -> x2, blocking collectives: none -> 28.2 us  [the longest x1 16 us: block_body(): arrived = lax.all_to_all(terms, 'shard', 0, 0)]
    ppermute x4 -> x16, starting transfers between devices: 7.89 us -> 19.8 us  [sent(): lax.ppermute(array, 'shard', [(i, i ^ distance) for i in range(size)])]
  transfers between devices with their start and end apart: 5 -> 16, of which waited for: 5 -> 5; matrix products, arithmetic and copies ran while one was open for 2% -> 2% of each run, Pallas kernels for 0% -> 29%
where the time goes in v2:
time: 99.6 us; the launch traced here: 99.2 us
  Pallas kernels  45.1 us (45%)
  blocking collectives  28.2 us (28%)
  starting transfers between devices  19.8 us (20%)
  waiting for transfers between devices  4.21 us (4%)
    ppermute x16, starting transfers between devices, sent(): lax.ppermute(array, 'shard', [(i, i ^ distance) for i in range(size)])  19.8 us
    all_to_all x1, blocking collectives, block_body(): arrived = lax.all_to_all(terms, 'shard', 0, 0)  16 us
    pallas_call x3, Pallas kernels, feed(): pl.pallas_call(functools.partial(feed_kernel, entries, len(pieces)), in_s...  12.2 us
    all_to_all x1, blocking collectives, block_body(): shares = lax.all_to_all(pairs, 'shard', 0, 0, axis_index_groups=same_core)  12.2 us
    pallas_call x1, Pallas kernels, hidden_units(): pl.pallas_call(functools.partial(hidden_kernel, entries), in_specs=[SMEM_...  11.2 us
    pallas_call x2, Pallas kernels, fetched(): pl.pallas_call(functools.partial(fetch_kernel, copies_of), in_specs=[SMEM...  9.05 us
    ppermute x16, waiting for transfers between devices, sent(): lax.ppermute(array, 'shard', [(i, i ^ distance) for i in range(size)])  4.21 us
    pallas_call x1, Pallas kernels, readied(): pl.pallas_call(ready_kernel, in_specs=[SMEM_SPEC, VMEM_SPEC] + [HBM_SPEC]...  3.87 us
  transfers between devices with their start and end apart: 16, of which 5 were waited for; matrix products, arithmetic and copies ran while one was open for 2% of the time, Pallas kernels for 29%

profile of v2, /device:TPU:0, one launch (start us, length us, event | category | flops | bytes accessed | tf_op | source)
XLA Modules:
  0.0 99.2 jit_solution(12461944660138534032)
XLA Ops:
  0.0 0.8 shard_map.109
  0.8 5.1 %collective-permute-start.2 = (bf16[144,128]{1,0:T(8,128)(2,1)S(1)}, bf16[144,128]{1,0:T(8,128)(2,1)S(1)}, u32[]{:S(2)}, u32[]{:S(2)}) collective-permute-start(bf16[144,128]{1,0:T(8,128)(2,1)S(1)} %get-tuple-element.24.refs_0_), channel_id=1, source_target_pairs={{0,12},{1,13},{2,14},{3,15},{4,8},{5,9},{6,10},{7,11},{8,4},{9,5},... | collective-permute-start | bytes 110600 | tf_op jit(solution)/shard_map/ppermute | solution.py:157
  8.2 3.5 %shard_map.111.refs_4_.early = bf16[5,512,1664]{2,1,0:T(8,128)(2,1)S(1)} custom-call(s32[1]{0:T(128)} %bitcast.me_ref.refs_0_, s32[289]{0:T(512)S(1)} %pad_add_fusion.table_ref.after_ref, bf16[8192,1664]{1,0:T(8,128)(2,1)} %gate_hbm.1), custom_call_target="tpu_custom_call" | custom-call | bytes 8519680 | tf_op jit(solution)/shard_map/pallas_call | solution.py:448
  11.8 1.7 %collective-permute-start.3 = (bf16[4,144,128]{2,1,0:T(8,128)(2,1)S(1)}, bf16[4,144,128]{2,1,0:T(8,128)(2,1)S(1)}, u32[]{:S(2)}, u32[]{:S(2)}) collective-permute-start(bf16[4,144,128]{2,1,0:T(8,128)(2,1)S(1)} %shard_map.112.refs_0_.refs_2_.refs_4_), channel_id=1, source_target_pairs={{0,2},{1,3},{2,0},{3,1},{4,6},{5,7},{6,4},{7,5},{8,10},{9,11},{10,... | collective-permute-start | bytes 442376 | tf_op jit(solution)/shard_map/ppermute | solution.py:157
  13.5 3.9 %shard_map.110 = (bf16[16,2,32,512]{3,2,1,0:T(8,128)(2,1)S(1)}, s32[49]{0:T(128)S(1)}, f32[2,128,128]{2,1,0:T(8,128)S(1)}, f32[16,128]{1,0:T(8,128)S(1)}) custom-call(s32[289]{0:T(512)S(1)} %pad_add_fusion.table_ref.after_ref, bf16[128,128]{1,0:T(8,128)(2,1)S(1)} %get-tuple-element.22.query_ref, bf16[16,2,32,512]{3,2,1,0:T(8,128)(2,1)} %pages_hbm.1, ...), custom_call_target="tpu_custom_call" | custom-call | flops 4194304 | bytes 2097152 | tf_op jit(solution)/shard_map/pallas_call | solution.py:313
  17.5 1.1 %shard_map.114.refs_2_ = bf16[16,72,128]{2,1,0:T(8,128)(2,1)S(1)} custom-call(s32[49]{0:T(128)S(1)} %get-tuple-element.23.found_ref, bf16[4,144,128]{2,1,0:T(8,128)(2,1)S(1)} %shard_map.112.refs_0_.refs_2_.refs_4_, bf16[4,144,128]{2,1,0:T(8,128)(2,1)S(1)} %collective-permute-done.3.refs_1_.refs_2_, bf16[16,2,32,512]{3,2,1,0:T(8,128)(2,1)S(1)} %get-tuple-element.26.refs_2_.refs_1_), custom_call_target="tpu_custom_call" | custom-call | flops 67108864 | bytes 1048576 | tf_op jit(solution)/shard_map/pallas_call | solution.py:388
  19.1 1.1 %shard_map.115 = bf16[16,72,128]{2,1,0:T(8,128)(2,1)S(1)} custom-call(s32[49]{0:T(128)S(1)} %get-tuple-element.23.found_ref, bf16[8,144,128]{2,1,0:T(8,128)(2,1)S(1)} %collective-permute-done.4.refs_0_.gain_ref, bf16[16,2,32,512]{3,2,1,0:T(8,128)(2,1)S(1)} %get-tuple-element.26.refs_2_.refs_1_, ...), custom_call_target="tpu_custom_call", output_to_operand_aliasing={{}: (3, {})} | custom-call | flops 67108864 | bytes 1048576 | tf_op jit(solution)/shard_map/pallas_call | solution.py:388
  20.2 16.0 %all_to_all.10.arrived_ref = bf16[16,72,128]{2,1,0:T(8,128)(2,1)S(1)} all-to-all(bf16[16,72,128]{2,1,0:T(8,128)(2,1)S(1)} %shard_map.115), channel_id=1, replica_groups=mesh['groups'=2,'shard'=16] {'shard'}, dimensions={0} | all-to-all | bytes 589824 | tf_op jit(solution)/shard_map/all_to_all | solution.py:820
  36.5 1.1 %collective-permute-start.7 = (bf16[128,128]{1,0:T(8,128)(2,1)S(1)}, bf16[128,128]{1,0:T(8,128)(2,1)S(1)}, u32[]{:S(2)}, u32[]{:S(2)}) collective-permute-start(bf16[128,128]{1,0:T(8,128)(2,1)S(1)} %shard_map.116.refs_0_), channel_id=1, source_target_pairs={{0,12},{1,13},{2,14},{3,15},{4,8},{5,9},{6,10},{7,11},{8,4},{9,5},... | collective-permute-start | bytes 98312 | tf_op jit(solution)/shard_map/ppermute | solution.py:157
  38.2 2.8 %collective-permute-start.5 = (bf16[128,128]{1,0:T(8,128)(2,1)S(1)}, bf16[128,128]{1,0:T(8,128)(2,1)S(1)}, u32[]{:S(2)}, u32[]{:S(2)}) collective-permute-start(bf16[128,128]{1,0:T(8,128)(2,1)S(1)} %shard_map.116.refs_0_), channel_id=1, source_target_pairs={{0,4},{1,5},{2,6},{3,7},{4,0},{5,1},{6,2},{7,3},{8,12},{9,13},{10,... | collective-permute-start | bytes 98312 | tf_op jit(solution)/shard_map/ppermute | solution.py:157
  40.9 1.3 %collective-permute-done.7.refs_3_ = bf16[128,128]{1,0:T(8,128)(2,1)S(1)} collective-permute-done((bf16[128,128]{1,0:T(8,128)(2,1)S(1)}, bf16[128,128]{1,0:T(8,128)(2,1)S(1)}, u32[]{:S(2)}, u32[]{:S(2)}) %collective-permute-start.7) | collective-permute-done | bytes 32800 | tf_op jit(solution)/shard_map/ppermute | solution.py:157
  44.0 5.5 %shard_map.118.refs_2_.held_ref = bf16[8,1664,512]{2,1,0:T(8,128)(2,1)S(1)} custom-call(s32[1]{0:T(128)} %bitcast.me_ref.refs_0_, bf16[4,128,128]{2,1,0:T(8,128)(2,1)S(1)} %shard_map.117.after_ref.refs_0_.near_ref, bf16[1664,8192]{1,0:T(8,128)(2,1)} %down_hbm.1), custom_call_target="tpu_custom_call" | custom-call | bytes 13631488 | tf_op jit(solution)/shard_map/pallas_call | solution.py:448
  49.6 1.5 %collective-permute-done.9.odd_ref = bf16[8,128,128]{2,1,0:T(8,128)(2,1)S(1)} collective-permute-done((bf16[8,128,128]{2,1,0:T(8,128)(2,1)S(1)}, bf16[8,128,128]{2,1,0:T(8,128)(2,1)S(1)}, u32[]{:S(2)}, u32[]{:S(2)}) %collective-permute-start.9) | collective-permute-done | bytes 262176 | tf_op jit(solution)/shard_map/ppermute | solution.py:157
  51.1 2.2 %shard_map.120.refs_1_.refs_0_.stream_ref = bf16[32,512]{1,0:T(8,128)(2,1)S(1)} custom-call(s32[1]{0:T(128)} %bitcast.me_ref.refs_0_, bf16[4,128,128]{2,1,0:T(8,128)(2,1)S(1)} %shard_map.117.after_ref.refs_0_.near_ref, bf16[4,128,128]{2,1,0:T(8,128)(2,1)S(1)} %collective-permute-done.8.refs_1_.second_ref, ...), custom_call_target="tpu_custom_call" | custom-call | flops 268435456 | bytes 8388608 | tf_op jit(solution)/shard_map/pallas_call | solution.py:524
  53.4 1.7 %collective-permute-start.12 = (bf16[32,512]{1,0:T(8,128)(2,1)S(1)}, bf16[32,512]{1,0:T(8,128)(2,1)S(1)}, u32[]{:S(2)}, u32[]{:S(2)}) collective-permute-start(bf16[32,512]{1,0:T(8,128)(2,1)S(1)} %shard_map.120.refs_1_.refs_0_.stream_ref), channel_id=1, source_target_pairs={{0,12},{1,13},{2,14},{3,15},{4,8},{5,9},{6,10},{7,11},{8,4},{9,5},... | collective-permute-start | bytes 98312 | tf_op jit(solution)/shard_map/ppermute | solution.py:157
  55.1 1.1 %collective-permute-start.11 = (bf16[32,512]{1,0:T(8,128)(2,1)S(1)}, bf16[32,512]{1,0:T(8,128)(2,1)S(1)}, u32[]{:S(2)}, u32[]{:S(2)}) collective-permute-start(bf16[32,512]{1,0:T(8,128)(2,1)S(1)} %shard_map.120.refs_1_.refs_0_.stream_ref), channel_id=1, source_target_pairs={{0,8},{1,9},{2,10},{3,11},{4,12},{5,13},{6,14},{7,15},{8,0},{9,1},... | collective-permute-start | bytes 98312 | tf_op jit(solution)/shard_map/ppermute | solution.py:157
  56.2 1.7 %collective-permute-start.10 = (bf16[32,512]{1,0:T(8,128)(2,1)S(1)}, bf16[32,512]{1,0:T(8,128)(2,1)S(1)}, u32[]{:S(2)}, u32[]{:S(2)}) collective-permute-start(bf16[32,512]{1,0:T(8,128)(2,1)S(1)} %shard_map.120.refs_1_.refs_0_.stream_ref), channel_id=1, source_target_pairs={{0,4},{1,5},{2,6},{3,7},{4,0},{5,1},{6,2},{7,3},{8,12},{9,13},{10,... | collective-permute-start | bytes 98312 | tf_op jit(solution)/shard_map/ppermute | solution.py:157
  57.9 2.4 %shard_map.121 = (f32[32,1664]{1,0:T(8,128)S(1)}, f32[32,1664]{1,0:T(8,128)S(1)}, f32[32,512]{1,0:T(8,128)S(1)}) custom-call(s32[1]{0:T(128)} %bitcast.me_ref.refs_0_, bf16[32,512]{1,0:T(8,128)(2,1)S(1)} %shard_map.120.refs_1_.refs_0_.stream_ref, bf16[4,144,128]{2,1,0:T(8,128)(2,1)S(1)} %shard_map.112.refs_0_.refs_2_.refs_4_, bf16[8192,1664]{1,0:T(8,128)(2,1)} %gate_hbm.1, ...), custom_call_target="tpu_custom_call" | custom-call | flops 109051904 | bytes 3407872 | tf_op jit(solution)/shard_map/pallas_call | solution.py:607
  60.3 1.8 %collective-permute-start.13 = (bf16[4,32,512]{2,1,0:T(8,128)(2,1)S(1)}, bf16[4,32,512]{2,1,0:T(8,128)(2,1)S(1)}, u32[]{:S(2)}, u32[]{:S(2)}) collective-permute-start(bf16[4,32,512]{2,1,0:T(8,128)(2,1)S(1)} %shard_map.122.refs_0_), channel_id=1, source_target_pairs={{0,2},{1,3},{2,0},{3,1},{4,6},{5,7},{6,4},{7,5},{8,10},{9,11},{10,... | collective-permute-start | bytes 393224 | tf_op jit(solution)/shard_map/ppermute | solution.py:157
  62.1 4.4 %shard_map.123 = (f32[32,1664]{1,0:T(8,128)S(1)}, f32[32,1664]{1,0:T(8,128)S(1)}, f32[32,512]{1,0:T(8,128)S(1)}) custom-call(s32[1]{0:T(128)} %bitcast.me_ref.refs_0_, bf16[32,512]{1,0:T(8,128)(2,1)S(1)} %collective-permute-done.10.refs_1_, bf16[32,512]{1,0:T(8,128)(2,1)S(1)} %collective-permute-done.11.refs_2_, ...), custom_call_target="tpu_custom_call" | custom-call | flops 327155712 | bytes 10223616 | tf_op jit(solution)/shard_map/pallas_call | solution.py:607
  66.7 5.4 %shard_map.125 = (f32[32,1664]{1,0:T(8,128)S(1)}, f32[32,1664]{1,0:T(8,128)S(1)}, f32[32,512]{1,0:T(8,128)S(1)}) custom-call(s32[1]{0:T(128)} %bitcast.me_ref.refs_0_, bf16[4,32,512]{2,1,0:T(8,128)(2,1)S(1)} %collective-permute-done.13.refs_1_, bf16[4,144,128]{2,1,0:T(8,128)(2,1)S(1)} %collective-permute-done.3.refs_1_.refs_2_, bf16[8192,1664]{1,0:T(8,128)(2,1)} %gate_hbm.1, ...), custom_call_target="tpu_custom_call" | custom-call | flops 436207616 | bytes 13631488 | tf_op jit(solution)/shard_map/pallas_call | solution.py:607
  72.1 11.2 %shard_map.126 = (bf16[32,1664]{1,0:T(8,128)(2,1)S(1)}, bf16[8,32,512]{2,1,0:T(8,128)(2,1)S(1)}) custom-call(s32[1]{0:T(128)} %bitcast.me_ref.refs_0_, bf16[8,32,512]{2,1,0:T(8,128)(2,1)S(1)} %collective-permute-done.14.odd_ref, bf16[8,144,128]{2,1,0:T(8,128)(2,1)S(1)} %collective-permute-done.4.refs_0_.gain_ref, ...), custom_call_target="tpu_custom_call" | custom-call | flops 1308622848 | bytes 40894464 | tf_op jit(solution)/shard_map/pallas_call | solution.py:699
  83.9 2.4 %shard_map.127.mine_ref = f32[8,32,512]{2,1,0:T(8,128)S(1)} custom-call(bf16[32,1664]{1,0:T(8,128)(2,1)S(1)} %get-tuple-element.37.hidden_ref, bf16[8,1664,512]{2,1,0:T(8,128)(2,1)S(1)} %shard_map.118.refs_2_.held_ref), custom_call_target="tpu_custom_call" | custom-call | flops 436207616 | bytes 13631488 | tf_op jit(solution)/shard_map/pallas_call | solution.py:746
  86.4 12.2 %all_to_all.11.shares_ref = bf16[8,32,512]{2,1,0:T(8,128)(2,1)S(1)} all-to-all(bf16[8,32,512]{2,1,0:T(8,128)(2,1)S(1)} %shard_map.128), channel_id=1, replica_groups={{0,2,4,6,8,10,12,14},{1,3,5,7,9,11,13,15},{16,18,20,22,24,26,28,30},{17..., dimensions={0} | all-to-all | bytes 524288 | tf_op jit(solution)/shard_map/all_to_all | solution.py:840
  (39 shorter events, 6.9 us)
Async XLA Ops:
  0.8 10.9 %collective-permute-start.2 = (bf16[144,128]{1,0:T(8,128)(2,1)S(1)}, bf16[144,128]{1,0:T(8,128)(2,1)S(1)}, u32[]{:S(2)}, u32[]{:S(2)}) collective-permute-start(bf16[144,128]{1,0:T(8,128)(2,1)S(1)} %get-tuple-element.24.refs_0_), channel_id=1, source_target_pairs={{0,12},{1,13},{2,14},{3,15},{4,8},{5,9},{6,10},{7,11},{8,4},{9,5},... | collective-permute-start | bytes 110600 | tf_op jit(solution)/shard_map/ppermute | solution.py:157
  6.0 5.8 %collective-permute-start.1 = (bf16[144,128]{1,0:T(8,128)(2,1)S(1)}, bf16[144,128]{1,0:T(8,128)(2,1)S(1)}, u32[]{:S(2)}, u32[]{:S(2)}) collective-permute-start(bf16[144,128]{1,0:T(8,128)(2,1)S(1)} %get-tuple-element.24.refs_0_), channel_id=1, source_target_pairs={{0,8},{1,9},{2,10},{3,11},{4,12},{5,13},{6,14},{7,15},{8,0},{9,1},... | collective-permute-start | bytes 110600 | tf_op jit(solution)/shard_map/ppermute | solution.py:157
  6.0 5.8 %collective-permute-start = (bf16[144,128]{1,0:T(8,128)(2,1)S(1)}, bf16[144,128]{1,0:T(8,128)(2,1)S(1)}, u32[]{:S(2)}, u32[]{:S(2)}) collective-permute-start(bf16[144,128]{1,0:T(8,128)(2,1)S(1)} %get-tuple-element.24.refs_0_), channel_id=1, source_target_pairs={{0,4},{1,5},{2,6},{3,7},{4,0},{5,1},{6,2},{7,3},{8,12},{9,13},{10,... | collective-permute-start | bytes 110600 | tf_op jit(solution)/shard_map/ppermute | solution.py:157
  11.8 5.6 %collective-permute-start.3 = (bf16[4,144,128]{2,1,0:T(8,128)(2,1)S(1)}, bf16[4,144,128]{2,1,0:T(8,128)(2,1)S(1)}, u32[]{:S(2)}, u32[]{:S(2)}) collective-permute-start(bf16[4,144,128]{2,1,0:T(8,128)(2,1)S(1)} %shard_map.112.refs_0_.refs_2_.refs_4_), channel_id=1, source_target_pairs={{0,2},{1,3},{2,0},{3,1},{4,6},{5,7},{6,4},{7,5},{8,10},{9,11},{10,... | collective-permute-start | bytes 442376 | tf_op jit(solution)/shard_map/ppermute | solution.py:157
  17.4 1.6 %collective-permute-start.4 = (bf16[8,144,128]{2,1,0:T(8,128)(2,1)S(1)}, bf16[8,144,128]{2,1,0:T(8,128)(2,1)S(1)}, u32[]{:S(2)}, u32[]{:S(2)}) collective-permute-start(bf16[8,144,128]{2,1,0:T(8,128)(2,1)S(1)} %shard_map.113), channel_id=1, source_target_pairs={{0,1},{1,0},{2,3},{3,2},{4,5},{5,4},{6,7},{7,6},{8,9},{9,8},{10,11... | collective-permute-start | bytes 884744 | tf_op jit(solution)/shard_map/ppermute | solution.py:157
  36.5 5.8 %collective-permute-start.7 = (bf16[128,128]{1,0:T(8,128)(2,1)S(1)}, bf16[128,128]{1,0:T(8,128)(2,1)S(1)}, u32[]{:S(2)}, u32[]{:S(2)}) collective-permute-start(bf16[128,128]{1,0:T(8,128)(2,1)S(1)} %shard_map.116.refs_0_), channel_id=1, source_target_pairs={{0,12},{1,13},{2,14},{3,15},{4,8},{5,9},{6,10},{7,11},{8,4},{9,5},... | collective-permute-start | bytes 98312 | tf_op jit(solution)/shard_map/ppermute | solution.py:157
  37.6 5.4 %collective-permute-start.6 = (bf16[128,128]{1,0:T(8,128)(2,1)S(1)}, bf16[128,128]{1,0:T(8,128)(2,1)S(1)}, u32[]{:S(2)}, u32[]{:S(2)}) collective-permute-start(bf16[128,128]{1,0:T(8,128)(2,1)S(1)} %shard_map.116.refs_0_), channel_id=1, source_target_pairs={{0,8},{1,9},{2,10},{3,11},{4,12},{5,13},{6,14},{7,15},{8,0},{9,1},... | collective-permute-start | bytes 98312 | tf_op jit(solution)/shard_map/ppermute | solution.py:157
  38.2 4.9 %collective-permute-start.5 = (bf16[128,128]{1,0:T(8,128)(2,1)S(1)}, bf16[128,128]{1,0:T(8,128)(2,1)S(1)}, u32[]{:S(2)}, u32[]{:S(2)}) collective-permute-start(bf16[128,128]{1,0:T(8,128)(2,1)S(1)} %shard_map.116.refs_0_), channel_id=1, source_target_pairs={{0,4},{1,5},{2,6},{3,7},{4,0},{5,1},{6,2},{7,3},{8,12},{9,13},{10,... | collective-permute-start | bytes 98312 | tf_op jit(solution)/shard_map/ppermute | solution.py:157
  43.1 8.0 %slice-start = ((s8[8388608]{0:T(1024)(128)(4,1)}), s8[4194304]{0:T(1024)(128)(4,1)S(1)}, s32[]{:S(2)}) async-start(s8[8388608]{0:T(1024)(128)(4,1)} %bitcast.2), calls=%async_computation.2 | async-start | bytes 8388608
  43.1 8.0 %slice-start.1 = ((s8[8388608]{0:T(1024)(128)(4,1)}), s8[4194304]{0:T(1024)(128)(4,1)S(1)}, s32[]{:S(2)}) async-start(s8[8388608]{0:T(1024)(128)(4,1)} %bitcast.2), calls=%async_computation.3 | async-start | bytes 8388608
  43.1 6.3 %collective-permute-start.8 = (bf16[4,128,128]{2,1,0:T(8,128)(2,1)S(1)}, bf16[4,128,128]{2,1,0:T(8,128)(2,1)S(1)}, u32[]{:S(2)}, u32[]{:S(2)}) collective-permute-start(bf16[4,128,128]{2,1,0:T(8,128)(2,1)S(1)} %shard_map.117.after_ref.refs_0_.near_ref), channel_id=1, source_target_pairs={{0,2},{1,3},{2,0},{3,1},{4,6},{5,7},{6,4},{7,5},{8,10},{9,11},{10,... | collective-permute-start | bytes 393224 | tf_op jit(solution)/shard_map/ppermute | solution.py:157
  49.5 1.6 %collective-permute-start.9 = (bf16[8,128,128]{2,1,0:T(8,128)(2,1)S(1)}, bf16[8,128,128]{2,1,0:T(8,128)(2,1)S(1)}, u32[]{:S(2)}, u32[]{:S(2)}) collective-permute-start(bf16[8,128,128]{2,1,0:T(8,128)(2,1)S(1)} %shard_map.119), channel_id=1, source_target_pairs={{0,1},{1,0},{2,3},{3,2},{4,5},{5,4},{6,7},{7,6},{8,9},{9,8},{10,11... | collective-permute-start | bytes 786440 | tf_op jit(solution)/shard_map/ppermute | solution.py:157
  53.4 6.9 %collective-permute-start.12 = (bf16[32,512]{1,0:T(8,128)(2,1)S(1)}, bf16[32,512]{1,0:T(8,128)(2,1)S(1)}, u32[]{:S(2)}, u32[]{:S(2)}) collective-permute-start(bf16[32,512]{1,0:T(8,128)(2,1)S(1)} %shard_map.120.refs_1_.refs_0_.stream_ref), channel_id=1, source_target_pairs={{0,12},{1,13},{2,14},{3,15},{4,8},{5,9},{6,10},{7,11},{8,4},{9,5},... | collective-permute-start | bytes 98312 | tf_op jit(solution)/shard_map/ppermute | solution.py:157
  55.1 5.2 %collective-permute-start.11 = (bf16[32,512]{1,0:T(8,128)(2,1)S(1)}, bf16[32,512]{1,0:T(8,128)(2,1)S(1)}, u32[]{:S(2)}, u32[]{:S(2)}) collective-permute-start(bf16[32,512]{1,0:T(8,128)(2,1)S(1)} %shard_map.120.refs_1_.refs_0_.stream_ref), channel_id=1, source_target_pairs={{0,8},{1,9},{2,10},{3,11},{4,12},{5,13},{6,14},{7,15},{8,0},{9,1},... | collective-permute-start | bytes 98312 | tf_op jit(solution)/shard_map/ppermute | solution.py:157
  56.2 4.1 %collective-permute-start.10 = (bf16[32,512]{1,0:T(8,128)(2,1)S(1)}, bf16[32,512]{1,0:T(8,128)(2,1)S(1)}, u32[]{:S(2)}, u32[]{:S(2)}) collective-permute-start(bf16[32,512]{1,0:T(8,128)(2,1)S(1)} %shard_map.120.refs_1_.refs_0_.stream_ref), channel_id=1, source_target_pairs={{0,4},{1,5},{2,6},{3,7},{4,0},{5,1},{6,2},{7,3},{8,12},{9,13},{10,... | collective-permute-start | bytes 98312 | tf_op jit(solution)/shard_map/ppermute | solution.py:157
  60.3 6.3 %collective-permute-start.13 = (bf16[4,32,512]{2,1,0:T(8,128)(2,1)S(1)}, bf16[4,32,512]{2,1,0:T(8,128)(2,1)S(1)}, u32[]{:S(2)}, u32[]{:S(2)}) collective-permute-start(bf16[4,32,512]{2,1,0:T(8,128)(2,1)S(1)} %shard_map.122.refs_0_), channel_id=1, source_target_pairs={{0,2},{1,3},{2,0},{3,1},{4,6},{5,7},{6,4},{7,5},{8,10},{9,11},{10,... | collective-permute-start | bytes 393224 | tf_op jit(solution)/shard_map/ppermute | solution.py:157
  66.6 5.5 %collective-permute-start.14 = (bf16[8,32,512]{2,1,0:T(8,128)(2,1)S(1)}, bf16[8,32,512]{2,1,0:T(8,128)(2,1)S(1)}, u32[]{:S(2)}, u32[]{:S(2)}) collective-permute-start(bf16[8,32,512]{2,1,0:T(8,128)(2,1)S(1)} %shard_map.124), channel_id=1, source_target_pairs={{0,1},{1,0},{2,3},{3,2},{4,5},{5,4},{6,7},{7,6},{8,9},{9,8},{10,11... | collective-permute-start | bytes 786440 | tf_op jit(solution)/shard_map/ppermute | solution.py:157
  83.3 3.0 %collective-permute-start.15 = (bf16[8,32,512]{2,1,0:T(8,128)(2,1)S(1)}, bf16[8,32,512]{2,1,0:T(8,128)(2,1)S(1)}, u32[]{:S(2)}, u32[]{:S(2)}) collective-permute-start(bf16[8,32,512]{2,1,0:T(8,128)(2,1)S(1)} %get-tuple-element.38), channel_id=1, source_target_pairs={{0,1},{1,0},{2,3},{3,2},{4,5},{5,4},{6,7},{7,6},{8,9},{9,8},{10,11... | collective-permute-start | bytes 786440 | tf_op jit(solution)/shard_map/ppermute | solution.py:157

commit v3 on v2

v3 whole, which is shorter than its diff:
```python
import functools
import math

import jax
import jax.numpy as jnp
from jax import lax
from jax.experimental import pallas as pl
from jax.experimental.pallas import tpu as pltpu
from jax.sharding import PartitionSpec as P

D = 8192
HEADS = 64
KV_HEADS = 4
HEAD_DIM = 128


norm_eps = 1e-05


def swapped(array, axis, distance):
    return lax.ppermute(array, axis, [(i, i ^ 1 << distance) for i in range(lax.axis_size(axis))])


def new_token_terms(queries, new_kv, score_scale):
    seq_dev = queries.shape[0]
    group_size = HEADS // KV_HEADS
    query_heads = queries.reshape(seq_dev, KV_HEADS, group_size, HEAD_DIM)
    new_keys = new_kv[:, 0].reshape(seq_dev, KV_HEADS, HEAD_DIM)
    new_values = new_kv[:, 1].reshape(seq_dev, KV_HEADS, HEAD_DIM)
    scores = (
        jnp.einsum("bgqd,bgd->bgq", query_heads, new_keys, preferred_element_type=jnp.float32)
        * score_scale
    )
    weights = jnp.exp(scores)
    numerator = jnp.einsum(
        "bgq,bgd->bgqd",
        weights.astype(jnp.bfloat16),
        new_values,
        preferred_element_type=jnp.float32,
    )
    return (numerator.reshape(seq_dev, D), weights.reshape(seq_dev, HEADS))


def butterfly(items, position, mover):
    count = items[0].shape[0]
    for level in range(count.bit_length() - 1):
        upper_half = position // (1 << level) % 2 == 1
        halves = [
            entry.reshape((count >> level + 1, 2, 1 << level) + entry.shape[1:]) for entry in items
        ]
        outgoing = tuple(
            (jnp.where(upper_half, halves_one[:, 0], halves_one[:, 1]) for halves_one in halves)
        )
        incoming = mover(outgoing, level)
        rebuilt = []
        for entry, halves_one, arrived_one in zip(items, halves, incoming):
            lower_part = jnp.where(upper_half, arrived_one, halves_one[:, 0])
            upper_part = jnp.where(upper_half, halves_one[:, 1], arrived_one)
            rebuilt.append(jnp.stack([lower_part, upper_part], axis=1).reshape(entry.shape))
        items = tuple(rebuilt)
    return items


def body(
    queries,
    new_kv,
    kv_pages,
    page_table,
    lengths,
    residual,
    out_weight,
    norm_gain,
    gate_weight,
    up_weight,
    down_weight,
):
    seq_dev = queries.shape[0]
    page_count = kv_pages.shape[0]
    page_len = kv_pages.shape[2]
    all_seqs = page_table.shape[0]
    max_pages = page_table.shape[1]
    group_size = HEADS // KV_HEADS
    score_scale = 1.0 / math.sqrt(HEAD_DIM)
    device_pos = lax.axis_index("shard")
    own_first = device_pos * seq_dev
    own_lengths = lax.dynamic_slice_in_dim(lengths, own_first, seq_dev, 0)
    own_table = lax.dynamic_slice_in_dim(page_table, own_first, seq_dev, 0)
    holder_local = own_table // page_count % page_count
    page_ids = device_pos * page_count + jnp.arange(page_count, dtype=jnp.int32)
    matches = page_table[None, :, :] == page_ids[:, None, None]
    seq_of = jnp.sum(
        jnp.where(matches, jnp.arange(all_seqs, dtype=jnp.int32)[None, :, None], 0), axis=(1, 2)
    )
    owner_local = seq_of // seq_dev % page_count
    own_numerator, own_denominator = new_token_terms(queries, new_kv, score_scale)
    outgoing = jnp.zeros_like(kv_pages).at[owner_local].set(kv_pages)
    arrived = butterfly(
        (outgoing,), device_pos, lambda sending, level: (swapped(sending[0], "shard", level),)
    )[0]
    fetched = arrived[holder_local]
    context = max_pages * page_len
    key_rows = fetched[:, :, 0].reshape(seq_dev, context, KV_HEADS, HEAD_DIM)
    value_rows = fetched[:, :, 1].reshape(seq_dev, context, KV_HEADS, HEAD_DIM)
    query_heads = queries.reshape(seq_dev, KV_HEADS, group_size, HEAD_DIM)
    scores = (
        jnp.einsum("bgqd,btgd->bgqt", query_heads, key_rows, preferred_element_type=jnp.float32)
        * score_scale
    )
    position = jnp.arange(context, dtype=jnp.int32)
    alive = position[None, :] < own_lengths[:, None]
    weights = jnp.where(alive[:, None, None, :], jnp.exp(scores), 0.0)
    denominator = jnp.sum(weights, axis=-1).reshape(seq_dev, HEADS)
    numerator = jnp.einsum(
        "bgqt,btgd->bgqd",
        weights.astype(jnp.bfloat16),
        value_rows,
        preferred_element_type=jnp.float32,
    )
    numer_rows = numerator.reshape(seq_dev, D) + own_numerator
    denom_rows = denominator + own_denominator
    attended = (
        (numer_rows.reshape(seq_dev, HEADS, HEAD_DIM) / denom_rows[:, :, None])
        .reshape(seq_dev, D)
        .astype(jnp.bfloat16)
    )
    projected = jnp.dot(
        lax.all_gather(attended, "shard", axis=0, tiled=True),
        out_weight,
        preferred_element_type=jnp.float32,
    )
    stream = (residual.astype(jnp.float32) + projected).astype(jnp.bfloat16)
    wide = stream.astype(jnp.float32)
    square_sums = lax.psum(jnp.sum(wide * wide, axis=1), "shard")
    normed = (wide * lax.rsqrt(square_sums / D + norm_eps)[:, None] * norm_gain[None, :]).astype(
        jnp.bfloat16
    )
    block_cols = lax.all_gather(normed, "shard", axis=1, tiled=True)
    gate_acts = jnp.dot(block_cols, gate_weight, preferred_element_type=jnp.float32)
    up_acts = jnp.dot(block_cols, up_weight, preferred_element_type=jnp.float32)
    hidden = (jax.nn.silu(gate_acts) * up_acts).astype(jnp.bfloat16)
    partial_terms = jnp.dot(hidden, down_weight, preferred_element_type=jnp.float32)
    down_terms = lax.psum_scatter(partial_terms, "shard", scatter_dimension=1, tiled=True)
    return (wide + down_terms).astype(jnp.bfloat16)


GROUP = HEADS // KV_HEADS
HEAD_ROWS = 72
MIB = 2**20
VMEM_SPEC = pl.BlockSpec(memory_space=pltpu.VMEM)
SMEM_SPEC = pl.BlockSpec(memory_space=pltpu.SMEM)
HBM_SPEC = pl.BlockSpec(memory_space=pltpu.HBM)
CHUNK = 512


def sent(array, distance):
    size = lax.axis_size("shard")
    return lax.ppermute(array, "shard", [(i, i ^ distance) for i in range(size)])


def stack_kernel(count, *refs):
    out_ref, place = refs[-1], 0
    for part in refs[:count]:
        size = part.shape[0] if len(part.shape) == 3 else 1
        out_ref[place : place + size] = part[...].reshape((size,) + part.shape[-2:])
        place += size


def stacked(parts, after):
    size = sum(part.shape[0] if part.ndim == 3 else 1 for part in parts)
    return pl.pallas_call(
        functools.partial(stack_kernel, len(parts)),
        in_specs=[VMEM_SPEC] * len(parts) + [pl.BlockSpec(memory_space=pl.ANY)] * len(after),
        out_specs=VMEM_SPEC,
        out_shape=jax.ShapeDtypeStruct((size,) + parts[0].shape[-2:], parts[0].dtype),
        compiler_params=pltpu.CompilerParams(vmem_limit_bytes=4 * MIB),
        cost_estimate=pl.CostEstimate(flops=0, bytes_accessed=16 * MIB, transcendentals=0),
    )(*parts, *after)


def near_pieces(piece):
    return [piece] + [sent(piece, distance) for distance in (4, 8, 12)]


def device_at(me, entry):
    return me ^ (entry % 4 * 4 + entry // 4 % 2 * 2 + entry // 8)


def started(count, copy_at):
    def start(place, carry):
        copy_at(place).start()
        return carry

    lax.fori_loop(0, count, start, 0)


def in_vmem(array):
    return pltpu.with_memory_space_constraint(array, pltpu.VMEM)


def in_hbm(array):
    return pltpu.with_memory_space_constraint(array, pltpu.HBM)


def two_terms(wide):
    high = wide.astype(jnp.bfloat16).astype(jnp.float32)
    return high, wide - high


def pack_kernel(query_hbm, gain_hbm, out_ref, rows_ref, query, gain, wide, sems):
    copies = [
        pltpu.make_async_copy(query_hbm, query, sems.at[0]),
        pltpu.make_async_copy(gain_hbm, gain, sems.at[1]),
    ]
    for copy in copies:
        copy.start()
    for copy in copies:
        copy.wait()
    rows = 2 * HEADS
    for head in range(HEADS):
        cols = slice(head * HEAD_DIM, (head + 1) * HEAD_DIM)
        wide[pl.ds(head, 2, HEADS), :] = query[:, cols].astype(jnp.float32)
    out_ref[:rows, :] = wide[...].astype(jnp.bfloat16)
    rows_ref[...] = wide[...].astype(jnp.bfloat16)
    high, rest = two_terms(gain[...])
    middle, low = two_terms(rest)
    filler = jnp.zeros((16 - 3 * high.shape[0], HEAD_DIM), jnp.float32)
    out_ref[rows:, :] = jnp.concatenate([high, middle, low, filler]).astype(jnp.bfloat16)


def packed(queries, norm_gain):
    rows = 2 * HEADS
    gain = norm_gain.reshape(-1, HEAD_DIM)
    return pl.pallas_call(
        pack_kernel,
        in_specs=[HBM_SPEC] * 2,
        out_specs=[VMEM_SPEC] * 2,
        out_shape=[
            jax.ShapeDtypeStruct((rows + 16, HEAD_DIM), jnp.bfloat16),
            jax.ShapeDtypeStruct((rows, HEAD_DIM), jnp.bfloat16),
        ],
        scratch_shapes=[
            pltpu.VMEM(queries.shape, jnp.bfloat16),
            pltpu.VMEM(gain.shape, jnp.float32),
            pltpu.VMEM((rows, HEAD_DIM), jnp.float32),
            pltpu.SemaphoreType.DMA((2,)),
        ],
        compiler_params=pltpu.CompilerParams(vmem_limit_bytes=4 * MIB),
    )(in_hbm(queries), in_hbm(gain))


def context_terms(query, keys, values, alive):
    numerators, denominators = [], []
    for head in range(KV_HEADS):
        cols = slice(head * HEAD_DIM, (head + 1) * HEAD_DIM)
        scores = lax.dot_general(
            query[head * GROUP : (head + 1) * GROUP],
            keys[:, cols],
            (((1,), (1,)), ((), ())),
            preferred_element_type=jnp.float32,
        ) * (1.0 / math.sqrt(HEAD_DIM))
        weights = jnp.where(alive, jnp.exp(scores), 0.0)
        denominators.append(jnp.sum(weights, axis=1, keepdims=True))
        numerators.append(
            jnp.dot(
                weights.astype(jnp.bfloat16), values[:, cols], preferred_element_type=jnp.float32
            )
        )
    return jnp.concatenate(numerators), jnp.concatenate(denominators)


def ready_kernel(table_ref, query_ref, pages_hbm, new_hbm, pages, left_ref, second_ref, new_ref, new, sems):
    _, _, page_len, features = pages.shape
    count = pages_hbm.shape[0]
    sequences = 2 * 16
    per_row = (table_ref.shape[0] - 1) // sequences - 1
    me = table_ref[(per_row + 1) * sequences]
    new_copy = pltpu.make_async_copy(new_hbm, new, sems.at[16])
    new_copy.start()
    page_copy = lambda slot, entry: pltpu.make_async_copy(
        pages_hbm.at[slot], pages.at[entry], sems.at[entry]
    )
    line = lambda value: jnp.full((1, HEAD_DIM), value, dtype=jnp.int32)

    def ready(entry, carry):
        owner = device_at(me, entry)
        place, other = 0, 0
        for index in range(2 * per_row):
            holder = table_ref[2 * owner * per_row + index] // count
            place = jnp.where(holder == me, index, place)
            other = jnp.where(holder == me ^ 1, index, other)
        row = place // per_row
        slot = table_ref[2 * owner * per_row + place] % count
        page_copy(slot, entry).start()
        left = table_ref[sequences * per_row + 2 * owner + row] - page_len * (place % per_row)
        here = pl.ds(entry, 1)
        left_ref[here, :] = line(left)
        second_ref[here, :] = line(row)
        second_ref[pl.ds(16 + entry, 1), :] = line(other // per_row)
        return carry

    lax.fori_loop(0, 16, ready, 0)
    first_token = lax.broadcasted_iota(jnp.int32, (GROUP, 8), 1) < 1
    new_copy.wait()
    for row in range(2):
        lines = slice(row * HEADS, (row + 1) * HEADS)
        numerator, total = context_terms(
            query_ref[lines, :],
            jnp.broadcast_to(new[row, 0:1, :], (8, features)),
            jnp.broadcast_to(new[row, 1:2, :], (8, features)),
            first_token,
        )
        new_ref[0, lines, :] = numerator
        new_ref[1, lines, :] = jnp.broadcast_to(total, (HEADS, HEAD_DIM))
    for entry in range(16):
        page_copy(0, entry).wait()


def readied(table, query_rows, kv_pages, new_kv):
    return pl.pallas_call(
        ready_kernel,
        in_specs=[SMEM_SPEC, VMEM_SPEC] + [HBM_SPEC] * 2,
        out_specs=[VMEM_SPEC] * 4,
        out_shape=[
            pltpu.VMEM(kv_pages.shape, kv_pages.dtype),
            jax.ShapeDtypeStruct((16, HEAD_DIM), jnp.int32),
            jax.ShapeDtypeStruct((32, HEAD_DIM), jnp.int32),
            jax.ShapeDtypeStruct((2, 2 * HEADS, HEAD_DIM), jnp.float32),
        ],
        scratch_shapes=[pltpu.VMEM(new_kv.shape, jnp.bfloat16), pltpu.SemaphoreType.DMA((17,))],
        compiler_params=pltpu.CompilerParams(vmem_limit_bytes=4 * MIB),
        cost_estimate=pl.CostEstimate(flops=2**22, bytes_accessed=2**21, transcendentals=2**11),
    )(table, query_rows, in_hbm(kv_pages), in_hbm(new_kv))


def pages_kernel(entries, left_ref, second_ref, *refs):
    refs = list(refs)
    near, across = (refs.pop(0), refs.pop(0)) if entries[0] < 8 else (None, None)
    odd = None if entries[0] < 8 else refs.pop(0)
    pages, out_ref, scores, weights = refs[0], *refs[-3:]
    page_len, features = pages.shape[2:]
    line = lax.broadcasted_iota(jnp.int32, (HEADS, features), 0) // GROUP
    block = lax.broadcasted_iota(jnp.int32, (HEADS, features), 1) // HEAD_DIM
    own_block = (line == block).astype(jnp.float32).astype(jnp.bfloat16)
    for here, entry in enumerate(entries):
        source, place = piece_at(near, across, odd, entry)
        second = second_ref[entry : entry + 1, :].astype(jnp.float32)
        query = source[place, :HEADS, :].astype(jnp.float32) * (1.0 - second)
        query += source[place, HEADS : 2 * HEADS, :].astype(jnp.float32) * second
        query = query.astype(jnp.bfloat16)
        spread = jnp.concatenate([query] * KV_HEADS, axis=1) * own_block
        scores[here] = lax.dot_general(
            spread,
            pages[entry, 0],
            (((1,), (1,)), ((), ())),
            preferred_element_type=jnp.float32,
        )
    position = lax.broadcasted_iota(jnp.int32, (HEADS, page_len), 1)
    lane = lax.broadcasted_iota(jnp.int32, (HEADS, HEAD_DIM), 1)
    denominators = jnp.zeros((HEADS, HEAD_DIM), jnp.float32)
    for here, entry in enumerate(entries):
        raised = jnp.exp(scores[here] * (1.0 / math.sqrt(HEAD_DIM)))
        weight = jnp.where(position < left_ref[entry : entry + 1, :page_len], raised, 0.0)
        weights[here] = weight.astype(jnp.bfloat16)
        total = jnp.sum(weight, axis=1, keepdims=True)
        denominators = jnp.where(lane == here, total, denominators)
    for here, entry in enumerate(entries):
        numerator = jnp.dot(
            weights[here], pages[entry, 1], preferred_element_type=jnp.float32
        )
        for head in range(KV_HEADS):
            lines = slice(head * GROUP, (head + 1) * GROUP)
            out_ref[here, lines, :] = numerator[
                lines, head * HEAD_DIM : (head + 1) * HEAD_DIM
            ].astype(jnp.bfloat16)
    high, low = two_terms(jnp.swapaxes(denominators, 0, 1)[: len(entries)])
    lasts = jnp.concatenate([high, low], axis=1)
    first_line = lax.broadcasted_iota(jnp.int32, (HEAD_ROWS - HEADS, HEAD_DIM), 0) == 0
    for here, entry in enumerate(entries):
        out_ref[here, HEADS:, :] = jnp.where(
            first_line, lasts[here : here + 1], 0.0
        ).astype(jnp.bfloat16)


def piece_at(near, second, odd, entry):
    if entry < 4:
        return near, entry
    return (second, entry - 4) if entry < 8 else (odd, entry - 8)


def page_terms(left, second, entries, pieces, pages, beside=()):
    return pl.pallas_call(
        functools.partial(pages_kernel, entries),
        in_specs=[VMEM_SPEC] * (len(pieces) + 3)
        + [pl.BlockSpec(memory_space=pl.ANY)] * len(beside),
        out_specs=VMEM_SPEC,
        out_shape=jax.ShapeDtypeStruct((len(entries), HEAD_ROWS, HEAD_DIM), jnp.bfloat16),
        scratch_shapes=[
            pltpu.VMEM((len(entries), HEADS, pages.shape[2]), jnp.float32),
            pltpu.VMEM((len(entries), HEADS, pages.shape[2]), jnp.bfloat16),
        ],
        compiler_params=pltpu.CompilerParams(vmem_limit_bytes=6 * MIB),
        cost_estimate=pl.CostEstimate(flops=2**26, bytes_accessed=2**20, transcendentals=2**14),
    )(left, second, *pieces, in_vmem(pages), *beside)


def opened(piece):
    last = piece[HEADS:, :].astype(jnp.float32)[:1]
    return piece[:HEADS, :].astype(jnp.float32), last[:, :HEADS] + last[:, HEADS:]


def closed(numerator, denominator):
    last = jnp.concatenate(two_terms(denominator), axis=1)
    first_line = lax.broadcasted_iota(jnp.int32, (HEAD_ROWS - HEADS, HEAD_DIM), 0) == 0
    return numerator.astype(jnp.bfloat16), jnp.where(first_line, last, 0.0).astype(jnp.bfloat16)


def two_rows(second_ref, entry, mine, theirs):
    sums = [[0.0, 0.0], [0.0, 0.0]]
    for line, (numerator, denominator) in zip((entry, 16 + entry), (mine, theirs)):
        second = second_ref[line : line + 1, :].astype(jnp.float32)
        for row, share in enumerate((1.0 - second, second)):
            sums[row][0] = sums[row][0] + numerator * share
            sums[row][1] = sums[row][1] + denominator * share[:, :HEADS]
    return sums


def core_kernel(second_ref, mine_ref, theirs_ref, out_ref):
    for place in range(4):
        mine, theirs = opened(mine_ref[place]), opened(theirs_ref[4 + place])
        for row, terms in enumerate(two_rows(second_ref, 4 + place, mine, theirs)):
            out_ref[place, row, :HEADS, :], out_ref[place, row, HEADS:, :] = closed(*terms)


def across_core(second, mine, theirs):
    return pl.pallas_call(
        core_kernel,
        in_specs=[VMEM_SPEC] * 3,
        out_specs=VMEM_SPEC,
        out_shape=jax.ShapeDtypeStruct((4, 2, HEAD_ROWS, HEAD_DIM), jnp.bfloat16),
        compiler_params=pltpu.CompilerParams(vmem_limit_bytes=4 * MIB),
    )(second, mine, theirs)


def chip_kernel(second_ref, mine_ref, theirs_ref, arrived_ref, unused_ref, *out_refs):
    for place in range(4):
        mine, theirs = opened(mine_ref[place]), opened(theirs_ref[place])
        for row, terms in enumerate(two_rows(second_ref, place, mine, theirs)):
            numerator, denominator = opened(arrived_ref[place, row])
            sums = closed(terms[0] + numerator, terms[1] + denominator)
            out_refs[place][row, :HEADS, :], out_refs[place][row, HEADS:, :] = sums


def across_y(second, mine, theirs, arrived, beside):
    return pl.pallas_call(
        chip_kernel,
        in_specs=[VMEM_SPEC] * 4 + [pl.BlockSpec(memory_space=pl.ANY)],
        out_specs=[VMEM_SPEC] * 4,
        out_shape=[jax.ShapeDtypeStruct((2, HEAD_ROWS, HEAD_DIM), jnp.bfloat16)] * 4,
        compiler_params=pltpu.CompilerParams(vmem_limit_bytes=4 * MIB),
    )(second, mine, theirs, arrived, beside)


def combine_kernel(*refs):
    shares, new_ref, out_ref = refs[:4], refs[4], refs[-1]
    for row in range(2):
        lines = slice(row * HEADS, (row + 1) * HEADS)
        total, lower = new_ref[0, lines, :], jnp.zeros((1, HEADS), jnp.float32)
        for share in shares:
            numerator, denominator = opened(share[row])
            total = total + numerator
            lower = lower + denominator
        padded = jnp.concatenate([lower, jnp.zeros((1, HEADS), jnp.float32)], axis=1)
        column = jnp.swapaxes(jnp.broadcast_to(padded, (8, HEAD_DIM)), 0, 1)[:HEADS, :1]
        out_ref[lines, :] = (total / (column + new_ref[1, lines, :])).astype(jnp.bfloat16)


def combined(shares, new_terms, beside):
    return pl.pallas_call(
        combine_kernel,
        in_specs=[VMEM_SPEC] * 5 + [pl.BlockSpec(memory_space=pl.ANY)],
        out_specs=VMEM_SPEC,
        out_shape=jax.ShapeDtypeStruct((2 * HEADS, HEAD_DIM), jnp.bfloat16),
        compiler_params=pltpu.CompilerParams(vmem_limit_bytes=4 * MIB),
        cost_estimate=pl.CostEstimate(
            flops=2**22, bytes_accessed=48 * MIB, transcendentals=2**11
        ),
    )(*shares, new_terms, beside)


def fetch_kernel(parts, after_ref, *refs):
    weights, outs, sems = refs[: len(parts)], refs[len(parts) : -1], refs[-1]
    me = lax.axis_index("shard")
    copies = []
    for (place_of, entries), weight_hbm, out_ref in zip(parts, weights, outs):
        for place, entry in enumerate(entries):
            copies.append(
                pltpu.make_async_copy(
                    place_of(weight_hbm, device_at(me, entry)),
                    out_ref.at[place],
                    sems.at[len(copies)],
                )
            )
    for copy in copies:
        copy.start()
    for copy in copies:
        copy.wait()


def fetched(after, *parts):
    count = sum(len(entries) for _, _, entries in parts)
    weights = [weight for weight, _, _ in parts]
    shapes = [
        pltpu.VMEM((len(entries),) + place_of(weight, None), weight.dtype)
        for weight, place_of, entries in parts
    ]
    size = sum(math.prod(shape.shape) for shape in shapes)
    return pl.pallas_call(
        functools.partial(fetch_kernel, [part[1:] for part in parts]),
        in_specs=[pl.BlockSpec(memory_space=pl.ANY)] + [HBM_SPEC] * len(parts),
        out_specs=[VMEM_SPEC] * len(parts),
        out_shape=shapes,
        scratch_shapes=[pltpu.SemaphoreType.DMA((count,))],
        compiler_params=pltpu.CompilerParams(vmem_limit_bytes=MIB),
        cost_estimate=pl.CostEstimate(flops=0, bytes_accessed=2 * size, transcendentals=0),
    )(after, *[in_hbm(weight) for weight in weights])


def rows_at(weight, device):
    if device is None:
        return (CHUNK, weight.shape[1])
    return weight.at[pl.ds(pl.multiple_of(device * CHUNK, CHUNK), CHUNK)]


def columns_at(weight, device):
    if device is None:
        return (weight.shape[0], CHUNK)
    return weight.at[:, pl.ds(pl.multiple_of(device * CHUNK, CHUNK), CHUNK)]


def out_kernel(
    near_ref,
    second_ref,
    odd_ref,
    weight_ref,
    residual,
    out_ref,
    wide,
    left,
):
    me = lax.axis_index("shard")
    for entry in range(16):
        source, place = piece_at(near_ref, second_ref, odd_ref, entry)
        start = pl.multiple_of(device_at(me, entry) * 2 * HEADS, 2 * HEADS)
        wide[pl.ds(start, 2 * HEADS), :] = source[place].astype(jnp.float32)
    for head in range(HEADS):
        rows = [wide[pl.ds(row * HEADS + head, 16, 2 * HEADS), :] for row in range(2)]
        left[:, head * HEAD_DIM : (head + 1) * HEAD_DIM] = jnp.concatenate(rows).astype(
            jnp.bfloat16
        )
    total = jnp.dot(left[...], weight_ref[...], preferred_element_type=jnp.float32)
    line = lax.broadcasted_iota(jnp.int32, (32, 32), 0)
    entry = lax.broadcasted_iota(jnp.int32, (32, 32), 1)
    turn = ((line % 2) * 16 + line // 2 == entry).astype(jnp.float32)
    turned = lax.dot_general(
        turn,
        total,
        (((1,), (0,)), ((), ())),
        precision=lax.Precision.HIGHEST,
        preferred_element_type=jnp.float32,
    )
    out_ref[...] = (residual[...].astype(jnp.float32) + turned).astype(jnp.bfloat16)


def projected(near, second, odd, residual, held_weight):
    rows, width = residual.shape
    return pl.pallas_call(
        out_kernel,
        in_specs=[VMEM_SPEC] * 5,
        out_specs=VMEM_SPEC,
        out_shape=jax.ShapeDtypeStruct((rows, width), jnp.bfloat16),
        scratch_shapes=[
            pltpu.VMEM((32 * HEADS, HEAD_DIM), jnp.float32),
            pltpu.VMEM((rows, D), jnp.bfloat16),
        ],
        compiler_params=pltpu.CompilerParams(vmem_limit_bytes=4 * MIB),
        cost_estimate=pl.CostEstimate(
            flops=2 * rows * D * width, bytes_accessed=2 * D * width, transcendentals=0
        ),
    )(near, second, odd, held_weight, residual)


def normed_pieces(entries, pieces, gain_ref, squares):
    lefts = []
    for place, entry in enumerate(entries):
        stream = pieces[place][...] if len(pieces) == len(entries) else pieces[0][place]
        wide = stream.astype(jnp.float32)
        squares = squares + wide * wide
        terms = gain_ref[entry % 4 if entry < 8 else entry - 8, 2 * HEADS :, :]
        terms = terms.astype(jnp.float32)
        gain = terms[0:4] + terms[4:8] + terms[8:12]
        gain = jnp.concatenate([gain[part : part + 1] for part in range(4)], axis=1)
        lefts.append((wide * gain).astype(jnp.bfloat16))
    return lefts, squares


def terms_of(lefts, blocks):
    left = jnp.concatenate(lefts, axis=1)
    weight = blocks[...].reshape(left.shape[1], blocks.shape[-1])
    return jnp.dot(left, weight, preferred_element_type=jnp.float32)


def feed_kernel(entries, piece_count, held, *refs):
    refs = list(refs)
    take = lambda number: [refs.pop(0) for _ in range(number)]
    pieces = take(piece_count)
    gain_ref, gate_ref, up_ref = take(3)
    gates_in, ups_in, squares_in = [None] * 3 if entries[0] == 0 else take(3)
    gates, ups, squares_out = take(3)
    copies = []
    if not held:
        sources = gate_ref, up_ref
        *targets, sems = refs
        gate_ref, up_ref = targets
        me = lax.axis_index("shard")
        count = len(entries)
        copies = [
            lambda place, number=number: pltpu.make_async_copy(
                rows_at(sources[number], device_at(me, entries[0] + place)),
                targets[number].at[place],
                sems.at[number * count + place],
            )
            for number in range(2)
        ]
        for copy_at in copies:
            started(count, copy_at)
    squares = 0.0 if squares_in is None else squares_in[...]
    lefts, squares_out[...] = normed_pieces(entries, pieces, gain_ref, squares)
    for number, (total, start, blocks) in enumerate(
        ((gates, gates_in, gate_ref), (ups, ups_in, up_ref))
    ):
        for place in range(len(entries) if copies else 0):
            copies[number](place).wait()
        terms = terms_of(lefts, blocks)
        total[...] = terms if start is None else start[...] + terms


def feed(entries, pieces, gain, sums, gate_weight, up_weight, held=False):
    rows = pieces[0].shape[-2]
    width = gate_weight.shape[-1]
    count = len(entries)
    total = jax.ShapeDtypeStruct((rows, width), jnp.float32)
    here = in_vmem if held else in_hbm
    slots = pltpu.VMEM((count, CHUNK, width), jnp.bfloat16)
    return pl.pallas_call(
        functools.partial(feed_kernel, entries, len(pieces), held),
        in_specs=[VMEM_SPEC] * (len(pieces) + 1)
        + [VMEM_SPEC if held else HBM_SPEC] * 2
        + [VMEM_SPEC] * len(sums),
        out_specs=[VMEM_SPEC] * 3,
        out_shape=[total, total, jax.ShapeDtypeStruct((rows, CHUNK), jnp.float32)],
        scratch_shapes=[] if held else [slots, slots, pltpu.SemaphoreType.DMA((2 * count,))],
        compiler_params=pltpu.CompilerParams(
            vmem_limit_bytes=2 * MIB + (0 if held else 4 * count * CHUNK * width)
        ),
        cost_estimate=pl.CostEstimate(
            flops=4 * rows * count * CHUNK * width,
            bytes_accessed=4 * count * CHUNK * width,
            transcendentals=0,
        ),
    )(*pieces, gain, here(gate_weight), here(up_weight), *sums)


def hidden_kernel(entries, early_counts, *refs):
    refs = list(refs)
    take = lambda number: [refs.pop(0) for _ in range(number)]
    odd_ref, gain_ref = take(2)
    early = [take(number) for number in early_counts]
    sources = take(2)
    (down_hbm,) = take(1)
    starts = take(2)
    squares_in, hidden_ref, out_ref = take(3)
    totals = take(2)
    held, sems = take(2), take(2)
    down_held, down_sems = refs
    me = lax.axis_index("shard")
    count = len(entries)
    counts = [buffer.shape[0] for buffer in held]
    copies = [
        lambda place, number=number: pltpu.make_async_copy(
            rows_at(sources[number], device_at(me, entries[-1] + 1 - counts[number] + place)),
            held[number].at[place],
            sems[number].at[place],
        )
        for number in range(2)
    ]
    down_copy = lambda place: pltpu.make_async_copy(
        columns_at(down_hbm, device_at(me, entries[0] + place)),
        down_held.at[place],
        down_sems.at[place],
    )
    for number in range(2):
        started(counts[number], copies[number])
    started(count, down_copy)
    lefts, squares = normed_pieces(entries, [odd_ref], gain_ref, squares_in[...])
    places = [0, 0]
    for number in range(2):
        total = starts[number][...]
        for part in early[number]:
            place = places[number]
            places[number] += part.shape[0]
            total += terms_of(lefts[place : places[number]], part)
        totals[number][...] = total
    for number in range(2):
        for place in range(counts[number]):
            copies[number](place).wait()
        totals[number][...] += terms_of(lefts[places[number] :], held[number])
    scale = lax.rsqrt(jnp.sum(squares, axis=1, keepdims=True) / D + norm_eps)
    gates, ups = totals[0][...] * scale, totals[1][...] * scale
    hidden_ref[...] = (jax.nn.silu(gates) * ups).astype(jnp.bfloat16)
    for place in range(count):
        down_copy(place).wait()
        out_ref[place] = jnp.dot(
            hidden_ref[...], down_held[place], preferred_element_type=jnp.float32
        ).astype(jnp.bfloat16)


def hidden_units(entries, odd, gain, early, weights, down_weight, sums):
    rows = odd.shape[1]
    width = weights[0].shape[1]
    count = len(entries)
    later = [count - sum(part.shape[0] for part in parts) for parts in early]
    total = pltpu.VMEM((rows, width), jnp.float32)
    held = [pltpu.VMEM((number, CHUNK, width), jnp.bfloat16) for number in later]
    early_parts = [part for parts in early for part in parts]
    return pl.pallas_call(
        functools.partial(hidden_kernel, entries, [len(parts) for parts in early]),
        in_specs=[VMEM_SPEC] * (2 + len(early_parts)) + [HBM_SPEC] * 3 + [VMEM_SPEC] * 3,
        out_specs=[VMEM_SPEC] * 2,
        out_shape=[
            jax.ShapeDtypeStruct((rows, width), jnp.bfloat16),
            jax.ShapeDtypeStruct((count, rows, CHUNK), jnp.bfloat16),
        ],
        scratch_shapes=[total, total]
        + held
        + [pltpu.SemaphoreType.DMA((number,)) for number in later]
        + [pltpu.VMEM((count, width, CHUNK), jnp.bfloat16), pltpu.SemaphoreType.DMA((count,))],
        compiler_params=pltpu.CompilerParams(
            vmem_limit_bytes=2 * (sum(later) + count) * CHUNK * width + 2 * MIB
        ),
        cost_estimate=pl.CostEstimate(
            flops=2 * rows * 3 * count * CHUNK * width,
            bytes_accessed=2 * 3 * count * CHUNK * width,
            transcendentals=rows * width,
        ),
    )(
        odd,
        gain,
        *[in_vmem(part) for part in early_parts],
        *[in_hbm(weight) for weight in weights],
        in_hbm(down_weight),
        *sums,
    )


def down_kernel(choice, hidden_ref, *refs):
    out_ref = refs[-1]
    for place, (number, index) in enumerate(choice):
        out_ref[place] = jnp.dot(
            hidden_ref[...], refs[number][index], preferred_element_type=jnp.float32
        )


def down_terms(hidden, parts, choice):
    rows, depth = hidden.shape
    return pl.pallas_call(
        functools.partial(down_kernel, choice),
        in_specs=[VMEM_SPEC] * (1 + len(parts)),
        out_specs=VMEM_SPEC,
        out_shape=jax.ShapeDtypeStruct((len(choice), rows, CHUNK), jnp.float32),
        compiler_params=pltpu.CompilerParams(vmem_limit_bytes=4 * MIB),
        cost_estimate=pl.CostEstimate(
            flops=2 * rows * depth * CHUNK * len(choice),
            bytes_accessed=2 * depth * CHUNK * len(choice),
            transcendentals=0,
        ),
    )(hidden, *[in_vmem(part) for part in parts])


def far_kernel(mine_ref, theirs_ref, out_ref):
    for place in range(4):
        out_ref[place] = (mine_ref[place] + theirs_ref[4 + place].astype(jnp.float32)).astype(
            jnp.bfloat16
        )


def far_pairs(mine, theirs):
    return pl.pallas_call(
        far_kernel,
        in_specs=[VMEM_SPEC] * 2,
        out_specs=VMEM_SPEC,
        out_shape=jax.ShapeDtypeStruct((4,) + theirs.shape[1:], jnp.bfloat16),
        compiler_params=pltpu.CompilerParams(vmem_limit_bytes=4 * MIB),
    )(mine, theirs)


def near_kernel(mine_ref, theirs_ref, arrived_ref, own_ref, *out_refs):
    for place, out_ref in enumerate((own_ref,) + out_refs):
        total = mine_ref[place] + theirs_ref[place].astype(jnp.float32)
        total = total + arrived_ref[place].astype(jnp.float32)
        out_ref[...] = total.astype(out_ref.dtype)


def near_sums(mine, theirs, arrived):
    block = theirs.shape[1:]
    return pl.pallas_call(
        near_kernel,
        in_specs=[VMEM_SPEC] * 3,
        out_specs=[VMEM_SPEC] * 4,
        out_shape=[jax.ShapeDtypeStruct(block, jnp.float32)]
        + [jax.ShapeDtypeStruct(block, jnp.bfloat16)] * 3,
        compiler_params=pltpu.CompilerParams(vmem_limit_bytes=4 * MIB),
    )(mine, theirs, arrived)


def finish_kernel(stream_ref, *refs):
    total = stream_ref[...].astype(jnp.float32)
    for share in refs[:-1]:
        total = total + share[...].astype(jnp.float32)
    refs[-1][...] = total.astype(jnp.bfloat16)


def finished(stream, shares):
    return pl.pallas_call(
        finish_kernel,
        in_specs=[VMEM_SPEC] * (1 + len(shares)),
        out_specs=VMEM_SPEC,
        out_shape=jax.ShapeDtypeStruct(stream.shape, jnp.bfloat16),
        compiler_params=pltpu.CompilerParams(vmem_limit_bytes=4 * MIB),
    )(stream, *shares)


def block_body(
    queries,
    new_kv,
    kv_pages,
    page_table,
    lengths,
    residual,
    out_weight,
    norm_gain,
    gate_weight,
    up_weight,
    down_weight,
):
    me = lax.axis_index("shard").astype(jnp.int32)[None]
    table = jnp.concatenate([page_table.reshape(-1), lengths, me])
    own, query_rows = packed(queries, norm_gain)
    middle, late = (4, 5, 6, 7), tuple(range(8, 16))

    pages, left, of_second, new_terms = readied(table, query_rows, kv_pages, new_kv)
    near = stacked(near_pieces(own), (new_terms,))
    second = sent(near, 2)
    (early_gate,) = fetched(near, (gate_weight, rows_at, late[:5]))
    odd = sent(stacked([near, second], (early_gate,)), 1)
    gains = near, second, odd
    along = page_terms(left, of_second, (0, 1, 2, 3), (near, second), pages)
    theirs = page_terms(left, of_second, late, (odd,), pages, (along,))
    across = page_terms(left, of_second, middle, (near, second), pages)

    theirs = sent(theirs, 1)
    across = across_core(of_second, across, theirs)
    arrived = sent(across, 2)
    gate_held, early_first = fetched(
        across, (gate_weight, rows_at, middle), (up_weight, rows_at, late[:2])
    )
    own, *others = across_y(of_second, along, theirs, arrived, gate_held)
    up_held, early_second = fetched(
        own, (up_weight, rows_at, middle), (up_weight, rows_at, late[2:4])
    )
    shares = [sent(other, distance) for other, distance in zip(others[::-1], (12, 8, 4))]
    attended = combined(shares + [own], new_terms, up_held)

    down_first, early_third = fetched(
        attended, (down_weight, columns_at, middle[:2]), (up_weight, rows_at, late[4:6])
    )
    near = stacked(near_pieces(attended), (down_first,))
    second = sent(near, 2)
    (down_rest,) = fetched(near, (down_weight, columns_at, middle[2:] + (0, 1, 2, 3)))
    odd = sent(stacked([near, second], (down_rest,)), 1)
    stream = projected(near, second, odd, residual, out_weight)

    weights = gate_weight, up_weight
    near = near_pieces(stream)
    sums = feed((0,), near[:1], gains[0], (), *weights)
    first = stacked(near, sums[:1])
    second = sent(first, 2)
    sums = feed((1, 2, 3), near[1:], gains[0], sums, *weights)
    odd = sent(stacked([first, second], sums[:1]), 1)
    sums = feed(middle, [second], gains[1], sums, gate_held, up_held, held=True)
    early = (early_gate,), (early_first, early_second, early_third)
    hidden, theirs = hidden_units(late, odd, gains[2], early, weights, down_weight, sums)

    theirs = sent(theirs, 1)
    far = down_terms(hidden, (down_first, down_rest), ((0, 0), (0, 1), (1, 0), (1, 1)))
    arrived = sent(far_pairs(far, theirs), 2)
    mine = down_terms(hidden, (down_rest,), ((0, 2), (0, 3), (0, 4), (0, 5)))
    own, *others = near_sums(mine, theirs, arrived)
    shares = [sent(other, distance) for other, distance in zip(others[::-1], (12, 8, 4))]
    return finished(stream, shares + [own])


def solution(mesh):
    placed = (
        P(("groups", "shard"), None),
        P(("groups", "shard"), None, None),
        P(("groups", "shard"), None, None, None),
        P("groups", None),
        P("groups"),
        P("groups", "shard"),
        P(None, "shard"),
        P("shard"),
        P(None, "shard"),
        P(None, "shard"),
        P("shard", None),
    )
    chosen = block_body if mesh.shape["shard"] == 16 else body
    return jax.shard_map(
        chosen, mesh=mesh, in_specs=placed, out_specs=P("groups", "shard"), check_vma=False
    )
```

time: 99.6 us -> 94.1 us (0.945)
  blocking collectives: 28.2 us -> 0 us
  starting transfers between devices: 19.8 us -> 31.6 us
  waiting for transfers between devices: 4.21 us -> 10.9 us
  Pallas kernels: 45.1 us -> 49.4 us
    all_to_all x2 -> x0, blocking collectives: 28.2 us -> none  [the longest x1 16 us: block_body(): arrived = lax.all_to_all(terms, 'shard', 0, 0)]
    ppermute x16 -> x25, starting transfers between devices: 19.8 us -> 31.6 us  [sent(): lax.ppermute(array, 'shard', [(i, i ^ distance) for i in range(size)])]
    ppermute x16 -> x25, waiting for transfers between devices: 4.21 us -> 10.9 us  [sent(): lax.ppermute(array, 'shard', [(i, i ^ distance) for i in range(size)])]
    pallas_call x13 -> x21, Pallas kernels: 40.3 us -> 45 us  [the longest x5 19.4 us: fetched(): pl.pallas_call(functools.partial(fetch_kernel, [part[1:] for part in part...]
  transfers between devices with their start and end apart: 16 -> 25, of which waited for: 5 -> 10; matrix products, arithmetic and copies ran while one was open for 2% -> 2% of each run, Pallas kernels for 29% -> 39%
where the time goes in v3:
time: 94.1 us; the launch traced here: 93.8 us
  Pallas kernels  49.4 us (52%)
  starting transfers between devices  31.6 us (34%)
  waiting for transfers between devices  10.9 us (12%)
    ppermute x25, starting transfers between devices, sent(): lax.ppermute(array, 'shard', [(i, i ^ distance) for i in range(size)])  31.6 us
    pallas_call x5, Pallas kernels, fetched(): pl.pallas_call(functools.partial(fetch_kernel, [part[1:] for part in part...  19.4 us
    ppermute x25, waiting for transfers between devices, sent(): lax.ppermute(array, 'shard', [(i, i ^ distance) for i in range(size)])  10.9 us
    pallas_call x3, Pallas kernels, feed(): pl.pallas_call(functools.partial(feed_kernel, entries, len(pieces), held)...  9.81 us
    pallas_call x1, Pallas kernels, hidden_units(): pl.pallas_call(functools.partial(hidden_kernel, entries, [len(parts) for...  8.77 us
    pallas_call x1, Pallas kernels, readied(): pl.pallas_call(ready_kernel, in_specs=[SMEM_SPEC, VMEM_SPEC] + [HBM_SPEC]...  3.53 us
    pallas_call x2, Pallas kernels, down_terms(): pl.pallas_call(functools.partial(down_kernel, choice), in_specs=[VMEM_SPE...  2.5 us
  transfers between devices with their start and end apart: 25, of which 10 were waited for; matrix products, arithmetic and copies ran while one was open for 2% of the time, Pallas kernels for 39%

profile of v3, /device:TPU:0, one launch (start us, length us, event | category | flops | bytes accessed | tf_op | source)
XLA Modules:
  0.0 93.8 jit_solution(5851723161426313832)
XLA Ops:
  0.8 5.1 %collective-permute-start.2 = (bf16[144,128]{1,0:T(8,128)(2,1)S(1)}, bf16[144,128]{1,0:T(8,128)(2,1)S(1)}, u32[]{:S(2)}, u32[]{:S(2)}) collective-permute-start(bf16[144,128]{1,0:T(8,128)(2,1)S(1)} %get-tuple-element.39.refs_0_), channel_id=1, source_target_pairs={{0,12},{1,13},{2,14},{3,15},{4,8},{5,9},{6,10},{7,11},{8,4},{9,5},... | collective-permute-start | bytes 110600 | tf_op jit(solution)/shard_map/ppermute | solution.py:157
  8.2 3.5 %shard_map.110 = (bf16[16,2,32,512]{3,2,1,0:T(8,128)(2,1)S(1)}, s32[16,128]{1,0:T(8,128)S(1)}, s32[32,128]{1,0:T(8,128)S(1)}, f32[2,128,128]{2,1,0:T(8,128)S(1)}) custom-call(s32[289]{0:T(512)S(1)} %pad_add_fusion.table_ref, bf16[128,128]{1,0:T(8,128)(2,1)S(1)} %get-tuple-element.36.query_ref, bf16[16,2,32,512]{3,2,1,0:T(8,128)(2,1)} %pages_hbm.1, ...), custom_call_target="tpu_custom_call" | custom-call | flops 4194304 | bytes 2097152 | tf_op jit(solution)/shard_map/pallas_call | solution.py:319
  11.8 1.7 %collective-permute-start.3 = (bf16[4,144,128]{2,1,0:T(8,128)(2,1)S(1)}, bf16[4,144,128]{2,1,0:T(8,128)(2,1)S(1)}, u32[]{:S(2)}, u32[]{:S(2)}) collective-permute-start(bf16[4,144,128]{2,1,0:T(8,128)(2,1)S(1)} %shard_map.111.refs_0_.after_ref.refs_1_.refs_3_), channel_id=1, source_target_pairs={{0,2},{1,3},{2,0},{3,1},{4,6},{5,7},{6,4},{7,5},{8,10},{9,11},{10,... | collective-permute-start | bytes 442376 | tf_op jit(solution)/shard_map/ppermute | solution.py:157
  13.5 3.5 %shard_map.113.refs_2_ = bf16[5,512,1664]{2,1,0:T(8,128)(2,1)S(1)} custom-call(bf16[4,144,128]{2,1,0:T(8,128)(2,1)S(1)} %shard_map.111.refs_0_.after_ref.refs_1_.refs_3_, bf16[8192,1664]{1,0:T(8,128)(2,1)} %refs_6_.1), custom_call_target="tpu_custom_call" | custom-call | bytes 8519680 | tf_op jit(solution)/shard_map/pallas_call | solution.py:517
  20.8 1.7 %collective-permute-start.6 = (bf16[4,2,72,128]{3,2,1,0:T(8,128)(2,1)S(1)}, bf16[4,2,72,128]{3,2,1,0:T(8,128)(2,1)S(1)}, u32[]{:S(2)}, u32[]{:S(2)}) collective-permute-start(bf16[4,2,72,128]{3,2,1,0:T(8,128)(2,1)S(1)} %shard_map.117.after_ref), channel_id=1, source_target_pairs={{0,2},{1,3},{2,0},{3,1},{4,6},{5,7},{6,4},{7,5},{8,10},{9,11},{10,... | collective-permute-start | bytes 442376 | tf_op jit(solution)/shard_map/ppermute | solution.py:157
  22.5 4.0 %shard_map.118 = (bf16[4,512,1664]{2,1,0:T(8,128)(2,1)S(1)}, bf16[2,512,1664]{2,1,0:T(8,128)(2,1)S(1)}) custom-call(bf16[4,2,72,128]{3,2,1,0:T(8,128)(2,1)S(1)} %shard_map.117.after_ref, bf16[8192,1664]{1,0:T(8,128)(2,1)} %refs_6_.1, bf16[8192,1664]{1,0:T(8,128)(2,1)} %refs_7_.1), custom_call_target="tpu_custom_call" | custom-call | bytes 10223616 | tf_op jit(solution)/shard_map/pallas_call | solution.py:517
  26.9 3.7 %collective-permute-start.7 = (bf16[2,72,128]{2,1,0:T(8,128)(2,1)S(1)}, bf16[2,72,128]{2,1,0:T(8,128)(2,1)S(1)}, u32[]{:S(2)}, u32[]{:S(2)}) collective-permute-start(bf16[2,72,128]{2,1,0:T(8,128)(2,1)S(1)} %get-tuple-element.43), channel_id=1, source_target_pairs={{0,12},{1,13},{2,14},{3,15},{4,8},{5,9},{6,10},{7,11},{8,4},{9,5},... | collective-permute-start | bytes 110600 | tf_op jit(solution)/shard_map/ppermute | solution.py:157
  31.4 4.0 %shard_map.120 = (bf16[4,512,1664]{2,1,0:T(8,128)(2,1)S(1)}, bf16[2,512,1664]{2,1,0:T(8,128)(2,1)S(1)}) custom-call(bf16[2,72,128]{2,1,0:T(8,128)(2,1)S(1)} %get-tuple-element.46.after_ref.refs_3_, bf16[8192,1664]{1,0:T(8,128)(2,1)} %refs_7_.1, bf16[8192,1664]{1,0:T(8,128)(2,1)} %refs_7_.1), custom_call_target="tpu_custom_call" | custom-call | bytes 10223616 | tf_op jit(solution)/shard_map/pallas_call | solution.py:517
  35.8 3.6 %collective-permute-start.12 = (bf16[128,128]{1,0:T(8,128)(2,1)S(1)}, bf16[128,128]{1,0:T(8,128)(2,1)S(1)}, u32[]{:S(2)}, u32[]{:S(2)}) collective-permute-start(bf16[128,128]{1,0:T(8,128)(2,1)S(1)} %shard_map.121.after_ref.refs_0_), channel_id=1, source_target_pairs={{0,12},{1,13},{2,14},{3,15},{4,8},{5,9},{6,10},{7,11},{8,4},{9,5},... | collective-permute-start | bytes 98312 | tf_op jit(solution)/shard_map/ppermute | solution.py:157
  40.3 3.1 %shard_map.122 = (bf16[2,1664,512]{2,1,0:T(8,128)(2,1)S(1)}, bf16[2,512,1664]{2,1,0:T(8,128)(2,1)S(1)}) custom-call(bf16[128,128]{1,0:T(8,128)(2,1)S(1)} %shard_map.121.after_ref.refs_0_, bf16[1664,8192]{1,0:T(8,128)(2,1)} %refs_8_.1, bf16[8192,1664]{1,0:T(8,128)(2,1)} %refs_7_.1), custom_call_target="tpu_custom_call" | custom-call | bytes 6815744 | tf_op jit(solution)/shard_map/pallas_call | solution.py:517
  44.3 1.6 %collective-permute-start.13 = (bf16[4,128,128]{2,1,0:T(8,128)(2,1)S(1)}, bf16[4,128,128]{2,1,0:T(8,128)(2,1)S(1)}, u32[]{:S(2)}, u32[]{:S(2)}) collective-permute-start(bf16[4,128,128]{2,1,0:T(8,128)(2,1)S(1)} %shard_map.123.after_ref.refs_0_.near_ref), channel_id=1, source_target_pairs={{0,2},{1,3},{2,0},{3,1},{4,6},{5,7},{6,4},{7,5},{8,10},{9,11},{10,... | collective-permute-start | bytes 393224 | tf_op jit(solution)/shard_map/ppermute | solution.py:157
  45.9 4.8 %shard_map.124.refs_2_.refs_0_.refs_1_ = bf16[6,1664,512]{2,1,0:T(8,128)(2,1)S(1)} custom-call(bf16[4,128,128]{2,1,0:T(8,128)(2,1)S(1)} %shard_map.123.after_ref.refs_0_.near_ref, bf16[1664,8192]{1,0:T(8,128)(2,1)} %refs_8_.1), custom_call_target="tpu_custom_call" | custom-call | bytes 10223616 | tf_op jit(solution)/shard_map/pallas_call | solution.py:517
  50.8 1.5 %collective-permute-done.14.odd_ref = bf16[8,128,128]{2,1,0:T(8,128)(2,1)S(1)} collective-permute-done((bf16[8,128,128]{2,1,0:T(8,128)(2,1)S(1)}, bf16[8,128,128]{2,1,0:T(8,128)(2,1)S(1)}, u32[]{:S(2)}, u32[]{:S(2)}) %collective-permute-start.14) | collective-permute-done | bytes 262176 | tf_op jit(solution)/shard_map/ppermute | solution.py:157
  52.4 1.7 %shard_map.126.refs_0_.stream_ref = bf16[32,512]{1,0:T(8,128)(2,1)S(1)} custom-call(bf16[4,128,128]{2,1,0:T(8,128)(2,1)S(1)} %shard_map.123.after_ref.refs_0_.near_ref, bf16[4,128,128]{2,1,0:T(8,128)(2,1)S(1)} %collective-permute-done.13.refs_1_.second_ref, bf16[8,128,128]{2,1,0:T(8,128)(2,1)S(1)} %collective-permute-done.14.odd_ref, ...), custom_call_target="tpu_custom_call" | custom-call | flops 268435456 | bytes 8388608 | tf_op jit(solution)/shard_map/pallas_call | solution.py:576
  54.1 2.7 %collective-permute-start.17 = (bf16[32,512]{1,0:T(8,128)(2,1)S(1)}, bf16[32,512]{1,0:T(8,128)(2,1)S(1)}, u32[]{:S(2)}, u32[]{:S(2)}) collective-permute-start(bf16[32,512]{1,0:T(8,128)(2,1)S(1)} %shard_map.126.refs_0_.stream_ref), channel_id=1, source_target_pairs={{0,12},{1,13},{2,14},{3,15},{4,8},{5,9},{6,10},{7,11},{8,4},{9,5},... | collective-permute-start | bytes 98312 | tf_op jit(solution)/shard_map/ppermute | solution.py:157
  56.8 1.7 %collective-permute-start.15 = (bf16[32,512]{1,0:T(8,128)(2,1)S(1)}, bf16[32,512]{1,0:T(8,128)(2,1)S(1)}, u32[]{:S(2)}, u32[]{:S(2)}) collective-permute-start(bf16[32,512]{1,0:T(8,128)(2,1)S(1)} %shard_map.126.refs_0_.stream_ref), channel_id=1, source_target_pairs={{0,4},{1,5},{2,6},{3,7},{4,0},{5,1},{6,2},{7,3},{8,12},{9,13},{10,... | collective-permute-start | bytes 98312 | tf_op jit(solution)/shard_map/ppermute | solution.py:157
  58.5 2.4 %shard_map.127 = (f32[32,1664]{1,0:T(8,128)S(1)}, f32[32,1664]{1,0:T(8,128)S(1)}, f32[32,512]{1,0:T(8,128)S(1)}) custom-call(bf16[32,512]{1,0:T(8,128)(2,1)S(1)} %shard_map.126.refs_0_.stream_ref, bf16[4,144,128]{2,1,0:T(8,128)(2,1)S(1)} %shard_map.111.refs_0_.after_ref.refs_1_.refs_3_, bf16[8192,1664]{1,0:T(8,128)(2,1)} %refs_6_.1, bf16[8192,1664]{1,0:T(8,128)(2,1)} %refs_7_.1), custom_call_target="tpu_custom_call" | custom-call | flops 109051904 | bytes 3407872 | tf_op jit(solution)/shard_map/pallas_call | solution.py:654
  61.8 5.0 %shard_map.129 = (f32[32,1664]{1,0:T(8,128)S(1)}, f32[32,1664]{1,0:T(8,128)S(1)}, f32[32,512]{1,0:T(8,128)S(1)}) custom-call(bf16[32,512]{1,0:T(8,128)(2,1)S(1)} %collective-permute-done.15.refs_1_.refs_0_, bf16[32,512]{1,0:T(8,128)(2,1)S(1)} %collective-permute-done.16.refs_2_.refs_1_, bf16[32,512]{1,0:T(8,128)(2,1)S(1)} %collective-permute-done.17.refs_3_.refs_2_, ...), custom_call_target="tpu_custom_call" | custom-call | flops 327155712 | bytes 10223616 | tf_op jit(solution)/shard_map/pallas_call | solution.py:654
  66.9 2.4 %shard_map.131 = (f32[32,1664]{1,0:T(8,128)S(1)}, f32[32,1664]{1,0:T(8,128)S(1)}, f32[32,512]{1,0:T(8,128)S(1)}) custom-call(bf16[4,32,512]{2,1,0:T(8,128)(2,1)S(1)} %collective-permute-done.18.refs_1_.refs_0_, bf16[4,144,128]{2,1,0:T(8,128)(2,1)S(1)} %collective-permute-done.3.refs_1_, bf16[4,512,1664]{2,1,0:T(8,128)(2,1)S(1)} %get-tuple-element.42.unused_ref.refs_2_, ...), custom_call_target="tpu_custom_call" | custom-call | flops 436207616 | bytes 13631488 | tf_op jit(solution)/shard_map/pallas_call | solution.py:654
  69.3 8.8 %shard_map.132 = (bf16[32,1664]{1,0:T(8,128)(2,1)S(1)}, bf16[8,32,512]{2,1,0:T(8,128)(2,1)S(1)}) custom-call(bf16[8,32,512]{2,1,0:T(8,128)(2,1)S(1)} %collective-permute-done.19.refs_0_, bf16[8,144,128]{2,1,0:T(8,128)(2,1)S(1)} %collective-permute-done.4.refs_0_.refs_1_, bf16[5,512,1664]{2,1,0:T(8,128)(2,1)S(1)} %shard_map.113.refs_2_, ...), custom_call_target="tpu_custom_call" | custom-call | flops 1308622848 | bytes 40894464 | tf_op jit(solution)/shard_map/pallas_call | solution.py:735
  80.0 2.0 %collective-permute-start.21 = (bf16[4,32,512]{2,1,0:T(8,128)(2,1)S(1)}, bf16[4,32,512]{2,1,0:T(8,128)(2,1)S(1)}, u32[]{:S(2)}, u32[]{:S(2)}) collective-permute-start(bf16[4,32,512]{2,1,0:T(8,128)(2,1)S(1)} %shard_map.135), channel_id=1, source_target_pairs={{0,2},{1,3},{2,0},{3,1},{4,6},{5,7},{6,4},{7,5},{8,10},{9,11},{10,... | collective-permute-start | bytes 393224 | tf_op jit(solution)/shard_map/ppermute | solution.py:157
  83.2 2.7 %collective-permute-done.21.arrived_ref = bf16[4,32,512]{2,1,0:T(8,128)(2,1)S(1)} collective-permute-done((bf16[4,32,512]{2,1,0:T(8,128)(2,1)S(1)}, bf16[4,32,512]{2,1,0:T(8,128)(2,1)S(1)}, u32[]{:S(2)}, u32[]{:S(2)}) %collective-permute-start.21) | collective-permute-done | bytes 131104 | tf_op jit(solution)/shard_map/ppermute | solution.py:157
  85.9 2.1 %collective-permute-start.22 = (bf16[32,512]{1,0:T(8,128)(2,1)S(1)}, bf16[32,512]{1,0:T(8,128)(2,1)S(1)}, u32[]{:S(2)}, u32[]{:S(2)}) collective-permute-start(bf16[32,512]{1,0:T(8,128)(2,1)S(1)} %get-tuple-element.63), channel_id=1, source_target_pairs={{0,12},{1,13},{2,14},{3,15},{4,8},{5,9},{6,10},{7,11},{8,4},{9,5},... | collective-permute-start | bytes 98312 | tf_op jit(solution)/shard_map/ppermute | solution.py:157
  88.3 2.1 %collective-permute-start.24 = (bf16[32,512]{1,0:T(8,128)(2,1)S(1)}, bf16[32,512]{1,0:T(8,128)(2,1)S(1)}, u32[]{:S(2)}, u32[]{:S(2)}) collective-permute-start(bf16[32,512]{1,0:T(8,128)(2,1)S(1)} %get-tuple-element.65), channel_id=1, source_target_pairs={{0,4},{1,5},{2,6},{3,7},{4,0},{5,1},{6,2},{7,3},{8,12},{9,13},{10,... | collective-permute-start | bytes 98312 | tf_op jit(solution)/shard_map/ppermute | solution.py:157
  (65 shorter events, 18.1 us)
Async XLA Ops:
  0.8 10.9 %collective-permute-start.2 = (bf16[144,128]{1,0:T(8,128)(2,1)S(1)}, bf16[144,128]{1,0:T(8,128)(2,1)S(1)}, u32[]{:S(2)}, u32[]{:S(2)}) collective-permute-start(bf16[144,128]{1,0:T(8,128)(2,1)S(1)} %get-tuple-element.39.refs_0_), channel_id=1, source_target_pairs={{0,12},{1,13},{2,14},{3,15},{4,8},{5,9},{6,10},{7,11},{8,4},{9,5},... | collective-permute-start | bytes 110600 | tf_op jit(solution)/shard_map/ppermute | solution.py:157
  6.0 5.8 %collective-permute-start.1 = (bf16[144,128]{1,0:T(8,128)(2,1)S(1)}, bf16[144,128]{1,0:T(8,128)(2,1)S(1)}, u32[]{:S(2)}, u32[]{:S(2)}) collective-permute-start(bf16[144,128]{1,0:T(8,128)(2,1)S(1)} %get-tuple-element.39.refs_0_), channel_id=1, source_target_pairs={{0,8},{1,9},{2,10},{3,11},{4,12},{5,13},{6,14},{7,15},{8,0},{9,1},... | collective-permute-start | bytes 110600 | tf_op jit(solution)/shard_map/ppermute | solution.py:157
  6.0 5.8 %collective-permute-start = (bf16[144,128]{1,0:T(8,128)(2,1)S(1)}, bf16[144,128]{1,0:T(8,128)(2,1)S(1)}, u32[]{:S(2)}, u32[]{:S(2)}) collective-permute-start(bf16[144,128]{1,0:T(8,128)(2,1)S(1)} %get-tuple-element.39.refs_0_), channel_id=1, source_target_pairs={{0,4},{1,5},{2,6},{3,7},{4,0},{5,1},{6,2},{7,3},{8,12},{9,13},{10,... | collective-permute-start | bytes 110600 | tf_op jit(solution)/shard_map/ppermute | solution.py:157
  11.8 5.3 %collective-permute-start.3 = (bf16[4,144,128]{2,1,0:T(8,128)(2,1)S(1)}, bf16[4,144,128]{2,1,0:T(8,128)(2,1)S(1)}, u32[]{:S(2)}, u32[]{:S(2)}) collective-permute-start(bf16[4,144,128]{2,1,0:T(8,128)(2,1)S(1)} %shard_map.111.refs_0_.after_ref.refs_1_.refs_3_), channel_id=1, source_target_pairs={{0,2},{1,3},{2,0},{3,1},{4,6},{5,7},{6,4},{7,5},{8,10},{9,11},{10,... | collective-permute-start | bytes 442376 | tf_op jit(solution)/shard_map/ppermute | solution.py:157
  17.1 1.6 %collective-permute-start.4 = (bf16[8,144,128]{2,1,0:T(8,128)(2,1)S(1)}, bf16[8,144,128]{2,1,0:T(8,128)(2,1)S(1)}, u32[]{:S(2)}, u32[]{:S(2)}) collective-permute-start(bf16[8,144,128]{2,1,0:T(8,128)(2,1)S(1)} %shard_map.114), channel_id=1, source_target_pairs={{0,1},{1,0},{2,3},{3,2},{4,5},{5,4},{6,7},{7,6},{8,9},{9,8},{10,11... | collective-permute-start | bytes 884744 | tf_op jit(solution)/shard_map/ppermute | solution.py:157
  20.8 6.0 %collective-permute-start.6 = (bf16[4,2,72,128]{3,2,1,0:T(8,128)(2,1)S(1)}, bf16[4,2,72,128]{3,2,1,0:T(8,128)(2,1)S(1)}, u32[]{:S(2)}, u32[]{:S(2)}) collective-permute-start(bf16[4,2,72,128]{3,2,1,0:T(8,128)(2,1)S(1)} %shard_map.117.after_ref), channel_id=1, source_target_pairs={{0,2},{1,3},{2,0},{3,1},{4,6},{5,7},{6,4},{7,5},{8,10},{9,11},{10,... | collective-permute-start | bytes 442376 | tf_op jit(solution)/shard_map/ppermute | solution.py:157
  26.9 8.5 %collective-permute-start.7 = (bf16[2,72,128]{2,1,0:T(8,128)(2,1)S(1)}, bf16[2,72,128]{2,1,0:T(8,128)(2,1)S(1)}, u32[]{:S(2)}, u32[]{:S(2)}) collective-permute-start(bf16[2,72,128]{2,1,0:T(8,128)(2,1)S(1)} %get-tuple-element.43), channel_id=1, source_target_pairs={{0,12},{1,13},{2,14},{3,15},{4,8},{5,9},{6,10},{7,11},{8,4},{9,5},... | collective-permute-start | bytes 110600 | tf_op jit(solution)/shard_map/ppermute | solution.py:157
  30.7 4.9 %collective-permute-start.8 = (bf16[2,72,128]{2,1,0:T(8,128)(2,1)S(1)}, bf16[2,72,128]{2,1,0:T(8,128)(2,1)S(1)}, u32[]{:S(2)}, u32[]{:S(2)}) collective-permute-start(bf16[2,72,128]{2,1,0:T(8,128)(2,1)S(1)} %get-tuple-element.44), channel_id=1, source_target_pairs={{0,8},{1,9},{2,10},{3,11},{4,12},{5,13},{6,14},{7,15},{8,0},{9,1},... | collective-permute-start | bytes 110600 | tf_op jit(solution)/shard_map/ppermute | solution.py:157
  30.7 4.9 %collective-permute-start.9 = (bf16[2,72,128]{2,1,0:T(8,128)(2,1)S(1)}, bf16[2,72,128]{2,1,0:T(8,128)(2,1)S(1)}, u32[]{:S(2)}, u32[]{:S(2)}) collective-permute-start(bf16[2,72,128]{2,1,0:T(8,128)(2,1)S(1)} %get-tuple-element.45), channel_id=1, source_target_pairs={{0,4},{1,5},{2,6},{3,7},{4,0},{5,1},{6,2},{7,3},{8,12},{9,13},{10,... | collective-permute-start | bytes 110600 | tf_op jit(solution)/shard_map/ppermute | solution.py:157
  35.8 7.5 %collective-permute-start.12 = (bf16[128,128]{1,0:T(8,128)(2,1)S(1)}, bf16[128,128]{1,0:T(8,128)(2,1)S(1)}, u32[]{:S(2)}, u32[]{:S(2)}) collective-permute-start(bf16[128,128]{1,0:T(8,128)(2,1)S(1)} %shard_map.121.after_ref.refs_0_), channel_id=1, source_target_pairs={{0,12},{1,13},{2,14},{3,15},{4,8},{5,9},{6,10},{7,11},{8,4},{9,5},... | collective-permute-start | bytes 98312 | tf_op jit(solution)/shard_map/ppermute | solution.py:157
  39.4 4.8 %collective-permute-start.11 = (bf16[128,128]{1,0:T(8,128)(2,1)S(1)}, bf16[128,128]{1,0:T(8,128)(2,1)S(1)}, u32[]{:S(2)}, u32[]{:S(2)}) collective-permute-start(bf16[128,128]{1,0:T(8,128)(2,1)S(1)} %shard_map.121.after_ref.refs_0_), channel_id=1, source_target_pairs={{0,8},{1,9},{2,10},{3,11},{4,12},{5,13},{6,14},{7,15},{8,0},{9,1},... | collective-permute-start | bytes 98312 | tf_op jit(solution)/shard_map/ppermute | solution.py:157
  39.5 4.8 %collective-permute-start.10 = (bf16[128,128]{1,0:T(8,128)(2,1)S(1)}, bf16[128,128]{1,0:T(8,128)(2,1)S(1)}, u32[]{:S(2)}, u32[]{:S(2)}) collective-permute-start(bf16[128,128]{1,0:T(8,128)(2,1)S(1)} %shard_map.121.after_ref.refs_0_), channel_id=1, source_target_pairs={{0,4},{1,5},{2,6},{3,7},{4,0},{5,1},{6,2},{7,3},{8,12},{9,13},{10,... | collective-permute-start | bytes 98312 | tf_op jit(solution)/shard_map/ppermute | solution.py:157
  44.3 6.4 %collective-permute-start.13 = (bf16[4,128,128]{2,1,0:T(8,128)(2,1)S(1)}, bf16[4,128,128]{2,1,0:T(8,128)(2,1)S(1)}, u32[]{:S(2)}, u32[]{:S(2)}) collective-permute-start(bf16[4,128,128]{2,1,0:T(8,128)(2,1)S(1)} %shard_map.123.after_ref.refs_0_.near_ref), channel_id=1, source_target_pairs={{0,2},{1,3},{2,0},{3,1},{4,6},{5,7},{6,4},{7,5},{8,10},{9,11},{10,... | collective-permute-start | bytes 393224 | tf_op jit(solution)/shard_map/ppermute | solution.py:157
  50.7 1.6 %collective-permute-start.14 = (bf16[8,128,128]{2,1,0:T(8,128)(2,1)S(1)}, bf16[8,128,128]{2,1,0:T(8,128)(2,1)S(1)}, u32[]{:S(2)}, u32[]{:S(2)}) collective-permute-start(bf16[8,128,128]{2,1,0:T(8,128)(2,1)S(1)} %shard_map.125), channel_id=1, source_target_pairs={{0,1},{1,0},{2,3},{3,2},{4,5},{5,4},{6,7},{7,6},{8,9},{9,8},{10,11... | collective-permute-start | bytes 786440 | tf_op jit(solution)/shard_map/ppermute | solution.py:157
  54.1 6.8 %collective-permute-start.17 = (bf16[32,512]{1,0:T(8,128)(2,1)S(1)}, bf16[32,512]{1,0:T(8,128)(2,1)S(1)}, u32[]{:S(2)}, u32[]{:S(2)}) collective-permute-start(bf16[32,512]{1,0:T(8,128)(2,1)S(1)} %shard_map.126.refs_0_.stream_ref), channel_id=1, source_target_pairs={{0,12},{1,13},{2,14},{3,15},{4,8},{5,9},{6,10},{7,11},{8,4},{9,5},... | collective-permute-start | bytes 98312 | tf_op jit(solution)/shard_map/ppermute | solution.py:157
  56.8 4.8 %collective-permute-start.16 = (bf16[32,512]{1,0:T(8,128)(2,1)S(1)}, bf16[32,512]{1,0:T(8,128)(2,1)S(1)}, u32[]{:S(2)}, u32[]{:S(2)}) collective-permute-start(bf16[32,512]{1,0:T(8,128)(2,1)S(1)} %shard_map.126.refs_0_.stream_ref), channel_id=1, source_target_pairs={{0,8},{1,9},{2,10},{3,11},{4,12},{5,13},{6,14},{7,15},{8,0},{9,1},... | collective-permute-start | bytes 98312 | tf_op jit(solution)/shard_map/ppermute | solution.py:157
  56.8 4.8 %collective-permute-start.15 = (bf16[32,512]{1,0:T(8,128)(2,1)S(1)}, bf16[32,512]{1,0:T(8,128)(2,1)S(1)}, u32[]{:S(2)}, u32[]{:S(2)}) collective-permute-start(bf16[32,512]{1,0:T(8,128)(2,1)S(1)} %shard_map.126.refs_0_.stream_ref), channel_id=1, source_target_pairs={{0,4},{1,5},{2,6},{3,7},{4,0},{5,1},{6,2},{7,3},{8,12},{9,13},{10,... | collective-permute-start | bytes 98312 | tf_op jit(solution)/shard_map/ppermute | solution.py:157
  61.6 5.2 %collective-permute-start.18 = (bf16[4,32,512]{2,1,0:T(8,128)(2,1)S(1)}, bf16[4,32,512]{2,1,0:T(8,128)(2,1)S(1)}, u32[]{:S(2)}, u32[]{:S(2)}) collective-permute-start(bf16[4,32,512]{2,1,0:T(8,128)(2,1)S(1)} %shard_map.128.refs_0_), channel_id=1, source_target_pairs={{0,2},{1,3},{2,0},{3,1},{4,6},{5,7},{6,4},{7,5},{8,10},{9,11},{10,... | collective-permute-start | bytes 393224 | tf_op jit(solution)/shard_map/ppermute | solution.py:157
  66.8 2.5 %collective-permute-start.19 = (bf16[8,32,512]{2,1,0:T(8,128)(2,1)S(1)}, bf16[8,32,512]{2,1,0:T(8,128)(2,1)S(1)}, u32[]{:S(2)}, u32[]{:S(2)}) collective-permute-start(bf16[8,32,512]{2,1,0:T(8,128)(2,1)S(1)} %shard_map.130), channel_id=1, source_target_pairs={{0,1},{1,0},{2,3},{3,2},{4,5},{5,4},{6,7},{7,6},{8,9},{9,8},{10,11... | collective-permute-start | bytes 786440 | tf_op jit(solution)/shard_map/ppermute | solution.py:157
  78.1 1.8 %collective-permute-start.20 = (bf16[8,32,512]{2,1,0:T(8,128)(2,1)S(1)}, bf16[8,32,512]{2,1,0:T(8,128)(2,1)S(1)}, u32[]{:S(2)}, u32[]{:S(2)}) collective-permute-start(bf16[8,32,512]{2,1,0:T(8,128)(2,1)S(1)} %get-tuple-element.62), channel_id=1, source_target_pairs={{0,1},{1,0},{2,3},{3,2},{4,5},{5,4},{6,7},{7,6},{8,9},{9,8},{10,11... | collective-permute-start | bytes 786440 | tf_op jit(solution)/shard_map/ppermute | solution.py:157
  80.0 5.9 %collective-permute-start.21 = (bf16[4,32,512]{2,1,0:T(8,128)(2,1)S(1)}, bf16[4,32,512]{2,1,0:T(8,128)(2,1)S(1)}, u32[]{:S(2)}, u32[]{:S(2)}) collective-permute-start(bf16[4,32,512]{2,1,0:T(8,128)(2,1)S(1)} %shard_map.135), channel_id=1, source_target_pairs={{0,2},{1,3},{2,0},{3,1},{4,6},{5,7},{6,4},{7,5},{8,10},{9,11},{10,... | collective-permute-start | bytes 393224 | tf_op jit(solution)/shard_map/ppermute | solution.py:157
  85.9 5.8 %collective-permute-start.22 = (bf16[32,512]{1,0:T(8,128)(2,1)S(1)}, bf16[32,512]{1,0:T(8,128)(2,1)S(1)}, u32[]{:S(2)}, u32[]{:S(2)}) collective-permute-start(bf16[32,512]{1,0:T(8,128)(2,1)S(1)} %get-tuple-element.63), channel_id=1, source_target_pairs={{0,12},{1,13},{2,14},{3,15},{4,8},{5,9},{6,10},{7,11},{8,4},{9,5},... | collective-permute-start | bytes 98312 | tf_op jit(solution)/shard_map/ppermute | solution.py:157
  88.0 5.2 %collective-permute-start.23 = (bf16[32,512]{1,0:T(8,128)(2,1)S(1)}, bf16[32,512]{1,0:T(8,128)(2,1)S(1)}, u32[]{:S(2)}, u32[]{:S(2)}) collective-permute-start(bf16[32,512]{1,0:T(8,128)(2,1)S(1)} %get-tuple-element.64), channel_id=1, source_target_pairs={{0,8},{1,9},{2,10},{3,11},{4,12},{5,13},{6,14},{7,15},{8,0},{9,1},... | collective-permute-start | bytes 98312 | tf_op jit(solution)/shard_map/ppermute | solution.py:157
  88.3 4.9 %collective-permute-start.24 = (bf16[32,512]{1,0:T(8,128)(2,1)S(1)}, bf16[32,512]{1,0:T(8,128)(2,1)S(1)}, u32[]{:S(2)}, u32[]{:S(2)}) collective-permute-start(bf16[32,512]{1,0:T(8,128)(2,1)S(1)} %get-tuple-element.65), channel_id=1, source_target_pairs={{0,4},{1,5},{2,6},{3,7},{4,0},{5,1},{6,2},{7,3},{8,12},{9,13},{10,... | collective-permute-start | bytes 98312 | tf_op jit(solution)/shard_map/ppermute | solution.py:157
  (4 other events, 19.2 us)

commit v4 on v3

--- a/solution.py
+++ b/solution.py
@@ -144,7 +144,7 @@
 
 
 GROUP = HEADS // KV_HEADS
-HEAD_ROWS = 72
+TAIL = 16
 MIB = 2**20
 VMEM_SPEC = pl.BlockSpec(memory_space=pltpu.VMEM)
 SMEM_SPEC = pl.BlockSpec(memory_space=pltpu.SMEM)
@@ -185,9 +185,10 @@
     return me ^ (entry % 4 * 4 + entry // 4 % 2 * 2 + entry // 8)
 
 
-def started(count, copy_at):
+def started(count, *copies):
     def start(place, carry):
-        copy_at(place).start()
+        for copy_at in copies:
+            copy_at(place).start()
         return carry
 
     lax.fori_loop(0, count, start, 0)
@@ -268,7 +269,7 @@
     return jnp.concatenate(numerators), jnp.concatenate(denominators)
 
 
-def ready_kernel(table_ref, query_ref, pages_hbm, new_hbm, pages, left_ref, second_ref, new_ref, new, sems):
+def ready_kernel(table_ref, query_ref, pages_hbm, new_hbm, after_ref, pages, left_ref, second_ref, new_ref, lower_ref, new, sems):
     _, _, page_len, features = pages.shape
     count = pages_hbm.shape[0]
     sequences = 2 * 16
@@ -309,27 +310,29 @@
             jnp.broadcast_to(new[row, 1:2, :], (8, features)),
             first_token,
         )
-        new_ref[0, lines, :] = numerator
-        new_ref[1, lines, :] = jnp.broadcast_to(total, (HEADS, HEAD_DIM))
+        new_ref[lines, :] = numerator
+        lower = jnp.swapaxes(jnp.broadcast_to(total, (HEADS, HEAD_DIM)), 0, 1)
+        lower_ref[8 * row : 8 * (row + 1), :] = lower[:8]
     for entry in range(16):
         page_copy(0, entry).wait()
 
 
-def readied(table, query_rows, kv_pages, new_kv):
+def readied(table, query_rows, kv_pages, new_kv, after):
     return pl.pallas_call(
         ready_kernel,
-        in_specs=[SMEM_SPEC, VMEM_SPEC] + [HBM_SPEC] * 2,
-        out_specs=[VMEM_SPEC] * 4,
+        in_specs=[SMEM_SPEC, VMEM_SPEC] + [HBM_SPEC] * 2 + [pl.BlockSpec(memory_space=pl.ANY)],
+        out_specs=[VMEM_SPEC] * 5,
         out_shape=[
             pltpu.VMEM(kv_pages.shape, kv_pages.dtype),
             jax.ShapeDtypeStruct((16, HEAD_DIM), jnp.int32),
             jax.ShapeDtypeStruct((32, HEAD_DIM), jnp.int32),
-            jax.ShapeDtypeStruct((2, 2 * HEADS, HEAD_DIM), jnp.float32),
+            jax.ShapeDtypeStruct((2 * HEADS, HEAD_DIM), jnp.float32),
+            jax.ShapeDtypeStruct((16, HEADS), jnp.float32),
         ],
         scratch_shapes=[pltpu.VMEM(new_kv.shape, jnp.bfloat16), pltpu.SemaphoreType.DMA((17,))],
         compiler_params=pltpu.CompilerParams(vmem_limit_bytes=4 * MIB),
         cost_estimate=pl.CostEstimate(flops=2**22, bytes_accessed=2**21, transcendentals=2**11),
-    )(table, query_rows, in_hbm(kv_pages), in_hbm(new_kv))
+    )(table, query_rows, in_hbm(kv_pages), in_hbm(new_kv), after)
 
 
 def pages_kernel(entries, left_ref, second_ref, *refs):
@@ -369,16 +372,24 @@
         )
         for head in range(KV_HEADS):
             lines = slice(head * GROUP, (head + 1) * GROUP)
-            out_ref[here, lines, :] = numerator[
+            out_ref[here * HEADS + head * GROUP : here * HEADS + (head + 1) * GROUP, :] = numerator[
                 lines, head * HEAD_DIM : (head + 1) * HEAD_DIM
             ].astype(jnp.bfloat16)
-    high, low = two_terms(jnp.swapaxes(denominators, 0, 1)[: len(entries)])
-    lasts = jnp.concatenate([high, low], axis=1)
-    first_line = lax.broadcasted_iota(jnp.int32, (HEAD_ROWS - HEADS, HEAD_DIM), 0) == 0
-    for here, entry in enumerate(entries):
-        out_ref[here, HEADS:, :] = jnp.where(
-            first_line, lasts[here : here + 1], 0.0
-        ).astype(jnp.bfloat16)
+    sealed(out_ref, jnp.swapaxes(denominators, 0, 1)[: len(entries)])
+
+
+def sealed(out_ref, denominators):
+    count = denominators.shape[0]
+    filler = jnp.zeros((TAIL - count, HEAD_DIM), jnp.float32)
+    lasts = jnp.concatenate(two_terms(denominators), axis=1)
+    out_ref[count * HEADS :, :] = jnp.concatenate([lasts, filler]).astype(jnp.bfloat16)
+
+
+def opened(message, place):
+    start = message.shape[0] - TAIL
+    last = message[start:, :].astype(jnp.float32)[place : place + 1]
+    numerator = message[place * HEADS : (place + 1) * HEADS, :].astype(jnp.float32)
+    return numerator, last[:, :HEADS] + last[:, HEADS:]
 
 
 def piece_at(near, second, odd, entry):
@@ -393,7 +404,7 @@
         in_specs=[VMEM_SPEC] * (len(pieces) + 3)
         + [pl.BlockSpec(memory_space=pl.ANY)] * len(beside),
         out_specs=VMEM_SPEC,
-        out_shape=jax.ShapeDtypeStruct((len(entries), HEAD_ROWS, HEAD_DIM), jnp.bfloat16),
+        out_shape=jax.ShapeDtypeStruct((len(entries) * HEADS + TAIL, HEAD_DIM), jnp.bfloat16),
         scratch_shapes=[
             pltpu.VMEM((len(entries), HEADS, pages.shape[2]), jnp.float32),
             pltpu.VMEM((len(entries), HEADS, pages.shape[2]), jnp.bfloat16),
@@ -401,17 +412,6 @@
         compiler_params=pltpu.CompilerParams(vmem_limit_bytes=6 * MIB),
         cost_estimate=pl.CostEstimate(flops=2**26, bytes_accessed=2**20, transcendentals=2**14),
     )(left, second, *pieces, in_vmem(pages), *beside)
-
-
-def opened(piece):
-    last = piece[HEADS:, :].astype(jnp.float32)[:1]
-    return piece[:HEADS, :].astype(jnp.float32), last[:, :HEADS] + last[:, HEADS:]
-
-
-def closed(numerator, denominator):
-    last = jnp.concatenate(two_terms(denominator), axis=1)
-    first_line = lax.broadcasted_iota(jnp.int32, (HEAD_ROWS - HEADS, HEAD_DIM), 0) == 0
-    return numerator.astype(jnp.bfloat16), jnp.where(first_line, last, 0.0).astype(jnp.bfloat16)
 
 
 def two_rows(second_ref, entry, mine, theirs):
@@ -425,10 +425,14 @@
 
 
 def core_kernel(second_ref, mine_ref, theirs_ref, out_ref):
+    lowers = []
     for place in range(4):
-        mine, theirs = opened(mine_ref[place]), opened(theirs_ref[4 + place])
-        for row, terms in enumerate(two_rows(second_ref, 4 + place, mine, theirs)):
-            out_ref[place, row, :HEADS, :], out_ref[place, row, HEADS:, :] = closed(*terms)
+        mine, theirs = opened(mine_ref, place), opened(theirs_ref, 4 + place)
+        for row, (part, lower) in enumerate(two_rows(second_ref, 4 + place, mine, theirs)):
+            start = (2 * place + row) * HEADS
+            out_ref[start : start + HEADS, :] = part.astype(jnp.bfloat16)
+            lowers.append(lower)
+    sealed(out_ref, jnp.concatenate(lowers))
 
 
 def across_core(second, mine, theirs):
@@ -436,55 +440,65 @@
         core_kernel,
         in_specs=[VMEM_SPEC] * 3,
         out_specs=VMEM_SPEC,
-        out_shape=jax.ShapeDtypeStruct((4, 2, HEAD_ROWS, HEAD_DIM), jnp.bfloat16),
+        out_shape=jax.ShapeDtypeStruct((8 * HEADS + TAIL, HEAD_DIM), jnp.bfloat16),
         compiler_params=pltpu.CompilerParams(vmem_limit_bytes=4 * MIB),
     )(second, mine, theirs)
 
 
-def chip_kernel(second_ref, mine_ref, theirs_ref, arrived_ref, unused_ref, *out_refs):
+def chip_kernel(second_ref, mine_ref, theirs_ref, arrived_ref, new_ref, lower_ref, *refs):
+    out_ref = refs[-1]
+    lowers = []
     for place in range(4):
-        mine, theirs = opened(mine_ref[place]), opened(theirs_ref[place])
-        for row, terms in enumerate(two_rows(second_ref, place, mine, theirs)):
-            numerator, denominator = opened(arrived_ref[place, row])
-            sums = closed(terms[0] + numerator, terms[1] + denominator)
-            out_refs[place][row, :HEADS, :], out_refs[place][row, HEADS:, :] = sums
-
-
-def across_y(second, mine, theirs, arrived, beside):
+        mine, theirs = opened(mine_ref, place), opened(theirs_ref, place)
+        for row, (part, lower) in enumerate(two_rows(second_ref, place, mine, theirs)):
+            arrived, arrived_lower = opened(arrived_ref, 2 * place + row)
+            part, lower = part + arrived, lower + arrived_lower
+            if place == 0:
+                part = part + new_ref[row * HEADS : (row + 1) * HEADS, :]
+                lower = lower + lower_ref[8 * row : 8 * row + 1, :]
+            start = (2 * place + row) * HEADS
+            out_ref[start : start + HEADS, :] = part.astype(jnp.bfloat16)
+            lowers.append(lower)
+    sealed(out_ref, jnp.concatenate(lowers))
+
+
+def across_y(second, mine, theirs, arrived, new_terms, beside):
     return pl.pallas_call(
         chip_kernel,
-        in_specs=[VMEM_SPEC] * 4 + [pl.BlockSpec(memory_space=pl.ANY)],
-        out_specs=[VMEM_SPEC] * 4,
-        out_shape=[jax.ShapeDtypeStruct((2, HEAD_ROWS, HEAD_DIM), jnp.bfloat16)] * 4,
-        compiler_params=pltpu.CompilerParams(vmem_limit_bytes=4 * MIB),
-    )(second, mine, theirs, arrived, beside)
+        in_specs=[VMEM_SPEC] * 6 + [pl.BlockSpec(memory_space=pl.ANY)] * len(beside),
+        out_specs=VMEM_SPEC,
+        out_shape=jax.ShapeDtypeStruct((8 * HEADS + TAIL, HEAD_DIM), jnp.bfloat16),
+        compiler_params=pltpu.CompilerParams(vmem_limit_bytes=4 * MIB),
+    )(second, mine, theirs, arrived, *new_terms, *beside)
 
 
 def combine_kernel(*refs):
-    shares, new_ref, out_ref = refs[:4], refs[4], refs[-1]
-    for row in range(2):
-        lines = slice(row * HEADS, (row + 1) * HEADS)
-        total, lower = new_ref[0, lines, :], jnp.zeros((1, HEADS), jnp.float32)
-        for share in shares:
-            numerator, denominator = opened(share[row])
-            total = total + numerator
-            lower = lower + denominator
-        padded = jnp.concatenate([lower, jnp.zeros((1, HEADS), jnp.float32)], axis=1)
-        column = jnp.swapaxes(jnp.broadcast_to(padded, (8, HEAD_DIM)), 0, 1)[:HEADS, :1]
-        out_ref[lines, :] = (total / (column + new_ref[1, lines, :])).astype(jnp.bfloat16)
-
-
-def combined(shares, new_terms, beside):
+    shares, out_ref = refs[:4], refs[-1]
+    parts, lowers = [], []
+    for place in range(4):
+        for row in range(2):
+            terms = [opened(share, 2 * (place ^ j) + row) for j, share in enumerate(shares)]
+            parts.append(sum(part for part, _ in terms))
+            lowers.append(sum(lower for _, lower in terms))
+    lower = jnp.concatenate([jnp.concatenate(lowers), jnp.zeros((8, HEADS), jnp.float32)], axis=1)
+    columns = jnp.swapaxes(lower, 0, 1)
+    for index, part in enumerate(parts):
+        lines = slice(index % 2 * HEADS, (index % 2 + 1) * HEADS)
+        column = columns[:HEADS, index : index + 1]
+        out_ref[index // 2, lines, :] = (part / column).astype(jnp.bfloat16)
+
+
+def combined(shares, beside):
     return pl.pallas_call(
         combine_kernel,
-        in_specs=[VMEM_SPEC] * 5 + [pl.BlockSpec(memory_space=pl.ANY)],
+        in_specs=[VMEM_SPEC] * 4 + [pl.BlockSpec(memory_space=pl.ANY)] * len(beside),
         out_specs=VMEM_SPEC,
-        out_shape=jax.ShapeDtypeStruct((2 * HEADS, HEAD_DIM), jnp.bfloat16),
+        out_shape=jax.ShapeDtypeStruct((4, 2 * HEADS, HEAD_DIM), jnp.bfloat16),
         compiler_params=pltpu.CompilerParams(vmem_limit_bytes=4 * MIB),
         cost_estimate=pl.CostEstimate(
             flops=2**22, bytes_accessed=48 * MIB, transcendentals=2**11
         ),
-    )(*shares, new_terms, beside)
+    )(*shares, *beside)
 
 
 def fetch_kernel(parts, after_ref, *refs):
@@ -631,17 +645,22 @@
             )
             for number in range(2)
         ]
-        for copy_at in copies:
-            started(count, copy_at)
+        started(count, *copies)
     squares = 0.0 if squares_in is None else squares_in[...]
     lefts, squares_out[...] = normed_pieces(entries, pieces, gain_ref, squares)
-    for number, (total, start, blocks) in enumerate(
-        ((gates, gates_in, gate_ref), (ups, ups_in, up_ref))
-    ):
-        for place in range(len(entries) if copies else 0):
+    both = ((gates, gates_in, gate_ref), (ups, ups_in, up_ref))
+    if held:
+        for total, start, blocks in both:
+            total[...] = start[...] + terms_of(lefts, blocks)
+        return
+    for place in range(len(entries)):
+        for number, (total, start, blocks) in enumerate(both):
             copies[number](place).wait()
-        terms = terms_of(lefts, blocks)
-        total[...] = terms if start is None else start[...] + terms
+            terms = jnp.dot(lefts[place], blocks[place], preferred_element_type=jnp.float32)
+            if place > 0:
+                total[...] += terms
+            else:
+                total[...] = terms if start is None else start[...] + terms
 
 
 def feed(entries, pieces, gain, sums, gate_weight, up_weight, held=False):
@@ -762,28 +781,28 @@
     )
 
 
-def down_kernel(choice, hidden_ref, *refs):
-    out_ref = refs[-1]
-    for place, (number, index) in enumerate(choice):
+def down_kernel(hidden_ref, held_ref, out_ref):
+    for place in range(held_ref.shape[0]):
         out_ref[place] = jnp.dot(
-            hidden_ref[...], refs[number][index], preferred_element_type=jnp.float32
+            hidden_ref[...], held_ref[place], preferred_element_type=jnp.float32
         )
 
 
-def down_terms(hidden, parts, choice):
+def down_terms(hidden, held):
     rows, depth = hidden.shape
-    return pl.pallas_call(
-        functools.partial(down_kernel, choice),
-        in_specs=[VMEM_SPEC] * (1 + len(parts)),
+    count = held.shape[0]
+    return pl.pallas_call(
+        down_kernel,
+        in_specs=[VMEM_SPEC] * 2,
         out_specs=VMEM_SPEC,
-        out_shape=jax.ShapeDtypeStruct((len(choice), rows, CHUNK), jnp.float32),
+        out_shape=jax.ShapeDtypeStruct((count, rows, CHUNK), jnp.float32),
         compiler_params=pltpu.CompilerParams(vmem_limit_bytes=4 * MIB),
         cost_estimate=pl.CostEstimate(
-            flops=2 * rows * depth * CHUNK * len(choice),
-            bytes_accessed=2 * depth * CHUNK * len(choice),
+            flops=2 * rows * depth * CHUNK * count,
+            bytes_accessed=2 * depth * CHUNK * count,
             transcendentals=0,
         ),
-    )(hidden, *[in_vmem(part) for part in parts])
+    )(hidden, in_vmem(held))
 
 
 def far_kernel(mine_ref, theirs_ref, out_ref):
@@ -857,11 +876,11 @@
     own, query_rows = packed(queries, norm_gain)
     middle, late = (4, 5, 6, 7), tuple(range(8, 16))
 
-    pages, left, of_second, new_terms = readied(table, query_rows, kv_pages, new_kv)
-    near = stacked(near_pieces(own), (new_terms,))
+    (early_gate,) = fetched(table, (gate_weight, rows_at, late[:3]))
+    near = stacked(near_pieces(own), (early_gate,))
     second = sent(near, 2)
-    (early_gate,) = fetched(near, (gate_weight, rows_at, late[:5]))
-    odd = sent(stacked([near, second], (early_gate,)), 1)
+    pages, left, of_second, *new_terms = readied(table, query_rows, kv_pages, new_kv, near)
+    odd = sent(stacked([near, second], new_terms[:1]), 1)
     gains = near, second, odd
     along = page_terms(left, of_second, (0, 1, 2, 3), (near, second), pages)
     theirs = page_terms(left, of_second, late, (odd,), pages, (along,))
@@ -873,19 +892,17 @@
     gate_held, early_first = fetched(
         across, (gate_weight, rows_at, middle), (up_weight, rows_at, late[:2])
     )
-    own, *others = across_y(of_second, along, theirs, arrived, gate_held)
-    up_held, early_second = fetched(
-        own, (up_weight, rows_at, middle), (up_weight, rows_at, late[2:4])
-    )
-    shares = [sent(other, distance) for other, distance in zip(others[::-1], (12, 8, 4))]
-    attended = combined(shares + [own], new_terms, up_held)
-
-    down_first, early_third = fetched(
-        attended, (down_weight, columns_at, middle[:2]), (up_weight, rows_at, late[4:6])
-    )
-    near = stacked(near_pieces(attended), (down_first,))
+    own = across_y(of_second, along, theirs, arrived, new_terms, (gate_held,))
+    up_held, early_second, down_first = fetched(
+        own,
+        (up_weight, rows_at, middle),
+        (up_weight, rows_at, late[2:6]),
+        (down_weight, columns_at, middle),
+    )
+    near = combined(near_pieces(own), (up_held,))
+
     second = sent(near, 2)
-    (down_rest,) = fetched(near, (down_weight, columns_at, middle[2:] + (0, 1, 2, 3)))
+    (down_rest,) = fetched(near, (down_weight, columns_at, (0, 1, 2, 3)))
     odd = sent(stacked([near, second], (down_rest,)), 1)
     stream = projected(near, second, odd, residual, out_weight)
 
@@ -897,13 +914,13 @@
     sums = feed((1, 2, 3), near[1:], gains[0], sums, *weights)
     odd = sent(stacked([first, second], sums[:1]), 1)
     sums = feed(middle, [second], gains[1], sums, gate_held, up_held, held=True)
-    early = (early_gate,), (early_first, early_second, early_third)
+    early = (early_gate,), (early_first, early_second)
     hidden, theirs = hidden_units(late, odd, gains[2], early, weights, down_weight, sums)
 
     theirs = sent(theirs, 1)
-    far = down_terms(hidden, (down_first, down_rest), ((0, 0), (0, 1), (1, 0), (1, 1)))
+    far = down_terms(hidden, down_first)
     arrived = sent(far_pairs(far, theirs), 2)
-    mine = down_terms(hidden, (down_rest,), ((0, 2), (0, 3), (0, 4), (0, 5)))
+    mine = down_terms(hidden, down_rest)
     own, *others = near_sums(mine, theirs, arrived)
     shares = [sent(other, distance) for other, distance in zip(others[::-1], (12, 8, 4))]
     return finished(stream, shares + [own])

time: 94.1 us -> 89.4 us (0.950)
  starting transfers between devices: 31.6 us -> 26.5 us
  waiting for transfers between devices: 10.9 us -> 13.7 us
  Pallas kernels: 49.4 us -> 47.1 us
    ppermute x25 -> x22, starting transfers between devices: 31.6 us -> 26.5 us  [sent(): lax.ppermute(array, 'shard', [(i, i ^ distance) for i in range(size)])]
    ppermute x25 -> x22, waiting for transfers between devices: 10.9 us -> 13.7 us  [sent(): lax.ppermute(array, 'shard', [(i, i ^ distance) for i in range(size)])]
    pallas_call x5 -> x4, Pallas kernels: 19.4 us -> 17.3 us  [fetched(): pl.pallas_call(functools.partial(fetch_kernel, [part[1:] for part in part...]
  transfers between devices with their start and end apart: 25 -> 22, of which waited for: 10 -> 10; matrix products, arithmetic and copies ran while one was open for 2% -> 2% of each run, Pallas kernels for 39% -> 38%
where the time goes in v4:
time: 89.4 us; the launch traced here: 89.1 us
  Pallas kernels  47.1 us (53%)
  starting transfers between devices  26.5 us (30%)
  waiting for transfers between devices  13.7 us (15%)
    ppermute x22, starting transfers between devices, sent(): lax.ppermute(array, 'shard', [(i, i ^ distance) for i in range(size)])  26.5 us
    pallas_call x4, Pallas kernels, fetched(): pl.pallas_call(functools.partial(fetch_kernel, [part[1:] for part in part...  17.3 us
    ppermute x22, waiting for transfers between devices, sent(): lax.ppermute(array, 'shard', [(i, i ^ distance) for i in range(size)])  13.7 us
    pallas_call x3, Pallas kernels, feed(): pl.pallas_call(functools.partial(feed_kernel, entries, len(pieces), held)...  9.24 us
    pallas_call x1, Pallas kernels, hidden_units(): pl.pallas_call(functools.partial(hidden_kernel, entries, [len(parts) for...  9.16 us
    pallas_call x1, Pallas kernels, readied(): pl.pallas_call(ready_kernel, in_specs=[SMEM_SPEC, VMEM_SPEC] + [HBM_SPEC]...  3.53 us
    pallas_call x2, Pallas kernels, down_terms(): pl.pallas_call(down_kernel, in_specs=[VMEM_SPEC] * 2, out_specs=VMEM_SPEC...  2.5 us
  transfers between devices with their start and end apart: 22, of which 10 were waited for; matrix products, arithmetic and copies ran while one was open for 2% of the time, Pallas kernels for 38%

profile of v4, /device:TPU:0, one launch (start us, length us, event | category | flops | bytes accessed | tf_op | source)
XLA Modules:
  0.0 89.1 jit_solution(8321893144146920839)
XLA Ops:
  0.8 5.1 %collective-permute-start.2 = (bf16[144,128]{1,0:T(8,128)(2,1)S(1)}, bf16[144,128]{1,0:T(8,128)(2,1)S(1)}, u32[]{:S(2)}, u32[]{:S(2)}) collective-permute-start(bf16[144,128]{1,0:T(8,128)(2,1)S(1)} %get-tuple-element.33.refs_0_), channel_id=1, source_target_pairs={{0,12},{1,13},{2,14},{3,15},{4,8},{5,9},{6,10},{7,11},{8,4},{9,5},... | collective-permute-start | bytes 110600 | tf_op jit(solution)/shard_map/ppermute | solution.py:157
  8.2 2.5 %shard_map.110.refs_4_.refs_2_ = bf16[3,512,1664]{2,1,0:T(8,128)(2,1)S(1)} custom-call(s32[289]{0:T(512)S(1)} %pad_add_fusion.after_ref.table_ref, bf16[8192,1664]{1,0:T(8,128)(2,1)} %refs_5_.3), custom_call_target="tpu_custom_call" | custom-call | bytes 5111808 | tf_op jit(solution)/shard_map/pallas_call | solution.py:531
  10.8 1.6 %collective-permute-start.3 = (bf16[4,144,128]{2,1,0:T(8,128)(2,1)S(1)}, bf16[4,144,128]{2,1,0:T(8,128)(2,1)S(1)}, u32[]{:S(2)}, u32[]{:S(2)}) collective-permute-start(bf16[4,144,128]{2,1,0:T(8,128)(2,1)S(1)} %shard_map.111.after_ref.refs_0_.refs_1_.refs_3_), channel_id=1, source_target_pairs={{0,2},{1,3},{2,0},{3,1},{4,6},{5,7},{6,4},{7,5},{8,10},{9,11},{10,... | collective-permute-start | bytes 442376 | tf_op jit(solution)/shard_map/ppermute | solution.py:157
  12.5 3.5 %shard_map.112 = (bf16[16,2,32,512]{3,2,1,0:T(8,128)(2,1)S(1)}, s32[16,128]{1,0:T(8,128)S(1)}, s32[32,128]{1,0:T(8,128)S(1)}, f32[128,128]{1,0:T(8,128)S(1)}, f32[16,64]{1,0:T(8,128)S(1)}) custom-call(s32[289]{0:T(512)S(1)} %pad_add_fusion.after_ref.table_ref, bf16[128,128]{1,0:T(8,128)(2,1)S(1)} %get-tuple-element.32.query_ref, ...), custom_call_target="tpu_custom_call" | custom-call | flops 4194304 | bytes 2097152 | tf_op jit(solution)/shard_map/pallas_call | solution.py:321
  19.8 1.6 %collective-permute-start.6 = (bf16[528,128]{1,0:T(8,128)(2,1)S(1)}, bf16[528,128]{1,0:T(8,128)(2,1)S(1)}, u32[]{:S(2)}, u32[]{:S(2)}) collective-permute-start(bf16[528,128]{1,0:T(8,128)(2,1)S(1)} %shard_map.117.after_ref), channel_id=1, source_target_pairs={{0,2},{1,3},{2,0},{3,1},{4,6},{5,7},{6,4},{7,5},{8,10},{9,11},{10,... | collective-permute-start | bytes 405512 | tf_op jit(solution)/shard_map/ppermute | solution.py:157
  21.4 4.0 %shard_map.118 = (bf16[4,512,1664]{2,1,0:T(8,128)(2,1)S(1)}, bf16[2,512,1664]{2,1,0:T(8,128)(2,1)S(1)}) custom-call(bf16[528,128]{1,0:T(8,128)(2,1)S(1)} %shard_map.117.after_ref, bf16[8192,1664]{1,0:T(8,128)(2,1)} %refs_5_.3, bf16[8192,1664]{1,0:T(8,128)(2,1)} %refs_6_.1), custom_call_target="tpu_custom_call" | custom-call | bytes 10223616 | tf_op jit(solution)/shard_map/pallas_call | solution.py:531
  25.6 3.7 %collective-permute-start.9 = (bf16[528,128]{1,0:T(8,128)(2,1)S(1)}, bf16[528,128]{1,0:T(8,128)(2,1)S(1)}, u32[]{:S(2)}, u32[]{:S(2)}) collective-permute-start(bf16[528,128]{1,0:T(8,128)(2,1)S(1)} %shard_map.119.after_ref.refs_0_), channel_id=1, source_target_pairs={{0,12},{1,13},{2,14},{3,15},{4,8},{5,9},{6,10},{7,11},{8,4},{9,5},... | collective-permute-start | bytes 405512 | tf_op jit(solution)/shard_map/ppermute | solution.py:157
  30.0 7.0 %shard_map.120 = (bf16[4,512,1664]{2,1,0:T(8,128)(2,1)S(1)}, bf16[4,512,1664]{2,1,0:T(8,128)(2,1)S(1)}, bf16[4,1664,512]{2,1,0:T(8,128)(2,1)S(1)}) custom-call(bf16[528,128]{1,0:T(8,128)(2,1)S(1)} %shard_map.119.after_ref.refs_0_, bf16[8192,1664]{1,0:T(8,128)(2,1)} %refs_6_.1, bf16[8192,1664]{1,0:T(8,128)(2,1)} %refs_6_.1, bf16[1664,8192]{1,0:T(8,128)(2,1)} %refs_7_.1), custom_call_target="tpu_custom_call" | custom-call | bytes 20447232 | tf_op jit(solution)/shard_map/pallas_call | solution.py:531
  37.0 3.3 %collective-permute-done.8.refs_2_ = bf16[528,128]{1,0:T(8,128)(2,1)S(1)} collective-permute-done((bf16[528,128]{1,0:T(8,128)(2,1)S(1)}, bf16[528,128]{1,0:T(8,128)(2,1)S(1)}, u32[]{:S(2)}, u32[]{:S(2)}) %collective-permute-start.8) | collective-permute-done | bytes 135200 | tf_op jit(solution)/shard_map/ppermute | solution.py:157
  41.8 3.7 %shard_map.122.refs_2_.held_ref = bf16[4,1664,512]{2,1,0:T(8,128)(2,1)S(1)} custom-call(bf16[4,128,128]{2,1,0:T(8,128)(2,1)S(1)} %shard_map.121.after_ref.refs_0_.near_ref, bf16[1664,8192]{1,0:T(8,128)(2,1)} %refs_7_.1), custom_call_target="tpu_custom_call" | custom-call | bytes 6815744 | tf_op jit(solution)/shard_map/pallas_call | solution.py:531
  45.8 1.5 %collective-permute-done.11.odd_ref = bf16[8,128,128]{2,1,0:T(8,128)(2,1)S(1)} collective-permute-done((bf16[8,128,128]{2,1,0:T(8,128)(2,1)S(1)}, bf16[8,128,128]{2,1,0:T(8,128)(2,1)S(1)}, u32[]{:S(2)}, u32[]{:S(2)}) %collective-permute-start.11) | collective-permute-done | bytes 262176 | tf_op jit(solution)/shard_map/ppermute | solution.py:157
  47.3 1.7 %shard_map.124.refs_0_.stream_ref = bf16[32,512]{1,0:T(8,128)(2,1)S(1)} custom-call(bf16[4,128,128]{2,1,0:T(8,128)(2,1)S(1)} %shard_map.121.after_ref.refs_0_.near_ref, bf16[4,128,128]{2,1,0:T(8,128)(2,1)S(1)} %collective-permute-done.10.refs_1_.second_ref, bf16[8,128,128]{2,1,0:T(8,128)(2,1)S(1)} %collective-permute-done.11.odd_ref, ...), custom_call_target="tpu_custom_call" | custom-call | flops 268435456 | bytes 8388608 | tf_op jit(solution)/shard_map/pallas_call | solution.py:590
  49.0 2.4 %collective-permute-start.14 = (bf16[32,512]{1,0:T(8,128)(2,1)S(1)}, bf16[32,512]{1,0:T(8,128)(2,1)S(1)}, u32[]{:S(2)}, u32[]{:S(2)}) collective-permute-start(bf16[32,512]{1,0:T(8,128)(2,1)S(1)} %shard_map.124.refs_0_.stream_ref), channel_id=1, source_target_pairs={{0,12},{1,13},{2,14},{3,15},{4,8},{5,9},{6,10},{7,11},{8,4},{9,5},... | collective-permute-start | bytes 98312 | tf_op jit(solution)/shard_map/ppermute | solution.py:157
  51.4 2.0 %collective-permute-start.12 = (bf16[32,512]{1,0:T(8,128)(2,1)S(1)}, bf16[32,512]{1,0:T(8,128)(2,1)S(1)}, u32[]{:S(2)}, u32[]{:S(2)}) collective-permute-start(bf16[32,512]{1,0:T(8,128)(2,1)S(1)} %shard_map.124.refs_0_.stream_ref), channel_id=1, source_target_pairs={{0,4},{1,5},{2,6},{3,7},{4,0},{5,1},{6,2},{7,3},{8,12},{9,13},{10,... | collective-permute-start | bytes 98312 | tf_op jit(solution)/shard_map/ppermute | solution.py:157
  53.4 2.4 %shard_map.125 = (f32[32,1664]{1,0:T(8,128)S(1)}, f32[32,1664]{1,0:T(8,128)S(1)}, f32[32,512]{1,0:T(8,128)S(1)}) custom-call(bf16[32,512]{1,0:T(8,128)(2,1)S(1)} %shard_map.124.refs_0_.stream_ref, bf16[4,144,128]{2,1,0:T(8,128)(2,1)S(1)} %shard_map.111.after_ref.refs_0_.refs_1_.refs_3_, bf16[8192,1664]{1,0:T(8,128)(2,1)} %refs_5_.3, bf16[8192,1664]{1,0:T(8,128)(2,1)} %refs_6_.1), custom_call_target="tpu_custom_call" | custom-call | flops 109051904 | bytes 3407872 | tf_op jit(solution)/shard_map/pallas_call | solution.py:673
  57.4 4.4 %shard_map.127 = (f32[32,1664]{1,0:T(8,128)S(1)}, f32[32,1664]{1,0:T(8,128)S(1)}, f32[32,512]{1,0:T(8,128)S(1)}) custom-call(bf16[32,512]{1,0:T(8,128)(2,1)S(1)} %collective-permute-done.12.refs_1_.refs_0_, bf16[32,512]{1,0:T(8,128)(2,1)S(1)} %collective-permute-done.13.refs_2_.refs_1_, bf16[32,512]{1,0:T(8,128)(2,1)S(1)} %collective-permute-done.14.refs_3_.refs_2_, ...), custom_call_target="tpu_custom_call" | custom-call | flops 327155712 | bytes 10223616 | tf_op jit(solution)/shard_map/pallas_call | solution.py:673
  62.0 2.4 %shard_map.129 = (f32[32,1664]{1,0:T(8,128)S(1)}, f32[32,1664]{1,0:T(8,128)S(1)}, f32[32,512]{1,0:T(8,128)S(1)}) custom-call(bf16[4,32,512]{2,1,0:T(8,128)(2,1)S(1)} %collective-permute-done.15.refs_1_.refs_0_, bf16[4,144,128]{2,1,0:T(8,128)(2,1)S(1)} %collective-permute-done.3.refs_1_, bf16[4,512,1664]{2,1,0:T(8,128)(2,1)S(1)} %get-tuple-element.39.refs_0_.refs_2_, ...), custom_call_target="tpu_custom_call" | custom-call | flops 436207616 | bytes 13631488 | tf_op jit(solution)/shard_map/pallas_call | solution.py:673
  64.4 9.2 %shard_map.130 = (bf16[32,1664]{1,0:T(8,128)(2,1)S(1)}, bf16[8,32,512]{2,1,0:T(8,128)(2,1)S(1)}) custom-call(bf16[8,32,512]{2,1,0:T(8,128)(2,1)S(1)} %collective-permute-done.16.refs_0_, bf16[8,144,128]{2,1,0:T(8,128)(2,1)S(1)} %collective-permute-done.4.refs_0_.refs_1_, bf16[3,512,1664]{2,1,0:T(8,128)(2,1)S(1)} %shard_map.110.refs_4_.refs_2_, ...), custom_call_target="tpu_custom_call" | custom-call | flops 1308622848 | bytes 40894464 | tf_op jit(solution)/shard_map/pallas_call | solution.py:754
  74.1 1.2 %shard_map.132.mine_ref = f32[4,32,512]{2,1,0:T(8,128)S(1)} custom-call(bf16[32,1664]{1,0:T(8,128)(2,1)S(1)} %get-tuple-element.52.hidden_ref, bf16[4,1664,512]{2,1,0:T(8,128)(2,1)S(1)} %get-tuple-element.54.held_ref), custom_call_target="tpu_custom_call" | custom-call | flops 218103808 | bytes 6815744 | tf_op jit(solution)/shard_map/pallas_call | solution.py:794
  77.7 3.5 %collective-permute-done.18.arrived_ref = bf16[4,32,512]{2,1,0:T(8,128)(2,1)S(1)} collective-permute-done((bf16[4,32,512]{2,1,0:T(8,128)(2,1)S(1)}, bf16[4,32,512]{2,1,0:T(8,128)(2,1)S(1)}, u32[]{:S(2)}, u32[]{:S(2)}) %collective-permute-start.18) | collective-permute-done | bytes 131104 | tf_op jit(solution)/shard_map/ppermute | solution.py:157
  81.2 2.1 %collective-permute-start.19 = (bf16[32,512]{1,0:T(8,128)(2,1)S(1)}, bf16[32,512]{1,0:T(8,128)(2,1)S(1)}, u32[]{:S(2)}, u32[]{:S(2)}) collective-permute-start(bf16[32,512]{1,0:T(8,128)(2,1)S(1)} %get-tuple-element.55), channel_id=1, source_target_pairs={{0,12},{1,13},{2,14},{3,15},{4,8},{5,9},{6,10},{7,11},{8,4},{9,5},... | collective-permute-start | bytes 98312 | tf_op jit(solution)/shard_map/ppermute | solution.py:157
  83.8 1.9 %collective-permute-start.21 = (bf16[32,512]{1,0:T(8,128)(2,1)S(1)}, bf16[32,512]{1,0:T(8,128)(2,1)S(1)}, u32[]{:S(2)}, u32[]{:S(2)}) collective-permute-start(bf16[32,512]{1,0:T(8,128)(2,1)S(1)} %get-tuple-element.57), channel_id=1, source_target_pairs={{0,4},{1,5},{2,6},{3,7},{4,0},{5,1},{6,2},{7,3},{8,12},{9,13},{10,... | collective-permute-start | bytes 98312 | tf_op jit(solution)/shard_map/ppermute | solution.py:157
  85.7 1.3 %collective-permute-done.19.refs_0_ = bf16[32,512]{1,0:T(8,128)(2,1)S(1)} collective-permute-done((bf16[32,512]{1,0:T(8,128)(2,1)S(1)}, bf16[32,512]{1,0:T(8,128)(2,1)S(1)}, u32[]{:S(2)}, u32[]{:S(2)}) %collective-permute-start.19) | collective-permute-done | bytes 32800 | tf_op jit(solution)/shard_map/ppermute | solution.py:157
  87.0 1.5 %collective-permute-done.20.refs_1_ = bf16[32,512]{1,0:T(8,128)(2,1)S(1)} collective-permute-done((bf16[32,512]{1,0:T(8,128)(2,1)S(1)}, bf16[32,512]{1,0:T(8,128)(2,1)S(1)}, u32[]{:S(2)}, u32[]{:S(2)}) %collective-permute-start.20) | collective-permute-done | bytes 32800 | tf_op jit(solution)/shard_map/ppermute | solution.py:157
  (57 shorter events, 15.3 us)
Async XLA Ops:
  0.8 9.9 %collective-permute-start.2 = (bf16[144,128]{1,0:T(8,128)(2,1)S(1)}, bf16[144,128]{1,0:T(8,128)(2,1)S(1)}, u32[]{:S(2)}, u32[]{:S(2)}) collective-permute-start(bf16[144,128]{1,0:T(8,128)(2,1)S(1)} %get-tuple-element.33.refs_0_), channel_id=1, source_target_pairs={{0,12},{1,13},{2,14},{3,15},{4,8},{5,9},{6,10},{7,11},{8,4},{9,5},... | collective-permute-start | bytes 110600 | tf_op jit(solution)/shard_map/ppermute | solution.py:157
  6.0 4.9 %collective-permute-start.1 = (bf16[144,128]{1,0:T(8,128)(2,1)S(1)}, bf16[144,128]{1,0:T(8,128)(2,1)S(1)}, u32[]{:S(2)}, u32[]{:S(2)}) collective-permute-start(bf16[144,128]{1,0:T(8,128)(2,1)S(1)} %get-tuple-element.33.refs_0_), channel_id=1, source_target_pairs={{0,8},{1,9},{2,10},{3,11},{4,12},{5,13},{6,14},{7,15},{8,0},{9,1},... | collective-permute-start | bytes 110600 | tf_op jit(solution)/shard_map/ppermute | solution.py:157
  6.0 4.9 %collective-permute-start = (bf16[144,128]{1,0:T(8,128)(2,1)S(1)}, bf16[144,128]{1,0:T(8,128)(2,1)S(1)}, u32[]{:S(2)}, u32[]{:S(2)}) collective-permute-start(bf16[144,128]{1,0:T(8,128)(2,1)S(1)} %get-tuple-element.33.refs_0_), channel_id=1, source_target_pairs={{0,4},{1,5},{2,6},{3,7},{4,0},{5,1},{6,2},{7,3},{8,12},{9,13},{10,... | collective-permute-start | bytes 110600 | tf_op jit(solution)/shard_map/ppermute | solution.py:157
  10.8 5.2 %collective-permute-start.3 = (bf16[4,144,128]{2,1,0:T(8,128)(2,1)S(1)}, bf16[4,144,128]{2,1,0:T(8,128)(2,1)S(1)}, u32[]{:S(2)}, u32[]{:S(2)}) collective-permute-start(bf16[4,144,128]{2,1,0:T(8,128)(2,1)S(1)} %shard_map.111.after_ref.refs_0_.refs_1_.refs_3_), channel_id=1, source_target_pairs={{0,2},{1,3},{2,0},{3,1},{4,6},{5,7},{6,4},{7,5},{8,10},{9,11},{10,... | collective-permute-start | bytes 442376 | tf_op jit(solution)/shard_map/ppermute | solution.py:157
  16.1 1.6 %collective-permute-start.4 = (bf16[8,144,128]{2,1,0:T(8,128)(2,1)S(1)}, bf16[8,144,128]{2,1,0:T(8,128)(2,1)S(1)}, u32[]{:S(2)}, u32[]{:S(2)}) collective-permute-start(bf16[8,144,128]{2,1,0:T(8,128)(2,1)S(1)} %shard_map.114), channel_id=1, source_target_pairs={{0,1},{1,0},{2,3},{3,2},{4,5},{5,4},{6,7},{7,6},{8,9},{9,8},{10,11... | collective-permute-start | bytes 884744 | tf_op jit(solution)/shard_map/ppermute | solution.py:157
  18.3 1.4 %collective-permute-start.5 = (bf16[528,128]{1,0:T(8,128)(2,1)S(1)}, bf16[528,128]{1,0:T(8,128)(2,1)S(1)}, u32[]{:S(2)}, u32[]{:S(2)}) collective-permute-start(bf16[528,128]{1,0:T(8,128)(2,1)S(1)} %shard_map.115), channel_id=1, source_target_pairs={{0,1},{1,0},{2,3},{3,2},{4,5},{5,4},{6,7},{7,6},{8,9},{9,8},{10,11... | collective-permute-start | bytes 405512 | tf_op jit(solution)/shard_map/ppermute | solution.py:157
  19.8 5.6 %collective-permute-start.6 = (bf16[528,128]{1,0:T(8,128)(2,1)S(1)}, bf16[528,128]{1,0:T(8,128)(2,1)S(1)}, u32[]{:S(2)}, u32[]{:S(2)}) collective-permute-start(bf16[528,128]{1,0:T(8,128)(2,1)S(1)} %shard_map.117.after_ref), channel_id=1, source_target_pairs={{0,2},{1,3},{2,0},{3,1},{4,6},{5,7},{6,4},{7,5},{8,10},{9,11},{10,... | collective-permute-start | bytes 405512 | tf_op jit(solution)/shard_map/ppermute | solution.py:157
  25.6 11.4 %collective-permute-start.9 = (bf16[528,128]{1,0:T(8,128)(2,1)S(1)}, bf16[528,128]{1,0:T(8,128)(2,1)S(1)}, u32[]{:S(2)}, u32[]{:S(2)}) collective-permute-start(bf16[528,128]{1,0:T(8,128)(2,1)S(1)} %shard_map.119.after_ref.refs_0_), channel_id=1, source_target_pairs={{0,12},{1,13},{2,14},{3,15},{4,8},{5,9},{6,10},{7,11},{8,4},{9,5},... | collective-permute-start | bytes 405512 | tf_op jit(solution)/shard_map/ppermute | solution.py:157
  29.3 11.0 %collective-permute-start.8 = (bf16[528,128]{1,0:T(8,128)(2,1)S(1)}, bf16[528,128]{1,0:T(8,128)(2,1)S(1)}, u32[]{:S(2)}, u32[]{:S(2)}) collective-permute-start(bf16[528,128]{1,0:T(8,128)(2,1)S(1)} %shard_map.119.after_ref.refs_0_), channel_id=1, source_target_pairs={{0,8},{1,9},{2,10},{3,11},{4,12},{5,13},{6,14},{7,15},{8,0},{9,1},... | collective-permute-start | bytes 405512 | tf_op jit(solution)/shard_map/ppermute | solution.py:157
  29.3 11.0 %collective-permute-start.7 = (bf16[528,128]{1,0:T(8,128)(2,1)S(1)}, bf16[528,128]{1,0:T(8,128)(2,1)S(1)}, u32[]{:S(2)}, u32[]{:S(2)}) collective-permute-start(bf16[528,128]{1,0:T(8,128)(2,1)S(1)} %shard_map.119.after_ref.refs_0_), channel_id=1, source_target_pairs={{0,4},{1,5},{2,6},{3,7},{4,0},{5,1},{6,2},{7,3},{8,12},{9,13},{10,... | collective-permute-start | bytes 405512 | tf_op jit(solution)/shard_map/ppermute | solution.py:157
  40.3 7.0 %slice-start = ((s8[8388608]{0:T(1024)(128)(4,1)}), s8[4194304]{0:T(1024)(128)(4,1)S(1)}, s32[]{:S(2)}) async-start(s8[8388608]{0:T(1024)(128)(4,1)} %bitcast.2), calls=%async_computation | async-start | bytes 8388608
  40.6 6.7 %slice-start.1 = ((s8[8388608]{0:T(1024)(128)(4,1)}), s8[4194304]{0:T(1024)(128)(4,1)S(1)}, s32[]{:S(2)}) async-start(s8[8388608]{0:T(1024)(128)(4,1)} %bitcast.2), calls=%async_computation.1 | async-start | bytes 8388608
  40.6 5.0 %collective-permute-start.10 = (bf16[4,128,128]{2,1,0:T(8,128)(2,1)S(1)}, bf16[4,128,128]{2,1,0:T(8,128)(2,1)S(1)}, u32[]{:S(2)}, u32[]{:S(2)}) collective-permute-start(bf16[4,128,128]{2,1,0:T(8,128)(2,1)S(1)} %shard_map.121.after_ref.refs_0_.near_ref), channel_id=1, source_target_pairs={{0,2},{1,3},{2,0},{3,1},{4,6},{5,7},{6,4},{7,5},{8,10},{9,11},{10,... | collective-permute-start | bytes 393224 | tf_op jit(solution)/shard_map/ppermute | solution.py:157
  45.7 1.6 %collective-permute-start.11 = (bf16[8,128,128]{2,1,0:T(8,128)(2,1)S(1)}, bf16[8,128,128]{2,1,0:T(8,128)(2,1)S(1)}, u32[]{:S(2)}, u32[]{:S(2)}) collective-permute-start(bf16[8,128,128]{2,1,0:T(8,128)(2,1)S(1)} %shard_map.123), channel_id=1, source_target_pairs={{0,1},{1,0},{2,3},{3,2},{4,5},{5,4},{6,7},{7,6},{8,9},{9,8},{10,11... | collective-permute-start | bytes 786440 | tf_op jit(solution)/shard_map/ppermute | solution.py:157
  49.0 6.8 %collective-permute-start.14 = (bf16[32,512]{1,0:T(8,128)(2,1)S(1)}, bf16[32,512]{1,0:T(8,128)(2,1)S(1)}, u32[]{:S(2)}, u32[]{:S(2)}) collective-permute-start(bf16[32,512]{1,0:T(8,128)(2,1)S(1)} %shard_map.124.refs_0_.stream_ref), channel_id=1, source_target_pairs={{0,12},{1,13},{2,14},{3,15},{4,8},{5,9},{6,10},{7,11},{8,4},{9,5},... | collective-permute-start | bytes 98312 | tf_op jit(solution)/shard_map/ppermute | solution.py:157
  51.4 4.8 %collective-permute-start.13 = (bf16[32,512]{1,0:T(8,128)(2,1)S(1)}, bf16[32,512]{1,0:T(8,128)(2,1)S(1)}, u32[]{:S(2)}, u32[]{:S(2)}) collective-permute-start(bf16[32,512]{1,0:T(8,128)(2,1)S(1)} %shard_map.124.refs_0_.stream_ref), channel_id=1, source_target_pairs={{0,8},{1,9},{2,10},{3,11},{4,12},{5,13},{6,14},{7,15},{8,0},{9,1},... | collective-permute-start | bytes 98312 | tf_op jit(solution)/shard_map/ppermute | solution.py:157
  51.4 4.8 %collective-permute-start.12 = (bf16[32,512]{1,0:T(8,128)(2,1)S(1)}, bf16[32,512]{1,0:T(8,128)(2,1)S(1)}, u32[]{:S(2)}, u32[]{:S(2)}) collective-permute-start(bf16[32,512]{1,0:T(8,128)(2,1)S(1)} %shard_map.124.refs_0_.stream_ref), channel_id=1, source_target_pairs={{0,4},{1,5},{2,6},{3,7},{4,0},{5,1},{6,2},{7,3},{8,12},{9,13},{10,... | collective-permute-start | bytes 98312 | tf_op jit(solution)/shard_map/ppermute | solution.py:157
  56.2 5.6 %collective-permute-start.15 = (bf16[4,32,512]{2,1,0:T(8,128)(2,1)S(1)}, bf16[4,32,512]{2,1,0:T(8,128)(2,1)S(1)}, u32[]{:S(2)}, u32[]{:S(2)}) collective-permute-start(bf16[4,32,512]{2,1,0:T(8,128)(2,1)S(1)} %shard_map.126.refs_0_), channel_id=1, source_target_pairs={{0,2},{1,3},{2,0},{3,1},{4,6},{5,7},{6,4},{7,5},{8,10},{9,11},{10,... | collective-permute-start | bytes 393224 | tf_op jit(solution)/shard_map/ppermute | solution.py:157
  61.9 2.5 %collective-permute-start.16 = (bf16[8,32,512]{2,1,0:T(8,128)(2,1)S(1)}, bf16[8,32,512]{2,1,0:T(8,128)(2,1)S(1)}, u32[]{:S(2)}, u32[]{:S(2)}) collective-permute-start(bf16[8,32,512]{2,1,0:T(8,128)(2,1)S(1)} %shard_map.128), channel_id=1, source_target_pairs={{0,1},{1,0},{2,3},{3,2},{4,5},{5,4},{6,7},{7,6},{8,9},{9,8},{10,11... | collective-permute-start | bytes 786440 | tf_op jit(solution)/shard_map/ppermute | solution.py:157
  73.6 1.8 %collective-permute-start.17 = (bf16[8,32,512]{2,1,0:T(8,128)(2,1)S(1)}, bf16[8,32,512]{2,1,0:T(8,128)(2,1)S(1)}, u32[]{:S(2)}, u32[]{:S(2)}) collective-permute-start(bf16[8,32,512]{2,1,0:T(8,128)(2,1)S(1)} %get-tuple-element.53), channel_id=1, source_target_pairs={{0,1},{1,0},{2,3},{3,2},{4,5},{5,4},{6,7},{7,6},{8,9},{9,8},{10,11... | collective-permute-start | bytes 786440 | tf_op jit(solution)/shard_map/ppermute | solution.py:157
  75.5 5.7 %collective-permute-start.18 = (bf16[4,32,512]{2,1,0:T(8,128)(2,1)S(1)}, bf16[4,32,512]{2,1,0:T(8,128)(2,1)S(1)}, u32[]{:S(2)}, u32[]{:S(2)}) collective-permute-start(bf16[4,32,512]{2,1,0:T(8,128)(2,1)S(1)} %shard_map.133), channel_id=1, source_target_pairs={{0,2},{1,3},{2,0},{3,1},{4,6},{5,7},{6,4},{7,5},{8,10},{9,11},{10,... | collective-permute-start | bytes 393224 | tf_op jit(solution)/shard_map/ppermute | solution.py:157
  81.2 5.8 %collective-permute-start.19 = (bf16[32,512]{1,0:T(8,128)(2,1)S(1)}, bf16[32,512]{1,0:T(8,128)(2,1)S(1)}, u32[]{:S(2)}, u32[]{:S(2)}) collective-permute-start(bf16[32,512]{1,0:T(8,128)(2,1)S(1)} %get-tuple-element.55), channel_id=1, source_target_pairs={{0,12},{1,13},{2,14},{3,15},{4,8},{5,9},{6,10},{7,11},{8,4},{9,5},... | collective-permute-start | bytes 98312 | tf_op jit(solution)/shard_map/ppermute | solution.py:157
  83.3 5.2 %collective-permute-start.20 = (bf16[32,512]{1,0:T(8,128)(2,1)S(1)}, bf16[32,512]{1,0:T(8,128)(2,1)S(1)}, u32[]{:S(2)}, u32[]{:S(2)}) collective-permute-start(bf16[32,512]{1,0:T(8,128)(2,1)S(1)} %get-tuple-element.56), channel_id=1, source_target_pairs={{0,8},{1,9},{2,10},{3,11},{4,12},{5,13},{6,14},{7,15},{8,0},{9,1},... | collective-permute-start | bytes 98312 | tf_op jit(solution)/shard_map/ppermute | solution.py:157
  83.8 4.7 %collective-permute-start.21 = (bf16[32,512]{1,0:T(8,128)(2,1)S(1)}, bf16[32,512]{1,0:T(8,128)(2,1)S(1)}, u32[]{:S(2)}, u32[]{:S(2)}) collective-permute-start(bf16[32,512]{1,0:T(8,128)(2,1)S(1)} %get-tuple-element.57), channel_id=1, source_target_pairs={{0,4},{1,5},{2,6},{3,7},{4,0},{5,1},{6,2},{7,3},{8,12},{9,13},{10,... | collective-permute-start | bytes 98312 | tf_op jit(solution)/shard_map/ppermute | solution.py:157
  (1 other events, 1.8 us)

commit v5 on v4

--- a/solution.py
+++ b/solution.py
@@ -617,20 +617,39 @@
     return lefts, squares
 
 
+def product(left, weight_at, width):
+    step = 128 if width % 128 == 0 else width
+    tiles = [
+        jnp.dot(left, weight_at(slice(start, start + step)), preferred_element_type=jnp.float32)
+        for start in range(0, width, step)
+    ]
+    return jnp.concatenate(tiles, axis=1)
+
+
 def terms_of(lefts, blocks):
     left = jnp.concatenate(lefts, axis=1)
-    weight = blocks[...].reshape(left.shape[1], blocks.shape[-1])
-    return jnp.dot(left, weight, preferred_element_type=jnp.float32)
-
-
-def feed_kernel(entries, piece_count, held, *refs):
+    here = lambda cols: blocks[:, :, cols].reshape(left.shape[1], -1)
+    return product(left, here, blocks.shape[-1])
+
+
+def feed_kernel(entries, piece_count, held, ahead, *refs):
     refs = list(refs)
     take = lambda number: [refs.pop(0) for _ in range(number)]
     pieces = take(piece_count)
     gain_ref, gate_ref, up_ref = take(3)
     gates_in, ups_in, squares_in = [None] * 3 if entries[0] == 0 else take(3)
+    ahead_hbm = take(1)[0] if ahead else None
     gates, ups, squares_out = take(3)
     copies = []
+    if ahead:
+        ahead_out, ahead_sems = refs
+        me = lax.axis_index("shard")
+        ahead_copy = lambda place: pltpu.make_async_copy(
+            rows_at(ahead_hbm, device_at(me, ahead[0] + place)),
+            ahead_out.at[place],
+            ahead_sems.at[place],
+        )
+        started(len(ahead), ahead_copy)
     if not held:
         sources = gate_ref, up_ref
         *targets, sems = refs
@@ -652,6 +671,8 @@
     if held:
         for total, start, blocks in both:
             total[...] = start[...] + terms_of(lefts, blocks)
+        for place in range(len(ahead)):
+            ahead_copy(place).wait()
         return
     for place in range(len(entries)):
         for number, (total, start, blocks) in enumerate(both):
@@ -663,7 +684,7 @@
                 total[...] = terms if start is None else start[...] + terms
 
 
-def feed(entries, pieces, gain, sums, gate_weight, up_weight, held=False):
+def feed(entries, pieces, gain, sums, gate_weight, up_weight, held=False, ahead=(), ahead_weight=None):
     rows = pieces[0].shape[-2]
     width = gate_weight.shape[-1]
     count = len(entries)
@@ -671,13 +692,17 @@
     here = in_vmem if held else in_hbm
     slots = pltpu.VMEM((count, CHUNK, width), jnp.bfloat16)
     return pl.pallas_call(
-        functools.partial(feed_kernel, entries, len(pieces), held),
+        functools.partial(feed_kernel, entries, len(pieces), held, ahead),
         in_specs=[VMEM_SPEC] * (len(pieces) + 1)
         + [VMEM_SPEC if held else HBM_SPEC] * 2
-        + [VMEM_SPEC] * len(sums),
-        out_specs=[VMEM_SPEC] * 3,
-        out_shape=[total, total, jax.ShapeDtypeStruct((rows, CHUNK), jnp.float32)],
-        scratch_shapes=[] if held else [slots, slots, pltpu.SemaphoreType.DMA((2 * count,))],
+        + [VMEM_SPEC] * len(sums)
+        + [HBM_SPEC] * bool(ahead),
+        out_specs=[VMEM_SPEC] * (3 + bool(ahead)),
+        out_shape=[total, total, jax.ShapeDtypeStruct((rows, CHUNK), jnp.float32)]
+        + [pltpu.VMEM((len(ahead), CHUNK, width), jnp.bfloat16)] * bool(ahead),
+        scratch_shapes=[pltpu.SemaphoreType.DMA((max(len(ahead), 1),))] * bool(ahead)
+        if held
+        else [slots, slots, pltpu.SemaphoreType.DMA((2 * count,))],
         compiler_params=pltpu.CompilerParams(
             vmem_limit_bytes=2 * MIB + (0 if held else 4 * count * CHUNK * width)
         ),
@@ -686,7 +711,7 @@
             bytes_accessed=4 * count * CHUNK * width,
             transcendentals=0,
         ),
-    )(*pieces, gain, here(gate_weight), here(up_weight), *sums)
+    )(*pieces, gain, here(gate_weight), here(up_weight), *sums, *([in_hbm(ahead_weight)] if ahead else []))
 
 
 def hidden_kernel(entries, early_counts, *refs):
@@ -738,9 +763,8 @@
     hidden_ref[...] = (jax.nn.silu(gates) * ups).astype(jnp.bfloat16)
     for place in range(count):
         down_copy(place).wait()
-        out_ref[place] = jnp.dot(
-            hidden_ref[...], down_held[place], preferred_element_type=jnp.float32
-        ).astype(jnp.bfloat16)
+        here = lambda cols: down_held[place, :, cols]
+        out_ref[place] = product(hidden_ref[...], here, CHUNK).astype(jnp.bfloat16)
 
 
 def hidden_units(entries, odd, gain, early, weights, down_weight, sums):
@@ -764,7 +788,7 @@
         + [pltpu.SemaphoreType.DMA((number,)) for number in later]
         + [pltpu.VMEM((count, width, CHUNK), jnp.bfloat16), pltpu.SemaphoreType.DMA((count,))],
         compiler_params=pltpu.CompilerParams(
-            vmem_limit_bytes=2 * (sum(later) + count) * CHUNK * width + 2 * MIB
+            vmem_limit_bytes=2 * (sum(later) + count) * CHUNK * width + MIB
         ),
         cost_estimate=pl.CostEstimate(
             flops=2 * rows * 3 * count * CHUNK * width,
@@ -783,9 +807,7 @@
 
 def down_kernel(hidden_ref, held_ref, out_ref):
     for place in range(held_ref.shape[0]):
-        out_ref[place] = jnp.dot(
-            hidden_ref[...], held_ref[place], preferred_element_type=jnp.float32
-        )
+        out_ref[place] = product(hidden_ref[...], lambda cols: held_ref[place, :, cols], CHUNK)
 
 
 def down_terms(hidden, held):
@@ -913,8 +935,18 @@
     second = sent(first, 2)
     sums = feed((1, 2, 3), near[1:], gains[0], sums, *weights)
     odd = sent(stacked([first, second], sums[:1]), 1)
-    sums = feed(middle, [second], gains[1], sums, gate_held, up_held, held=True)
-    early = (early_gate,), (early_first, early_second)
+    *sums, more_gate = feed(
+        middle,
+        [second],
+        gains[1],
+        sums,
+        gate_held,
+        up_held,
+        held=True,
+        ahead=late[3:5],
+        ahead_weight=gate_weight,
+    )
+    early = (early_gate, more_gate), (early_first, early_second)
     hidden, theirs = hidden_units(late, odd, gains[2], early, weights, down_weight, sums)
 
     theirs = sent(theirs, 1)

time: 89.4 us -> 88.3 us (0.988)
  Pallas kernels: 47.1 us -> 45.5 us
    pallas_call x1, Pallas kernels: 9.16 us -> 8.13 us  [hidden_units(): pl.pallas_call(functools.partial(hidden_kernel, entries, [len(parts) for...]
  transfers between devices with their start and end apart: 22 -> 22, of which waited for: 10 -> 10; matrix products, arithmetic and copies ran while one was open for 2% -> 2% of each run, Pallas kernels for 38% -> 37%
where the time goes in v5:
time: 88.3 us; the launch traced here: 88 us
  Pallas kernels  45.5 us (52%)
  starting transfers between devices  26.4 us (30%)
  waiting for transfers between devices  14.1 us (16%)
  local copies, waits for them, and re-layouts  1.02 us (1%)
    ppermute x22, starting transfers between devices, sent(): lax.ppermute(array, 'shard', [(i, i ^ distance) for i in range(size)])  26.4 us
    pallas_call x4, Pallas kernels, fetched(): pl.pallas_call(functools.partial(fetch_kernel, [part[1:] for part in part...  17.3 us
    ppermute x22, waiting for transfers between devices, sent(): lax.ppermute(array, 'shard', [(i, i ^ distance) for i in range(size)])  14.1 us
    pallas_call x3, Pallas kernels, feed(): pl.pallas_call(functools.partial(feed_kernel, entries, len(pieces), held,...  8.98 us
    pallas_call x1, Pallas kernels, hidden_units(): pl.pallas_call(functools.partial(hidden_kernel, entries, [len(parts) for...  8.13 us
    pallas_call x1, Pallas kernels, readied(): pl.pallas_call(ready_kernel, in_specs=[SMEM_SPEC, VMEM_SPEC] + [HBM_SPEC]...  3.53 us
    pallas_call x2, Pallas kernels, down_terms(): pl.pallas_call(down_kernel, in_specs=[VMEM_SPEC] * 2, out_specs=VMEM_SPEC...  2.15 us
  transfers between devices with their start and end apart: 22, of which 10 were waited for; matrix products, arithmetic and copies ran while one was open for 2% of the time, Pallas kernels for 37%

profile of v5, /device:TPU:0, one launch (start us, length us, event | category | flops | bytes accessed | tf_op | source)
XLA Modules:
  0.0 88.0 jit_solution(196048602646443637)
XLA Ops:
  0.8 5.1 %collective-permute-start.2 = (bf16[144,128]{1,0:T(8,128)(2,1)S(1)}, bf16[144,128]{1,0:T(8,128)(2,1)S(1)}, u32[]{:S(2)}, u32[]{:S(2)}) collective-permute-start(bf16[144,128]{1,0:T(8,128)(2,1)S(1)} %get-tuple-element.34.refs_0_), channel_id=1, source_target_pairs={{0,12},{1,13},{2,14},{3,15},{4,8},{5,9},{6,10},{7,11},{8,4},{9,5},... | collective-permute-start | bytes 110600 | tf_op jit(solution)/shard_map/ppermute | solution.py:157
  8.2 2.5 %shard_map.110.refs_4_.refs_2_ = bf16[3,512,1664]{2,1,0:T(8,128)(2,1)S(1)} custom-call(s32[289]{0:T(512)S(1)} %pad_add_fusion.after_ref.table_ref, bf16[8192,1664]{1,0:T(8,128)(2,1)} %refs_6_.1), custom_call_target="tpu_custom_call" | custom-call | bytes 5111808 | tf_op jit(solution)/shard_map/pallas_call | solution.py:531
  10.8 1.6 %collective-permute-start.3 = (bf16[4,144,128]{2,1,0:T(8,128)(2,1)S(1)}, bf16[4,144,128]{2,1,0:T(8,128)(2,1)S(1)}, u32[]{:S(2)}, u32[]{:S(2)}) collective-permute-start(bf16[4,144,128]{2,1,0:T(8,128)(2,1)S(1)} %shard_map.111.after_ref.refs_0_.refs_1_.refs_3_), channel_id=1, source_target_pairs={{0,2},{1,3},{2,0},{3,1},{4,6},{5,7},{6,4},{7,5},{8,10},{9,11},{10,... | collective-permute-start | bytes 442376 | tf_op jit(solution)/shard_map/ppermute | solution.py:157
  12.5 3.5 %shard_map.112 = (bf16[16,2,32,512]{3,2,1,0:T(8,128)(2,1)S(1)}, s32[16,128]{1,0:T(8,128)S(1)}, s32[32,128]{1,0:T(8,128)S(1)}, f32[128,128]{1,0:T(8,128)S(1)}, f32[16,64]{1,0:T(8,128)S(1)}) custom-call(s32[289]{0:T(512)S(1)} %pad_add_fusion.after_ref.table_ref, bf16[128,128]{1,0:T(8,128)(2,1)S(1)} %get-tuple-element.33.query_ref, ...), custom_call_target="tpu_custom_call" | custom-call | flops 4194304 | bytes 2097152 | tf_op jit(solution)/shard_map/pallas_call | solution.py:321
  19.8 1.6 %collective-permute-start.6 = (bf16[528,128]{1,0:T(8,128)(2,1)S(1)}, bf16[528,128]{1,0:T(8,128)(2,1)S(1)}, u32[]{:S(2)}, u32[]{:S(2)}) collective-permute-start(bf16[528,128]{1,0:T(8,128)(2,1)S(1)} %shard_map.117.after_ref), channel_id=1, source_target_pairs={{0,2},{1,3},{2,0},{3,1},{4,6},{5,7},{6,4},{7,5},{8,10},{9,11},{10,... | collective-permute-start | bytes 405512 | tf_op jit(solution)/shard_map/ppermute | solution.py:157
  21.4 4.0 %shard_map.118 = (bf16[4,512,1664]{2,1,0:T(8,128)(2,1)S(1)}, bf16[2,512,1664]{2,1,0:T(8,128)(2,1)S(1)}) custom-call(bf16[528,128]{1,0:T(8,128)(2,1)S(1)} %shard_map.117.after_ref, bf16[8192,1664]{1,0:T(8,128)(2,1)} %refs_6_.1, bf16[8192,1664]{1,0:T(8,128)(2,1)} %refs_7_.3), custom_call_target="tpu_custom_call" | custom-call | bytes 10223616 | tf_op jit(solution)/shard_map/pallas_call | solution.py:531
  25.6 3.7 %collective-permute-start.9 = (bf16[528,128]{1,0:T(8,128)(2,1)S(1)}, bf16[528,128]{1,0:T(8,128)(2,1)S(1)}, u32[]{:S(2)}, u32[]{:S(2)}) collective-permute-start(bf16[528,128]{1,0:T(8,128)(2,1)S(1)} %shard_map.119.after_ref.refs_0_), channel_id=1, source_target_pairs={{0,12},{1,13},{2,14},{3,15},{4,8},{5,9},{6,10},{7,11},{8,4},{9,5},... | collective-permute-start | bytes 405512 | tf_op jit(solution)/shard_map/ppermute | solution.py:157
  30.0 7.0 %shard_map.120 = (bf16[4,512,1664]{2,1,0:T(8,128)(2,1)S(1)}, bf16[4,512,1664]{2,1,0:T(8,128)(2,1)S(1)}, bf16[4,1664,512]{2,1,0:T(8,128)(2,1)S(1)}) custom-call(bf16[528,128]{1,0:T(8,128)(2,1)S(1)} %shard_map.119.after_ref.refs_0_, bf16[8192,1664]{1,0:T(8,128)(2,1)} %refs_7_.3, bf16[8192,1664]{1,0:T(8,128)(2,1)} %refs_7_.3, bf16[1664,8192]{1,0:T(8,128)(2,1)} %refs_8_.1), custom_call_target="tpu_custom_call" | custom-call | bytes 20447232 | tf_op jit(solution)/shard_map/pallas_call | solution.py:531
  37.0 3.3 %collective-permute-done.8.refs_2_ = bf16[528,128]{1,0:T(8,128)(2,1)S(1)} collective-permute-done((bf16[528,128]{1,0:T(8,128)(2,1)S(1)}, bf16[528,128]{1,0:T(8,128)(2,1)S(1)}, u32[]{:S(2)}, u32[]{:S(2)}) %collective-permute-start.8) | collective-permute-done | bytes 135200 | tf_op jit(solution)/shard_map/ppermute | solution.py:157
  41.7 3.7 %shard_map.122.refs_2_.held_ref = bf16[4,1664,512]{2,1,0:T(8,128)(2,1)S(1)} custom-call(bf16[4,128,128]{2,1,0:T(8,128)(2,1)S(1)} %shard_map.121.after_ref.refs_0_.near_ref, bf16[1664,8192]{1,0:T(8,128)(2,1)} %refs_8_.1), custom_call_target="tpu_custom_call" | custom-call | bytes 6815744 | tf_op jit(solution)/shard_map/pallas_call | solution.py:531
  45.8 1.5 %collective-permute-done.11.odd_ref = bf16[8,128,128]{2,1,0:T(8,128)(2,1)S(1)} collective-permute-done((bf16[8,128,128]{2,1,0:T(8,128)(2,1)S(1)}, bf16[8,128,128]{2,1,0:T(8,128)(2,1)S(1)}, u32[]{:S(2)}, u32[]{:S(2)}) %collective-permute-start.11) | collective-permute-done | bytes 262176 | tf_op jit(solution)/shard_map/ppermute | solution.py:157
  47.3 1.7 %shard_map.124.refs_0_.stream_ref = bf16[32,512]{1,0:T(8,128)(2,1)S(1)} custom-call(bf16[4,128,128]{2,1,0:T(8,128)(2,1)S(1)} %shard_map.121.after_ref.refs_0_.near_ref, bf16[4,128,128]{2,1,0:T(8,128)(2,1)S(1)} %collective-permute-done.10.refs_1_.second_ref, bf16[8,128,128]{2,1,0:T(8,128)(2,1)S(1)} %collective-permute-done.11.odd_ref, ...), custom_call_target="tpu_custom_call" | custom-call | flops 268435456 | bytes 8388608 | tf_op jit(solution)/shard_map/pallas_call | solution.py:590
  49.0 2.4 %collective-permute-start.14 = (bf16[32,512]{1,0:T(8,128)(2,1)S(1)}, bf16[32,512]{1,0:T(8,128)(2,1)S(1)}, u32[]{:S(2)}, u32[]{:S(2)}) collective-permute-start(bf16[32,512]{1,0:T(8,128)(2,1)S(1)} %shard_map.124.refs_0_.stream_ref), channel_id=1, source_target_pairs={{0,12},{1,13},{2,14},{3,15},{4,8},{5,9},{6,10},{7,11},{8,4},{9,5},... | collective-permute-start | bytes 98312 | tf_op jit(solution)/shard_map/ppermute | solution.py:157
  51.4 2.0 %collective-permute-start.12 = (bf16[32,512]{1,0:T(8,128)(2,1)S(1)}, bf16[32,512]{1,0:T(8,128)(2,1)S(1)}, u32[]{:S(2)}, u32[]{:S(2)}) collective-permute-start(bf16[32,512]{1,0:T(8,128)(2,1)S(1)} %shard_map.124.refs_0_.stream_ref), channel_id=1, source_target_pairs={{0,4},{1,5},{2,6},{3,7},{4,0},{5,1},{6,2},{7,3},{8,12},{9,13},{10,... | collective-permute-start | bytes 98312 | tf_op jit(solution)/shard_map/ppermute | solution.py:157
  53.4 2.4 %shard_map.125 = (f32[32,1664]{1,0:T(8,128)S(1)}, f32[32,1664]{1,0:T(8,128)S(1)}, f32[32,512]{1,0:T(8,128)S(1)}) custom-call(bf16[32,512]{1,0:T(8,128)(2,1)S(1)} %shard_map.124.refs_0_.stream_ref, bf16[4,144,128]{2,1,0:T(8,128)(2,1)S(1)} %shard_map.111.after_ref.refs_0_.refs_1_.refs_3_, bf16[8192,1664]{1,0:T(8,128)(2,1)} %refs_6_.1, bf16[8192,1664]{1,0:T(8,128)(2,1)} %refs_7_.3), custom_call_target="tpu_custom_call" | custom-call | flops 109051904 | bytes 3407872 | tf_op jit(solution)/shard_map/pallas_call | solution.py:694
  56.3 1.2 %collective-permute-start.15 = (bf16[4,32,512]{2,1,0:T(8,128)(2,1)S(1)}, bf16[4,32,512]{2,1,0:T(8,128)(2,1)S(1)}, u32[]{:S(2)}, u32[]{:S(2)}) collective-permute-start(bf16[4,32,512]{2,1,0:T(8,128)(2,1)S(1)} %shard_map.126.refs_0_), channel_id=1, source_target_pairs={{0,2},{1,3},{2,0},{3,1},{4,6},{5,7},{6,4},{7,5},{8,10},{9,11},{10,... | collective-permute-start | bytes 393224 | tf_op jit(solution)/shard_map/ppermute | solution.py:157
  57.4 4.4 %shard_map.127 = (f32[32,1664]{1,0:T(8,128)S(1)}, f32[32,1664]{1,0:T(8,128)S(1)}, f32[32,512]{1,0:T(8,128)S(1)}) custom-call(bf16[32,512]{1,0:T(8,128)(2,1)S(1)} %collective-permute-done.12.refs_1_.refs_0_, bf16[32,512]{1,0:T(8,128)(2,1)S(1)} %collective-permute-done.13.refs_2_.refs_1_, bf16[32,512]{1,0:T(8,128)(2,1)S(1)} %collective-permute-done.14.refs_3_.refs_2_, ...), custom_call_target="tpu_custom_call" | custom-call | flops 327155712 | bytes 10223616 | tf_op jit(solution)/shard_map/pallas_call | solution.py:694
  62.0 2.2 %shard_map.129 = (f32[32,1664]{1,0:T(8,128)S(1)}, f32[32,1664]{1,0:T(8,128)S(1)}, f32[32,512]{1,0:T(8,128)S(1)}, bf16[2,512,1664]{2,1,0:T(8,128)(2,1)S(1)}) custom-call(bf16[4,32,512]{2,1,0:T(8,128)(2,1)S(1)} %collective-permute-done.15.refs_1_.refs_0_, bf16[4,144,128]{2,1,0:T(8,128)(2,1)S(1)} %collective-permute-done.3.refs_1_, ...), custom_call_target="tpu_custom_call" | custom-call | flops 436207616 | bytes 13631488 | tf_op jit(solution)/shard_map/pallas_call | solution.py:694
  64.2 8.1 %shard_map.130 = (bf16[32,1664]{1,0:T(8,128)(2,1)S(1)}, bf16[8,32,512]{2,1,0:T(8,128)(2,1)S(1)}) custom-call(bf16[8,32,512]{2,1,0:T(8,128)(2,1)S(1)} %collective-permute-done.16.refs_0_, bf16[8,144,128]{2,1,0:T(8,128)(2,1)S(1)} %collective-permute-done.4.refs_0_.refs_1_, bf16[3,512,1664]{2,1,0:T(8,128)(2,1)S(1)} %shard_map.110.refs_4_.refs_2_, ...), custom_call_target="tpu_custom_call" | custom-call | flops 1308622848 | bytes 40894464 | tf_op jit(solution)/shard_map/pallas_call | solution.py:778
  76.2 3.9 %collective-permute-done.18.arrived_ref = bf16[4,32,512]{2,1,0:T(8,128)(2,1)S(1)} collective-permute-done((bf16[4,32,512]{2,1,0:T(8,128)(2,1)S(1)}, bf16[4,32,512]{2,1,0:T(8,128)(2,1)S(1)}, u32[]{:S(2)}, u32[]{:S(2)}) %collective-permute-start.18) | collective-permute-done | bytes 131104 | tf_op jit(solution)/shard_map/ppermute | solution.py:157
  80.1 2.1 %collective-permute-start.19 = (bf16[32,512]{1,0:T(8,128)(2,1)S(1)}, bf16[32,512]{1,0:T(8,128)(2,1)S(1)}, u32[]{:S(2)}, u32[]{:S(2)}) collective-permute-start(bf16[32,512]{1,0:T(8,128)(2,1)S(1)} %get-tuple-element.57), channel_id=1, source_target_pairs={{0,12},{1,13},{2,14},{3,15},{4,8},{5,9},{6,10},{7,11},{8,4},{9,5},... | collective-permute-start | bytes 98312 | tf_op jit(solution)/shard_map/ppermute | solution.py:157
  82.6 1.9 %collective-permute-start.21 = (bf16[32,512]{1,0:T(8,128)(2,1)S(1)}, bf16[32,512]{1,0:T(8,128)(2,1)S(1)}, u32[]{:S(2)}, u32[]{:S(2)}) collective-permute-start(bf16[32,512]{1,0:T(8,128)(2,1)S(1)} %get-tuple-element.59), channel_id=1, source_target_pairs={{0,4},{1,5},{2,6},{3,7},{4,0},{5,1},{6,2},{7,3},{8,12},{9,13},{10,... | collective-permute-start | bytes 98312 | tf_op jit(solution)/shard_map/ppermute | solution.py:157
  84.5 1.3 %collective-permute-done.19.refs_0_ = bf16[32,512]{1,0:T(8,128)(2,1)S(1)} collective-permute-done((bf16[32,512]{1,0:T(8,128)(2,1)S(1)}, bf16[32,512]{1,0:T(8,128)(2,1)S(1)}, u32[]{:S(2)}, u32[]{:S(2)}) %collective-permute-start.19) | collective-permute-done | bytes 32800 | tf_op jit(solution)/shard_map/ppermute | solution.py:157
  85.9 1.5 %collective-permute-done.20.refs_1_ = bf16[32,512]{1,0:T(8,128)(2,1)S(1)} collective-permute-done((bf16[32,512]{1,0:T(8,128)(2,1)S(1)}, bf16[32,512]{1,0:T(8,128)(2,1)S(1)}, u32[]{:S(2)}, u32[]{:S(2)}) %collective-permute-start.20) | collective-permute-done | bytes 32800 | tf_op jit(solution)/shard_map/ppermute | solution.py:157
  (64 shorter events, 15.1 us)
Async XLA Ops:
  0.8 9.9 %collective-permute-start.2 = (bf16[144,128]{1,0:T(8,128)(2,1)S(1)}, bf16[144,128]{1,0:T(8,128)(2,1)S(1)}, u32[]{:S(2)}, u32[]{:S(2)}) collective-permute-start(bf16[144,128]{1,0:T(8,128)(2,1)S(1)} %get-tuple-element.34.refs_0_), channel_id=1, source_target_pairs={{0,12},{1,13},{2,14},{3,15},{4,8},{5,9},{6,10},{7,11},{8,4},{9,5},... | collective-permute-start | bytes 110600 | tf_op jit(solution)/shard_map/ppermute | solution.py:157
  6.0 4.9 %collective-permute-start.1 = (bf16[144,128]{1,0:T(8,128)(2,1)S(1)}, bf16[144,128]{1,0:T(8,128)(2,1)S(1)}, u32[]{:S(2)}, u32[]{:S(2)}) collective-permute-start(bf16[144,128]{1,0:T(8,128)(2,1)S(1)} %get-tuple-element.34.refs_0_), channel_id=1, source_target_pairs={{0,8},{1,9},{2,10},{3,11},{4,12},{5,13},{6,14},{7,15},{8,0},{9,1},... | collective-permute-start | bytes 110600 | tf_op jit(solution)/shard_map/ppermute | solution.py:157
  6.0 4.9 %collective-permute-start = (bf16[144,128]{1,0:T(8,128)(2,1)S(1)}, bf16[144,128]{1,0:T(8,128)(2,1)S(1)}, u32[]{:S(2)}, u32[]{:S(2)}) collective-permute-start(bf16[144,128]{1,0:T(8,128)(2,1)S(1)} %get-tuple-element.34.refs_0_), channel_id=1, source_target_pairs={{0,4},{1,5},{2,6},{3,7},{4,0},{5,1},{6,2},{7,3},{8,12},{9,13},{10,... | collective-permute-start | bytes 110600 | tf_op jit(solution)/shard_map/ppermute | solution.py:157
  10.8 5.2 %collective-permute-start.3 = (bf16[4,144,128]{2,1,0:T(8,128)(2,1)S(1)}, bf16[4,144,128]{2,1,0:T(8,128)(2,1)S(1)}, u32[]{:S(2)}, u32[]{:S(2)}) collective-permute-start(bf16[4,144,128]{2,1,0:T(8,128)(2,1)S(1)} %shard_map.111.after_ref.refs_0_.refs_1_.refs_3_), channel_id=1, source_target_pairs={{0,2},{1,3},{2,0},{3,1},{4,6},{5,7},{6,4},{7,5},{8,10},{9,11},{10,... | collective-permute-start | bytes 442376 | tf_op jit(solution)/shard_map/ppermute | solution.py:157
  16.1 1.6 %collective-permute-start.4 = (bf16[8,144,128]{2,1,0:T(8,128)(2,1)S(1)}, bf16[8,144,128]{2,1,0:T(8,128)(2,1)S(1)}, u32[]{:S(2)}, u32[]{:S(2)}) collective-permute-start(bf16[8,144,128]{2,1,0:T(8,128)(2,1)S(1)} %shard_map.114), channel_id=1, source_target_pairs={{0,1},{1,0},{2,3},{3,2},{4,5},{5,4},{6,7},{7,6},{8,9},{9,8},{10,11... | collective-permute-start | bytes 884744 | tf_op jit(solution)/shard_map/ppermute | solution.py:157
  18.3 1.4 %collective-permute-start.5 = (bf16[528,128]{1,0:T(8,128)(2,1)S(1)}, bf16[528,128]{1,0:T(8,128)(2,1)S(1)}, u32[]{:S(2)}, u32[]{:S(2)}) collective-permute-start(bf16[528,128]{1,0:T(8,128)(2,1)S(1)} %shard_map.115), channel_id=1, source_target_pairs={{0,1},{1,0},{2,3},{3,2},{4,5},{5,4},{6,7},{7,6},{8,9},{9,8},{10,11... | collective-permute-start | bytes 405512 | tf_op jit(solution)/shard_map/ppermute | solution.py:157
  19.8 5.6 %collective-permute-start.6 = (bf16[528,128]{1,0:T(8,128)(2,1)S(1)}, bf16[528,128]{1,0:T(8,128)(2,1)S(1)}, u32[]{:S(2)}, u32[]{:S(2)}) collective-permute-start(bf16[528,128]{1,0:T(8,128)(2,1)S(1)} %shard_map.117.after_ref), channel_id=1, source_target_pairs={{0,2},{1,3},{2,0},{3,1},{4,6},{5,7},{6,4},{7,5},{8,10},{9,11},{10,... | collective-permute-start | bytes 405512 | tf_op jit(solution)/shard_map/ppermute | solution.py:157
  25.6 11.4 %collective-permute-start.9 = (bf16[528,128]{1,0:T(8,128)(2,1)S(1)}, bf16[528,128]{1,0:T(8,128)(2,1)S(1)}, u32[]{:S(2)}, u32[]{:S(2)}) collective-permute-start(bf16[528,128]{1,0:T(8,128)(2,1)S(1)} %shard_map.119.after_ref.refs_0_), channel_id=1, source_target_pairs={{0,12},{1,13},{2,14},{3,15},{4,8},{5,9},{6,10},{7,11},{8,4},{9,5},... | collective-permute-start | bytes 405512 | tf_op jit(solution)/shard_map/ppermute | solution.py:157
  29.2 11.0 %collective-permute-start.8 = (bf16[528,128]{1,0:T(8,128)(2,1)S(1)}, bf16[528,128]{1,0:T(8,128)(2,1)S(1)}, u32[]{:S(2)}, u32[]{:S(2)}) collective-permute-start(bf16[528,128]{1,0:T(8,128)(2,1)S(1)} %shard_map.119.after_ref.refs_0_), channel_id=1, source_target_pairs={{0,8},{1,9},{2,10},{3,11},{4,12},{5,13},{6,14},{7,15},{8,0},{9,1},... | collective-permute-start | bytes 405512 | tf_op jit(solution)/shard_map/ppermute | solution.py:157
  29.3 11.0 %collective-permute-start.7 = (bf16[528,128]{1,0:T(8,128)(2,1)S(1)}, bf16[528,128]{1,0:T(8,128)(2,1)S(1)}, u32[]{:S(2)}, u32[]{:S(2)}) collective-permute-start(bf16[528,128]{1,0:T(8,128)(2,1)S(1)} %shard_map.119.after_ref.refs_0_), channel_id=1, source_target_pairs={{0,4},{1,5},{2,6},{3,7},{4,0},{5,1},{6,2},{7,3},{8,12},{9,13},{10,... | collective-permute-start | bytes 405512 | tf_op jit(solution)/shard_map/ppermute | solution.py:157
  40.6 5.0 %collective-permute-start.10 = (bf16[4,128,128]{2,1,0:T(8,128)(2,1)S(1)}, bf16[4,128,128]{2,1,0:T(8,128)(2,1)S(1)}, u32[]{:S(2)}, u32[]{:S(2)}) collective-permute-start(bf16[4,128,128]{2,1,0:T(8,128)(2,1)S(1)} %shard_map.121.after_ref.refs_0_.near_ref), channel_id=1, source_target_pairs={{0,2},{1,3},{2,0},{3,1},{4,6},{5,7},{6,4},{7,5},{8,10},{9,11},{10,... | collective-permute-start | bytes 393224 | tf_op jit(solution)/shard_map/ppermute | solution.py:157
  45.7 1.6 %collective-permute-start.11 = (bf16[8,128,128]{2,1,0:T(8,128)(2,1)S(1)}, bf16[8,128,128]{2,1,0:T(8,128)(2,1)S(1)}, u32[]{:S(2)}, u32[]{:S(2)}) collective-permute-start(bf16[8,128,128]{2,1,0:T(8,128)(2,1)S(1)} %shard_map.123), channel_id=1, source_target_pairs={{0,1},{1,0},{2,3},{3,2},{4,5},{5,4},{6,7},{7,6},{8,9},{9,8},{10,11... | collective-permute-start | bytes 786440 | tf_op jit(solution)/shard_map/ppermute | solution.py:157
  49.0 6.8 %collective-permute-start.14 = (bf16[32,512]{1,0:T(8,128)(2,1)S(1)}, bf16[32,512]{1,0:T(8,128)(2,1)S(1)}, u32[]{:S(2)}, u32[]{:S(2)}) collective-permute-start(bf16[32,512]{1,0:T(8,128)(2,1)S(1)} %shard_map.124.refs_0_.stream_ref), channel_id=1, source_target_pairs={{0,12},{1,13},{2,14},{3,15},{4,8},{5,9},{6,10},{7,11},{8,4},{9,5},... | collective-permute-start | bytes 98312 | tf_op jit(solution)/shard_map/ppermute | solution.py:157
  51.4 4.8 %collective-permute-start.13 = (bf16[32,512]{1,0:T(8,128)(2,1)S(1)}, bf16[32,512]{1,0:T(8,128)(2,1)S(1)}, u32[]{:S(2)}, u32[]{:S(2)}) collective-permute-start(bf16[32,512]{1,0:T(8,128)(2,1)S(1)} %shard_map.124.refs_0_.stream_ref), channel_id=1, source_target_pairs={{0,8},{1,9},{2,10},{3,11},{4,12},{5,13},{6,14},{7,15},{8,0},{9,1},... | collective-permute-start | bytes 98312 | tf_op jit(solution)/shard_map/ppermute | solution.py:157
  51.4 4.8 %collective-permute-start.12 = (bf16[32,512]{1,0:T(8,128)(2,1)S(1)}, bf16[32,512]{1,0:T(8,128)(2,1)S(1)}, u32[]{:S(2)}, u32[]{:S(2)}) collective-permute-start(bf16[32,512]{1,0:T(8,128)(2,1)S(1)} %shard_map.124.refs_0_.stream_ref), channel_id=1, source_target_pairs={{0,4},{1,5},{2,6},{3,7},{4,0},{5,1},{6,2},{7,3},{8,12},{9,13},{10,... | collective-permute-start | bytes 98312 | tf_op jit(solution)/shard_map/ppermute | solution.py:157
  56.3 5.6 %collective-permute-start.15 = (bf16[4,32,512]{2,1,0:T(8,128)(2,1)S(1)}, bf16[4,32,512]{2,1,0:T(8,128)(2,1)S(1)}, u32[]{:S(2)}, u32[]{:S(2)}) collective-permute-start(bf16[4,32,512]{2,1,0:T(8,128)(2,1)S(1)} %shard_map.126.refs_0_), channel_id=1, source_target_pairs={{0,2},{1,3},{2,0},{3,1},{4,6},{5,7},{6,4},{7,5},{8,10},{9,11},{10,... | collective-permute-start | bytes 393224 | tf_op jit(solution)/shard_map/ppermute | solution.py:157
  61.9 2.3 %collective-permute-start.16 = (bf16[8,32,512]{2,1,0:T(8,128)(2,1)S(1)}, bf16[8,32,512]{2,1,0:T(8,128)(2,1)S(1)}, u32[]{:S(2)}, u32[]{:S(2)}) collective-permute-start(bf16[8,32,512]{2,1,0:T(8,128)(2,1)S(1)} %shard_map.128), channel_id=1, source_target_pairs={{0,1},{1,0},{2,3},{3,2},{4,5},{5,4},{6,7},{7,6},{8,9},{9,8},{10,11... | collective-permute-start | bytes 786440 | tf_op jit(solution)/shard_map/ppermute | solution.py:157
  62.0 10.9 %slice-start.2 = ((s8[6815744]{0:T(1024)(128)(4,1)}), s8[2621440]{0:T(1024)(128)(4,1)S(1)}, s32[]{:S(2)}) async-start(s8[6815744]{0:T(1024)(128)(4,1)} %bitcast.4), calls=%async_computation.2 | async-start | bytes 5242880
  64.2 8.8 %slice-start.3 = ((s8[6815744]{0:T(1024)(128)(4,1)}), s8[4194304]{0:T(1024)(128)(4,1)S(1)}, s32[]{:S(2)}) async-start(s8[6815744]{0:T(1024)(128)(4,1)} %bitcast.4), calls=%async_computation.3 | async-start | bytes 8388608
  72.3 1.8 %collective-permute-start.17 = (bf16[8,32,512]{2,1,0:T(8,128)(2,1)S(1)}, bf16[8,32,512]{2,1,0:T(8,128)(2,1)S(1)}, u32[]{:S(2)}, u32[]{:S(2)}) collective-permute-start(bf16[8,32,512]{2,1,0:T(8,128)(2,1)S(1)} %get-tuple-element.55), channel_id=1, source_target_pairs={{0,1},{1,0},{2,3},{3,2},{4,5},{5,4},{6,7},{7,6},{8,9},{9,8},{10,11... | collective-permute-start | bytes 786440 | tf_op jit(solution)/shard_map/ppermute | solution.py:157
  74.1 5.9 %collective-permute-start.18 = (bf16[4,32,512]{2,1,0:T(8,128)(2,1)S(1)}, bf16[4,32,512]{2,1,0:T(8,128)(2,1)S(1)}, u32[]{:S(2)}, u32[]{:S(2)}) collective-permute-start(bf16[4,32,512]{2,1,0:T(8,128)(2,1)S(1)} %shard_map.133), channel_id=1, source_target_pairs={{0,2},{1,3},{2,0},{3,1},{4,6},{5,7},{6,4},{7,5},{8,10},{9,11},{10,... | collective-permute-start | bytes 393224 | tf_op jit(solution)/shard_map/ppermute | solution.py:157
  80.1 5.8 %collective-permute-start.19 = (bf16[32,512]{1,0:T(8,128)(2,1)S(1)}, bf16[32,512]{1,0:T(8,128)(2,1)S(1)}, u32[]{:S(2)}, u32[]{:S(2)}) collective-permute-start(bf16[32,512]{1,0:T(8,128)(2,1)S(1)} %get-tuple-element.57), channel_id=1, source_target_pairs={{0,12},{1,13},{2,14},{3,15},{4,8},{5,9},{6,10},{7,11},{8,4},{9,5},... | collective-permute-start | bytes 98312 | tf_op jit(solution)/shard_map/ppermute | solution.py:157
  82.2 5.2 %collective-permute-start.20 = (bf16[32,512]{1,0:T(8,128)(2,1)S(1)}, bf16[32,512]{1,0:T(8,128)(2,1)S(1)}, u32[]{:S(2)}, u32[]{:S(2)}) collective-permute-start(bf16[32,512]{1,0:T(8,128)(2,1)S(1)} %get-tuple-element.58), channel_id=1, source_target_pairs={{0,8},{1,9},{2,10},{3,11},{4,12},{5,13},{6,14},{7,15},{8,0},{9,1},... | collective-permute-start | bytes 98312 | tf_op jit(solution)/shard_map/ppermute | solution.py:157
  82.6 4.7 %collective-permute-start.21 = (bf16[32,512]{1,0:T(8,128)(2,1)S(1)}, bf16[32,512]{1,0:T(8,128)(2,1)S(1)}, u32[]{:S(2)}, u32[]{:S(2)}) collective-permute-start(bf16[32,512]{1,0:T(8,128)(2,1)S(1)} %get-tuple-element.59), channel_id=1, source_target_pairs={{0,4},{1,5},{2,6},{3,7},{4,0},{5,1},{6,2},{7,3},{8,12},{9,13},{10,... | collective-permute-start | bytes 98312 | tf_op jit(solution)/shard_map/ppermute | solution.py:157
  (4 other events, 23.9 us)

commit v6 on v5

--- a/solution.py
+++ b/solution.py
@@ -178,7 +178,8 @@
 
 
 def near_pieces(piece):
-    return [piece] + [sent(piece, distance) for distance in (4, 8, 12)]
+    sends = {distance: sent(piece, distance) for distance in (8, 12, 4)}
+    return [piece] + [sends[distance] for distance in (4, 8, 12)]
 
 
 def device_at(me, entry):
@@ -677,7 +678,8 @@
     for place in range(len(entries)):
         for number, (total, start, blocks) in enumerate(both):
             copies[number](place).wait()
-            terms = jnp.dot(lefts[place], blocks[place], preferred_element_type=jnp.float32)
+            here = lambda cols: blocks[place, :, cols]
+            terms = product(lefts[place], here, blocks.shape[-1])
             if place > 0:
                 total[...] += terms
             else:

time: 88.3 us -> 88.2 us (level)
  no operation moved by 1% of the time
where the time goes in v6:
time: 88.2 us; the launch traced here: 87.9 us
  Pallas kernels  45.4 us (51%)
  starting transfers between devices  26.4 us (30%)
  waiting for transfers between devices  14.1 us (16%)
  local copies, waits for them, and re-layouts  1.02 us (1%)
    ppermute x22, starting transfers between devices, sent(): lax.ppermute(array, 'shard', [(i, i ^ distance) for i in range(size)])  26.4 us
    pallas_call x4, Pallas kernels, fetched(): pl.pallas_call(functools.partial(fetch_kernel, [part[1:] for part in part...  17.3 us
    ppermute x22, waiting for transfers between devices, sent(): lax.ppermute(array, 'shard', [(i, i ^ distance) for i in range(size)])  14.1 us
    pallas_call x3, Pallas kernels, feed(): pl.pallas_call(functools.partial(feed_kernel, entries, len(pieces), held,...  8.89 us
    pallas_call x1, Pallas kernels, hidden_units(): pl.pallas_call(functools.partial(hidden_kernel, entries, [len(parts) for...  8.13 us
    pallas_call x1, Pallas kernels, readied(): pl.pallas_call(ready_kernel, in_specs=[SMEM_SPEC, VMEM_SPEC] + [HBM_SPEC]...  3.53 us
    pallas_call x2, Pallas kernels, down_terms(): pl.pallas_call(down_kernel, in_specs=[VMEM_SPEC] * 2, out_specs=VMEM_SPEC...  2.15 us
  transfers between devices with their start and end apart: 22, of which 10 were waited for; matrix products, arithmetic and copies ran while one was open for 2% of the time, Pallas kernels for 37%

profile of v6, /device:TPU:0, one launch (start us, length us, event | category | flops | bytes accessed | tf_op | source)
XLA Modules:
  0.0 87.9 jit_solution(6633817199524662911)
XLA Ops:
  0.8 5.1 %collective-permute-start.2 = (bf16[144,128]{1,0:T(8,128)(2,1)S(1)}, bf16[144,128]{1,0:T(8,128)(2,1)S(1)}, u32[]{:S(2)}, u32[]{:S(2)}) collective-permute-start(bf16[144,128]{1,0:T(8,128)(2,1)S(1)} %get-tuple-element.34.refs_0_), channel_id=1, source_target_pairs={{0,12},{1,13},{2,14},{3,15},{4,8},{5,9},{6,10},{7,11},{8,4},{9,5},... | collective-permute-start | bytes 110600 | tf_op jit(solution)/shard_map/ppermute | solution.py:157
  8.2 2.5 %shard_map.110.refs_4_.refs_2_ = bf16[3,512,1664]{2,1,0:T(8,128)(2,1)S(1)} custom-call(s32[289]{0:T(512)S(1)} %pad_add_fusion.after_ref.table_ref, bf16[8192,1664]{1,0:T(8,128)(2,1)} %refs_6_.1), custom_call_target="tpu_custom_call" | custom-call | bytes 5111808 | tf_op jit(solution)/shard_map/pallas_call | solution.py:532
  10.8 1.6 %collective-permute-start.3 = (bf16[4,144,128]{2,1,0:T(8,128)(2,1)S(1)}, bf16[4,144,128]{2,1,0:T(8,128)(2,1)S(1)}, u32[]{:S(2)}, u32[]{:S(2)}) collective-permute-start(bf16[4,144,128]{2,1,0:T(8,128)(2,1)S(1)} %shard_map.111.after_ref.refs_0_.refs_1_.refs_3_), channel_id=1, source_target_pairs={{0,2},{1,3},{2,0},{3,1},{4,6},{5,7},{6,4},{7,5},{8,10},{9,11},{10,... | collective-permute-start | bytes 442376 | tf_op jit(solution)/shard_map/ppermute | solution.py:157
  12.5 3.5 %shard_map.112 = (bf16[16,2,32,512]{3,2,1,0:T(8,128)(2,1)S(1)}, s32[16,128]{1,0:T(8,128)S(1)}, s32[32,128]{1,0:T(8,128)S(1)}, f32[128,128]{1,0:T(8,128)S(1)}, f32[16,64]{1,0:T(8,128)S(1)}) custom-call(s32[289]{0:T(512)S(1)} %pad_add_fusion.after_ref.table_ref, bf16[128,128]{1,0:T(8,128)(2,1)S(1)} %get-tuple-element.33.query_ref, ...), custom_call_target="tpu_custom_call" | custom-call | flops 4194304 | bytes 2097152 | tf_op jit(solution)/shard_map/pallas_call | solution.py:322
  19.8 1.6 %collective-permute-start.6 = (bf16[528,128]{1,0:T(8,128)(2,1)S(1)}, bf16[528,128]{1,0:T(8,128)(2,1)S(1)}, u32[]{:S(2)}, u32[]{:S(2)}) collective-permute-start(bf16[528,128]{1,0:T(8,128)(2,1)S(1)} %shard_map.117.after_ref), channel_id=1, source_target_pairs={{0,2},{1,3},{2,0},{3,1},{4,6},{5,7},{6,4},{7,5},{8,10},{9,11},{10,... | collective-permute-start | bytes 405512 | tf_op jit(solution)/shard_map/ppermute | solution.py:157
  21.4 4.0 %shard_map.118 = (bf16[4,512,1664]{2,1,0:T(8,128)(2,1)S(1)}, bf16[2,512,1664]{2,1,0:T(8,128)(2,1)S(1)}) custom-call(bf16[528,128]{1,0:T(8,128)(2,1)S(1)} %shard_map.117.after_ref, bf16[8192,1664]{1,0:T(8,128)(2,1)} %refs_6_.1, bf16[8192,1664]{1,0:T(8,128)(2,1)} %refs_7_.3), custom_call_target="tpu_custom_call" | custom-call | bytes 10223616 | tf_op jit(solution)/shard_map/pallas_call | solution.py:532
  25.6 3.7 %collective-permute-start.9 = (bf16[528,128]{1,0:T(8,128)(2,1)S(1)}, bf16[528,128]{1,0:T(8,128)(2,1)S(1)}, u32[]{:S(2)}, u32[]{:S(2)}) collective-permute-start(bf16[528,128]{1,0:T(8,128)(2,1)S(1)} %shard_map.119.after_ref.refs_0_), channel_id=1, source_target_pairs={{0,12},{1,13},{2,14},{3,15},{4,8},{5,9},{6,10},{7,11},{8,4},{9,5},... | collective-permute-start | bytes 405512 | tf_op jit(solution)/shard_map/ppermute | solution.py:157
  30.0 7.0 %shard_map.120 = (bf16[4,512,1664]{2,1,0:T(8,128)(2,1)S(1)}, bf16[4,512,1664]{2,1,0:T(8,128)(2,1)S(1)}, bf16[4,1664,512]{2,1,0:T(8,128)(2,1)S(1)}) custom-call(bf16[528,128]{1,0:T(8,128)(2,1)S(1)} %shard_map.119.after_ref.refs_0_, bf16[8192,1664]{1,0:T(8,128)(2,1)} %refs_7_.3, bf16[8192,1664]{1,0:T(8,128)(2,1)} %refs_7_.3, bf16[1664,8192]{1,0:T(8,128)(2,1)} %refs_8_.1), custom_call_target="tpu_custom_call" | custom-call | bytes 20447232 | tf_op jit(solution)/shard_map/pallas_call | solution.py:532
  37.0 3.3 %collective-permute-done.8.refs_2_ = bf16[528,128]{1,0:T(8,128)(2,1)S(1)} collective-permute-done((bf16[528,128]{1,0:T(8,128)(2,1)S(1)}, bf16[528,128]{1,0:T(8,128)(2,1)S(1)}, u32[]{:S(2)}, u32[]{:S(2)}) %collective-permute-start.8) | collective-permute-done | bytes 135200 | tf_op jit(solution)/shard_map/ppermute | solution.py:157
  41.7 3.7 %shard_map.122.refs_2_.held_ref = bf16[4,1664,512]{2,1,0:T(8,128)(2,1)S(1)} custom-call(bf16[4,128,128]{2,1,0:T(8,128)(2,1)S(1)} %shard_map.121.after_ref.refs_0_.near_ref, bf16[1664,8192]{1,0:T(8,128)(2,1)} %refs_8_.1), custom_call_target="tpu_custom_call" | custom-call | bytes 6815744 | tf_op jit(solution)/shard_map/pallas_call | solution.py:532
  45.8 1.5 %collective-permute-done.11.odd_ref = bf16[8,128,128]{2,1,0:T(8,128)(2,1)S(1)} collective-permute-done((bf16[8,128,128]{2,1,0:T(8,128)(2,1)S(1)}, bf16[8,128,128]{2,1,0:T(8,128)(2,1)S(1)}, u32[]{:S(2)}, u32[]{:S(2)}) %collective-permute-start.11) | collective-permute-done | bytes 262176 | tf_op jit(solution)/shard_map/ppermute | solution.py:157
  47.3 1.7 %shard_map.124.refs_0_.stream_ref = bf16[32,512]{1,0:T(8,128)(2,1)S(1)} custom-call(bf16[4,128,128]{2,1,0:T(8,128)(2,1)S(1)} %shard_map.121.after_ref.refs_0_.near_ref, bf16[4,128,128]{2,1,0:T(8,128)(2,1)S(1)} %collective-permute-done.10.refs_1_.second_ref, bf16[8,128,128]{2,1,0:T(8,128)(2,1)S(1)} %collective-permute-done.11.odd_ref, ...), custom_call_target="tpu_custom_call" | custom-call | flops 268435456 | bytes 8388608 | tf_op jit(solution)/shard_map/pallas_call | solution.py:591
  49.0 2.4 %collective-permute-start.14 = (bf16[32,512]{1,0:T(8,128)(2,1)S(1)}, bf16[32,512]{1,0:T(8,128)(2,1)S(1)}, u32[]{:S(2)}, u32[]{:S(2)}) collective-permute-start(bf16[32,512]{1,0:T(8,128)(2,1)S(1)} %shard_map.124.refs_0_.stream_ref), channel_id=1, source_target_pairs={{0,12},{1,13},{2,14},{3,15},{4,8},{5,9},{6,10},{7,11},{8,4},{9,5},... | collective-permute-start | bytes 98312 | tf_op jit(solution)/shard_map/ppermute | solution.py:157
  51.4 2.0 %collective-permute-start.12 = (bf16[32,512]{1,0:T(8,128)(2,1)S(1)}, bf16[32,512]{1,0:T(8,128)(2,1)S(1)}, u32[]{:S(2)}, u32[]{:S(2)}) collective-permute-start(bf16[32,512]{1,0:T(8,128)(2,1)S(1)} %shard_map.124.refs_0_.stream_ref), channel_id=1, source_target_pairs={{0,4},{1,5},{2,6},{3,7},{4,0},{5,1},{6,2},{7,3},{8,12},{9,13},{10,... | collective-permute-start | bytes 98312 | tf_op jit(solution)/shard_map/ppermute | solution.py:157
  53.4 2.4 %shard_map.125 = (f32[32,1664]{1,0:T(8,128)S(1)}, f32[32,1664]{1,0:T(8,128)S(1)}, f32[32,512]{1,0:T(8,128)S(1)}) custom-call(bf16[32,512]{1,0:T(8,128)(2,1)S(1)} %shard_map.124.refs_0_.stream_ref, bf16[4,144,128]{2,1,0:T(8,128)(2,1)S(1)} %shard_map.111.after_ref.refs_0_.refs_1_.refs_3_, bf16[8192,1664]{1,0:T(8,128)(2,1)} %refs_6_.1, bf16[8192,1664]{1,0:T(8,128)(2,1)} %refs_7_.3), custom_call_target="tpu_custom_call" | custom-call | flops 109051904 | bytes 3407872 | tf_op jit(solution)/shard_map/pallas_call | solution.py:696
  56.3 1.2 %collective-permute-start.15 = (bf16[4,32,512]{2,1,0:T(8,128)(2,1)S(1)}, bf16[4,32,512]{2,1,0:T(8,128)(2,1)S(1)}, u32[]{:S(2)}, u32[]{:S(2)}) collective-permute-start(bf16[4,32,512]{2,1,0:T(8,128)(2,1)S(1)} %shard_map.126.refs_0_), channel_id=1, source_target_pairs={{0,2},{1,3},{2,0},{3,1},{4,6},{5,7},{6,4},{7,5},{8,10},{9,11},{10,... | collective-permute-start | bytes 393224 | tf_op jit(solution)/shard_map/ppermute | solution.py:157
  57.4 4.4 %shard_map.127 = (f32[32,1664]{1,0:T(8,128)S(1)}, f32[32,1664]{1,0:T(8,128)S(1)}, f32[32,512]{1,0:T(8,128)S(1)}) custom-call(bf16[32,512]{1,0:T(8,128)(2,1)S(1)} %collective-permute-done.12.refs_1_.refs_0_, bf16[32,512]{1,0:T(8,128)(2,1)S(1)} %collective-permute-done.13.refs_2_.refs_1_, bf16[32,512]{1,0:T(8,128)(2,1)S(1)} %collective-permute-done.14.refs_3_.refs_2_, ...), custom_call_target="tpu_custom_call" | custom-call | flops 327155712 | bytes 10223616 | tf_op jit(solution)/shard_map/pallas_call | solution.py:696
  61.9 2.2 %shard_map.129 = (f32[32,1664]{1,0:T(8,128)S(1)}, f32[32,1664]{1,0:T(8,128)S(1)}, f32[32,512]{1,0:T(8,128)S(1)}, bf16[2,512,1664]{2,1,0:T(8,128)(2,1)S(1)}) custom-call(bf16[4,32,512]{2,1,0:T(8,128)(2,1)S(1)} %collective-permute-done.15.refs_1_.refs_0_, bf16[4,144,128]{2,1,0:T(8,128)(2,1)S(1)} %collective-permute-done.3.refs_1_, ...), custom_call_target="tpu_custom_call" | custom-call | flops 436207616 | bytes 13631488 | tf_op jit(solution)/shard_map/pallas_call | solution.py:696
  64.1 8.1 %shard_map.130 = (bf16[32,1664]{1,0:T(8,128)(2,1)S(1)}, bf16[8,32,512]{2,1,0:T(8,128)(2,1)S(1)}) custom-call(bf16[8,32,512]{2,1,0:T(8,128)(2,1)S(1)} %collective-permute-done.16.refs_0_, bf16[8,144,128]{2,1,0:T(8,128)(2,1)S(1)} %collective-permute-done.4.refs_0_.refs_1_, bf16[3,512,1664]{2,1,0:T(8,128)(2,1)S(1)} %shard_map.110.refs_4_.refs_2_, ...), custom_call_target="tpu_custom_call" | custom-call | flops 1308622848 | bytes 40894464 | tf_op jit(solution)/shard_map/pallas_call | solution.py:780
  76.1 3.9 %collective-permute-done.18.arrived_ref = bf16[4,32,512]{2,1,0:T(8,128)(2,1)S(1)} collective-permute-done((bf16[4,32,512]{2,1,0:T(8,128)(2,1)S(1)}, bf16[4,32,512]{2,1,0:T(8,128)(2,1)S(1)}, u32[]{:S(2)}, u32[]{:S(2)}) %collective-permute-start.18) | collective-permute-done | bytes 131104 | tf_op jit(solution)/shard_map/ppermute | solution.py:157
  80.0 2.1 %collective-permute-start.19 = (bf16[32,512]{1,0:T(8,128)(2,1)S(1)}, bf16[32,512]{1,0:T(8,128)(2,1)S(1)}, u32[]{:S(2)}, u32[]{:S(2)}) collective-permute-start(bf16[32,512]{1,0:T(8,128)(2,1)S(1)} %get-tuple-element.57), channel_id=1, source_target_pairs={{0,12},{1,13},{2,14},{3,15},{4,8},{5,9},{6,10},{7,11},{8,4},{9,5},... | collective-permute-start | bytes 98312 | tf_op jit(solution)/shard_map/ppermute | solution.py:157
  82.6 1.9 %collective-permute-start.21 = (bf16[32,512]{1,0:T(8,128)(2,1)S(1)}, bf16[32,512]{1,0:T(8,128)(2,1)S(1)}, u32[]{:S(2)}, u32[]{:S(2)}) collective-permute-start(bf16[32,512]{1,0:T(8,128)(2,1)S(1)} %get-tuple-element.59), channel_id=1, source_target_pairs={{0,4},{1,5},{2,6},{3,7},{4,0},{5,1},{6,2},{7,3},{8,12},{9,13},{10,... | collective-permute-start | bytes 98312 | tf_op jit(solution)/shard_map/ppermute | solution.py:157
  84.5 1.3 %collective-permute-done.19.refs_0_ = bf16[32,512]{1,0:T(8,128)(2,1)S(1)} collective-permute-done((bf16[32,512]{1,0:T(8,128)(2,1)S(1)}, bf16[32,512]{1,0:T(8,128)(2,1)S(1)}, u32[]{:S(2)}, u32[]{:S(2)}) %collective-permute-start.19) | collective-permute-done | bytes 32800 | tf_op jit(solution)/shard_map/ppermute | solution.py:157
  85.8 1.5 %collective-permute-done.20.refs_1_ = bf16[32,512]{1,0:T(8,128)(2,1)S(1)} collective-permute-done((bf16[32,512]{1,0:T(8,128)(2,1)S(1)}, bf16[32,512]{1,0:T(8,128)(2,1)S(1)}, u32[]{:S(2)}, u32[]{:S(2)}) %collective-permute-start.20) | collective-permute-done | bytes 32800 | tf_op jit(solution)/shard_map/ppermute | solution.py:157
  (64 shorter events, 15.2 us)
Async XLA Ops:
  0.8 9.9 %collective-permute-start.2 = (bf16[144,128]{1,0:T(8,128)(2,1)S(1)}, bf16[144,128]{1,0:T(8,128)(2,1)S(1)}, u32[]{:S(2)}, u32[]{:S(2)}) collective-permute-start(bf16[144,128]{1,0:T(8,128)(2,1)S(1)} %get-tuple-element.34.refs_0_), channel_id=1, source_target_pairs={{0,12},{1,13},{2,14},{3,15},{4,8},{5,9},{6,10},{7,11},{8,4},{9,5},... | collective-permute-start | bytes 110600 | tf_op jit(solution)/shard_map/ppermute | solution.py:157
  6.0 4.9 %collective-permute-start.1 = (bf16[144,128]{1,0:T(8,128)(2,1)S(1)}, bf16[144,128]{1,0:T(8,128)(2,1)S(1)}, u32[]{:S(2)}, u32[]{:S(2)}) collective-permute-start(bf16[144,128]{1,0:T(8,128)(2,1)S(1)} %get-tuple-element.34.refs_0_), channel_id=1, source_target_pairs={{0,8},{1,9},{2,10},{3,11},{4,12},{5,13},{6,14},{7,15},{8,0},{9,1},... | collective-permute-start | bytes 110600 | tf_op jit(solution)/shard_map/ppermute | solution.py:157
  6.0 4.9 %collective-permute-start = (bf16[144,128]{1,0:T(8,128)(2,1)S(1)}, bf16[144,128]{1,0:T(8,128)(2,1)S(1)}, u32[]{:S(2)}, u32[]{:S(2)}) collective-permute-start(bf16[144,128]{1,0:T(8,128)(2,1)S(1)} %get-tuple-element.34.refs_0_), channel_id=1, source_target_pairs={{0,4},{1,5},{2,6},{3,7},{4,0},{5,1},{6,2},{7,3},{8,12},{9,13},{10,... | collective-permute-start | bytes 110600 | tf_op jit(solution)/shard_map/ppermute | solution.py:157
  10.8 5.2 %collective-permute-start.3 = (bf16[4,144,128]{2,1,0:T(8,128)(2,1)S(1)}, bf16[4,144,128]{2,1,0:T(8,128)(2,1)S(1)}, u32[]{:S(2)}, u32[]{:S(2)}) collective-permute-start(bf16[4,144,128]{2,1,0:T(8,128)(2,1)S(1)} %shard_map.111.after_ref.refs_0_.refs_1_.refs_3_), channel_id=1, source_target_pairs={{0,2},{1,3},{2,0},{3,1},{4,6},{5,7},{6,4},{7,5},{8,10},{9,11},{10,... | collective-permute-start | bytes 442376 | tf_op jit(solution)/shard_map/ppermute | solution.py:157
  16.1 1.6 %collective-permute-start.4 = (bf16[8,144,128]{2,1,0:T(8,128)(2,1)S(1)}, bf16[8,144,128]{2,1,0:T(8,128)(2,1)S(1)}, u32[]{:S(2)}, u32[]{:S(2)}) collective-permute-start(bf16[8,144,128]{2,1,0:T(8,128)(2,1)S(1)} %shard_map.114), channel_id=1, source_target_pairs={{0,1},{1,0},{2,3},{3,2},{4,5},{5,4},{6,7},{7,6},{8,9},{9,8},{10,11... | collective-permute-start | bytes 884744 | tf_op jit(solution)/shard_map/ppermute | solution.py:157
  18.3 1.4 %collective-permute-start.5 = (bf16[528,128]{1,0:T(8,128)(2,1)S(1)}, bf16[528,128]{1,0:T(8,128)(2,1)S(1)}, u32[]{:S(2)}, u32[]{:S(2)}) collective-permute-start(bf16[528,128]{1,0:T(8,128)(2,1)S(1)} %shard_map.115), channel_id=1, source_target_pairs={{0,1},{1,0},{2,3},{3,2},{4,5},{5,4},{6,7},{7,6},{8,9},{9,8},{10,11... | collective-permute-start | bytes 405512 | tf_op jit(solution)/shard_map/ppermute | solution.py:157
  19.8 5.6 %collective-permute-start.6 = (bf16[528,128]{1,0:T(8,128)(2,1)S(1)}, bf16[528,128]{1,0:T(8,128)(2,1)S(1)}, u32[]{:S(2)}, u32[]{:S(2)}) collective-permute-start(bf16[528,128]{1,0:T(8,128)(2,1)S(1)} %shard_map.117.after_ref), channel_id=1, source_target_pairs={{0,2},{1,3},{2,0},{3,1},{4,6},{5,7},{6,4},{7,5},{8,10},{9,11},{10,... | collective-permute-start | bytes 405512 | tf_op jit(solution)/shard_map/ppermute | solution.py:157
  25.6 11.4 %collective-permute-start.9 = (bf16[528,128]{1,0:T(8,128)(2,1)S(1)}, bf16[528,128]{1,0:T(8,128)(2,1)S(1)}, u32[]{:S(2)}, u32[]{:S(2)}) collective-permute-start(bf16[528,128]{1,0:T(8,128)(2,1)S(1)} %shard_map.119.after_ref.refs_0_), channel_id=1, source_target_pairs={{0,12},{1,13},{2,14},{3,15},{4,8},{5,9},{6,10},{7,11},{8,4},{9,5},... | collective-permute-start | bytes 405512 | tf_op jit(solution)/shard_map/ppermute | solution.py:157
  29.2 11.0 %collective-permute-start.8 = (bf16[528,128]{1,0:T(8,128)(2,1)S(1)}, bf16[528,128]{1,0:T(8,128)(2,1)S(1)}, u32[]{:S(2)}, u32[]{:S(2)}) collective-permute-start(bf16[528,128]{1,0:T(8,128)(2,1)S(1)} %shard_map.119.after_ref.refs_0_), channel_id=1, source_target_pairs={{0,8},{1,9},{2,10},{3,11},{4,12},{5,13},{6,14},{7,15},{8,0},{9,1},... | collective-permute-start | bytes 405512 | tf_op jit(solution)/shard_map/ppermute | solution.py:157
  29.3 11.0 %collective-permute-start.7 = (bf16[528,128]{1,0:T(8,128)(2,1)S(1)}, bf16[528,128]{1,0:T(8,128)(2,1)S(1)}, u32[]{:S(2)}, u32[]{:S(2)}) collective-permute-start(bf16[528,128]{1,0:T(8,128)(2,1)S(1)} %shard_map.119.after_ref.refs_0_), channel_id=1, source_target_pairs={{0,4},{1,5},{2,6},{3,7},{4,0},{5,1},{6,2},{7,3},{8,12},{9,13},{10,... | collective-permute-start | bytes 405512 | tf_op jit(solution)/shard_map/ppermute | solution.py:157
  40.6 5.0 %collective-permute-start.10 = (bf16[4,128,128]{2,1,0:T(8,128)(2,1)S(1)}, bf16[4,128,128]{2,1,0:T(8,128)(2,1)S(1)}, u32[]{:S(2)}, u32[]{:S(2)}) collective-permute-start(bf16[4,128,128]{2,1,0:T(8,128)(2,1)S(1)} %shard_map.121.after_ref.refs_0_.near_ref), channel_id=1, source_target_pairs={{0,2},{1,3},{2,0},{3,1},{4,6},{5,7},{6,4},{7,5},{8,10},{9,11},{10,... | collective-permute-start | bytes 393224 | tf_op jit(solution)/shard_map/ppermute | solution.py:157
  45.7 1.6 %collective-permute-start.11 = (bf16[8,128,128]{2,1,0:T(8,128)(2,1)S(1)}, bf16[8,128,128]{2,1,0:T(8,128)(2,1)S(1)}, u32[]{:S(2)}, u32[]{:S(2)}) collective-permute-start(bf16[8,128,128]{2,1,0:T(8,128)(2,1)S(1)} %shard_map.123), channel_id=1, source_target_pairs={{0,1},{1,0},{2,3},{3,2},{4,5},{5,4},{6,7},{7,6},{8,9},{9,8},{10,11... | collective-permute-start | bytes 786440 | tf_op jit(solution)/shard_map/ppermute | solution.py:157
  49.0 6.8 %collective-permute-start.14 = (bf16[32,512]{1,0:T(8,128)(2,1)S(1)}, bf16[32,512]{1,0:T(8,128)(2,1)S(1)}, u32[]{:S(2)}, u32[]{:S(2)}) collective-permute-start(bf16[32,512]{1,0:T(8,128)(2,1)S(1)} %shard_map.124.refs_0_.stream_ref), channel_id=1, source_target_pairs={{0,12},{1,13},{2,14},{3,15},{4,8},{5,9},{6,10},{7,11},{8,4},{9,5},... | collective-permute-start | bytes 98312 | tf_op jit(solution)/shard_map/ppermute | solution.py:157
  51.4 4.8 %collective-permute-start.13 = (bf16[32,512]{1,0:T(8,128)(2,1)S(1)}, bf16[32,512]{1,0:T(8,128)(2,1)S(1)}, u32[]{:S(2)}, u32[]{:S(2)}) collective-permute-start(bf16[32,512]{1,0:T(8,128)(2,1)S(1)} %shard_map.124.refs_0_.stream_ref), channel_id=1, source_target_pairs={{0,8},{1,9},{2,10},{3,11},{4,12},{5,13},{6,14},{7,15},{8,0},{9,1},... | collective-permute-start | bytes 98312 | tf_op jit(solution)/shard_map/ppermute | solution.py:157
  51.4 4.8 %collective-permute-start.12 = (bf16[32,512]{1,0:T(8,128)(2,1)S(1)}, bf16[32,512]{1,0:T(8,128)(2,1)S(1)}, u32[]{:S(2)}, u32[]{:S(2)}) collective-permute-start(bf16[32,512]{1,0:T(8,128)(2,1)S(1)} %shard_map.124.refs_0_.stream_ref), channel_id=1, source_target_pairs={{0,4},{1,5},{2,6},{3,7},{4,0},{5,1},{6,2},{7,3},{8,12},{9,13},{10,... | collective-permute-start | bytes 98312 | tf_op jit(solution)/shard_map/ppermute | solution.py:157
  56.3 5.6 %collective-permute-start.15 = (bf16[4,32,512]{2,1,0:T(8,128)(2,1)S(1)}, bf16[4,32,512]{2,1,0:T(8,128)(2,1)S(1)}, u32[]{:S(2)}, u32[]{:S(2)}) collective-permute-start(bf16[4,32,512]{2,1,0:T(8,128)(2,1)S(1)} %shard_map.126.refs_0_), channel_id=1, source_target_pairs={{0,2},{1,3},{2,0},{3,1},{4,6},{5,7},{6,4},{7,5},{8,10},{9,11},{10,... | collective-permute-start | bytes 393224 | tf_op jit(solution)/shard_map/ppermute | solution.py:157
  61.8 2.3 %collective-permute-start.16 = (bf16[8,32,512]{2,1,0:T(8,128)(2,1)S(1)}, bf16[8,32,512]{2,1,0:T(8,128)(2,1)S(1)}, u32[]{:S(2)}, u32[]{:S(2)}) collective-permute-start(bf16[8,32,512]{2,1,0:T(8,128)(2,1)S(1)} %shard_map.128), channel_id=1, source_target_pairs={{0,1},{1,0},{2,3},{3,2},{4,5},{5,4},{6,7},{7,6},{8,9},{9,8},{10,11... | collective-permute-start | bytes 786440 | tf_op jit(solution)/shard_map/ppermute | solution.py:157
  61.9 10.9 %slice-start.2 = ((s8[6815744]{0:T(1024)(128)(4,1)}), s8[2621440]{0:T(1024)(128)(4,1)S(1)}, s32[]{:S(2)}) async-start(s8[6815744]{0:T(1024)(128)(4,1)} %bitcast.4), calls=%async_computation.2 | async-start | bytes 5242880
  64.1 8.8 %slice-start.3 = ((s8[6815744]{0:T(1024)(128)(4,1)}), s8[4194304]{0:T(1024)(128)(4,1)S(1)}, s32[]{:S(2)}) async-start(s8[6815744]{0:T(1024)(128)(4,1)} %bitcast.4), calls=%async_computation.3 | async-start | bytes 8388608
  72.3 1.8 %collective-permute-start.17 = (bf16[8,32,512]{2,1,0:T(8,128)(2,1)S(1)}, bf16[8,32,512]{2,1,0:T(8,128)(2,1)S(1)}, u32[]{:S(2)}, u32[]{:S(2)}) collective-permute-start(bf16[8,32,512]{2,1,0:T(8,128)(2,1)S(1)} %get-tuple-element.55), channel_id=1, source_target_pairs={{0,1},{1,0},{2,3},{3,2},{4,5},{5,4},{6,7},{7,6},{8,9},{9,8},{10,11... | collective-permute-start | bytes 786440 | tf_op jit(solution)/shard_map/ppermute | solution.py:157
  74.1 5.9 %collective-permute-start.18 = (bf16[4,32,512]{2,1,0:T(8,128)(2,1)S(1)}, bf16[4,32,512]{2,1,0:T(8,128)(2,1)S(1)}, u32[]{:S(2)}, u32[]{:S(2)}) collective-permute-start(bf16[4,32,512]{2,1,0:T(8,128)(2,1)S(1)} %shard_map.133), channel_id=1, source_target_pairs={{0,2},{1,3},{2,0},{3,1},{4,6},{5,7},{6,4},{7,5},{8,10},{9,11},{10,... | collective-permute-start | bytes 393224 | tf_op jit(solution)/shard_map/ppermute | solution.py:157
  80.0 5.8 %collective-permute-start.19 = (bf16[32,512]{1,0:T(8,128)(2,1)S(1)}, bf16[32,512]{1,0:T(8,128)(2,1)S(1)}, u32[]{:S(2)}, u32[]{:S(2)}) collective-permute-start(bf16[32,512]{1,0:T(8,128)(2,1)S(1)} %get-tuple-element.57), channel_id=1, source_target_pairs={{0,12},{1,13},{2,14},{3,15},{4,8},{5,9},{6,10},{7,11},{8,4},{9,5},... | collective-permute-start | bytes 98312 | tf_op jit(solution)/shard_map/ppermute | solution.py:157
  82.1 5.2 %collective-permute-start.20 = (bf16[32,512]{1,0:T(8,128)(2,1)S(1)}, bf16[32,512]{1,0:T(8,128)(2,1)S(1)}, u32[]{:S(2)}, u32[]{:S(2)}) collective-permute-start(bf16[32,512]{1,0:T(8,128)(2,1)S(1)} %get-tuple-element.58), channel_id=1, source_target_pairs={{0,8},{1,9},{2,10},{3,11},{4,12},{5,13},{6,14},{7,15},{8,0},{9,1},... | collective-permute-start | bytes 98312 | tf_op jit(solution)/shard_map/ppermute | solution.py:157
  82.6 4.7 %collective-permute-start.21 = (bf16[32,512]{1,0:T(8,128)(2,1)S(1)}, bf16[32,512]{1,0:T(8,128)(2,1)S(1)}, u32[]{:S(2)}, u32[]{:S(2)}) collective-permute-start(bf16[32,512]{1,0:T(8,128)(2,1)S(1)} %get-tuple-element.59), channel_id=1, source_target_pairs={{0,4},{1,5},{2,6},{3,7},{4,0},{5,1},{6,2},{7,3},{8,12},{9,13},{10,... | collective-permute-start | bytes 98312 | tf_op jit(solution)/shard_map/ppermute | solution.py:157
  (4 other events, 23.9 us)
